TPU v7x, 256 devices: a whole 4x4x8 slice. The times are simulated.
256 devices in a mesh: seq: 4 (over y_lo, core), grp: 8 (over z), head: 8 (over x, y_hi).
Axes of the slice: x: 4, y: 4 (y_hi: 2, y_lo: 2; y = y_hi * 2 + y_lo), z: 8, core: 2. Of those that a mesh axis runs over, the one named last changes fastest.
Arguments:
- queries: bfloat16 [8, 512, 8192], P('grp', 'seq', 'head'), may hold values from -6 to 6
- key_heads: bfloat16 [8, 512, 1024], P('grp', 'seq', 'head'), may hold values from -6 to 6
- value_heads: bfloat16 [8, 512, 1024], P('grp', 'seq', 'head'), may hold values from -6 to 6
- cotangent: bfloat16 [8, 512, 8192], P('grp', 'seq', 'head'), may hold values from -6 to 6
- loss_mask: int32 [8, 512], P('grp', 'seq'), may hold values 0 or 1
- log_ratio: float32 [8, 512], P('grp', ('seq', 'head')), may hold values from -6 to 6
- block_counts: int32 [8], replicated, may hold values from 1 to 2, as said below
- response_order: int32 [8], replicated, may hold values from 0 to 7, each once
Outputs:
- attended: bfloat16 [8, 512, 8192], P('grp', 'seq', 'head')
- query_grad: bfloat16 [8, 512, 8192], P('grp', 'seq', 'head')
- key_grad: bfloat16 [8, 512, 1024], P('grp', 'seq', 'head')
- value_grad: bfloat16 [8, 512, 1024], P('grp', 'seq', 'head')
- pair_loss: float32 [4], replicated
Inputs may be any that keep to these rules, and one draw needn't show every extreme that they name: Response slot i holds 128 * block_counts[i] tokens at its start; the rest of its 256 rows is padding. Some slot holds a full response and some slot a single block. Slot i, slot i % 2 of response group 4 + i // 2, holds the chosen response of pair response_order[i] // 2 if the number is even, the rejected one if it is odd.
All inputs are finite; a program needn't handle non-finite values. No bound on the sum of `loss_mask` on one device may be relied on, other than what follows from the above.
Results may differ from a plain program's by a relative error of at most 0.033.
Values may be sent and summed in bfloat16 or wider, within the bound.
No kernel may reach another device: no remote copies, remote signals or barrier semaphores. Data moves between devices by JAX's collectives and lax.ppermute only.
A program may use at most 64 MiB of HBM per device.

v0:
```python
import math

import jax
import jax.numpy as jnp
from jax import lax
from jax.sharding import PartitionSpec as P

LEN_BLOCK = 128


BETA = 0.1
NEG_FILL = -1e30


def body(
    queries, key_heads, value_heads, cotangent, loss_mask, log_ratio, block_counts, response_order
):
    seq_count = lax.axis_size("seq")
    group_count = lax.axis_size("grp")
    head_count = lax.axis_size("head")
    seq_index = lax.axis_index("seq")
    group_index = lax.axis_index("grp")
    head_index = lax.axis_index("head")
    tok_rows = queries.shape[1]
    head_dim = key_heads.shape[2]
    group_tok = tok_rows * seq_count
    resp_len = group_tok // 2
    pairs = group_count // 2
    scaling = 1.0 / math.sqrt(head_dim)
    row_ids = seq_index * tok_rows + jnp.arange(tok_rows)
    is_response = group_index >= pairs
    slot_number = seq_index * tok_rows // resp_len
    slot_index = jnp.clip(2 * (group_index - pairs) + slot_number, 0, group_count - 1)
    position = row_ids - slot_number * resp_len
    length = block_counts[slot_index] * LEN_BLOCK
    is_valid = jnp.logical_or(jnp.logical_not(is_response), position < length)
    is_kept = jnp.logical_and(is_valid, loss_mask[0] > 0)
    piece_len = tok_rows // head_count
    kept_piece = lax.dynamic_slice_in_dim(is_kept, head_index * piece_len, piece_len)
    partial_ratio = jnp.sum(jnp.where(kept_piece, log_ratio[0], 0.0))
    response_id = response_order[slot_index]
    slot_mark = jnp.logical_and(is_response, jnp.arange(group_count) == response_id)
    ratio_terms = jnp.where(slot_mark, partial_ratio, 0.0)
    totals = lax.psum(ratio_terms, ("seq", "grp", "head"))
    margin = totals[0::2] - totals[1::2]
    pair_loss = jnp.logaddexp(0.0, -BETA * margin)
    weight = jax.nn.sigmoid(-BETA * margin)
    pair_number = response_id // 2
    signed = jnp.where(response_id % 2 == 0, -1.0, 1.0) * weight[pair_number]
    own_weight = weight[jnp.clip(group_index, 0, pairs - 1)]
    row_scale = jnp.where(is_kept, jnp.where(is_response, signed, own_weight), 0.0)
    grad_flat = (row_scale[:, None] * cotangent[0].astype(jnp.float32)).astype(jnp.bfloat16)
    local_pair = jnp.concatenate([key_heads[0], value_heads[0]], axis=1)
    source_group = jnp.where(is_response, pair_number, group_index)
    pair_width = 2 * head_dim
    seq_ids = jnp.arange(seq_count)
    piece_rows = lax.all_gather(local_pair[None], ("seq", "grp"), axis=0, tiled=True)
    joined = jnp.arange(piece_rows.shape[0])
    shard_of = joined // group_count
    group_of = joined % group_count
    same_shard = shard_of[None, :] == seq_ids[:, None]
    own_pick = jnp.logical_and(same_shard, (group_of == group_index)[None, :]).astype(jnp.bfloat16)
    prompt_pick = jnp.logical_and(same_shard, (group_of == source_group)[None, :]).astype(
        jnp.bfloat16
    )
    own_acc = jnp.einsum(
        "sk,ktc->stc", own_pick, piece_rows, preferred_element_type=jnp.float32
    ).astype(jnp.bfloat16)
    prompt_acc = jnp.einsum(
        "sk,ktc->stc", prompt_pick, piece_rows, preferred_element_type=jnp.float32
    ).astype(jnp.bfloat16)
    own_context = own_acc.reshape(group_tok, pair_width)
    prompt_context = prompt_acc.reshape(group_tok, pair_width)
    context = jnp.concatenate([prompt_context, own_context], axis=0)
    context_keys = context[:, :head_dim]
    context_values = context[:, head_dim:]
    key_count = 2 * group_tok
    block_len = math.gcd(256, key_count)
    query_rows = queries[0].reshape(tok_rows, -1, head_dim)
    grad_rows = grad_flat.reshape(tok_rows, -1, head_dim)
    head_group = query_rows.shape[1]
    prompt_end = jnp.where(is_response, (group_tok + block_len - 1) // block_len, 0).astype(
        jnp.int32
    )
    own_begin = (group_tok + jnp.where(is_response, slot_number * resp_len, 0)) // block_len
    own_begin = jnp.maximum(own_begin, prompt_end)
    own_end = (group_tok + (seq_index + 1) * tok_rows + block_len - 1) // block_len

    def sweep(step_fn, carried):
        carried = lax.fori_loop(jnp.int32(0), prompt_end, step_fn, carried)
        return lax.fori_loop(own_begin, own_end, step_fn, carried)

    def allowed_block(start_row):
        key_ids = start_row + jnp.arange(block_len)
        in_prompt = key_ids < group_tok
        own_row = key_ids - group_tok
        same_slot = jnp.logical_or(jnp.logical_not(is_response), own_row // resp_len == slot_number)
        own_ok = jnp.logical_and(
            own_row[None, :] <= row_ids[:, None],
            jnp.logical_and(same_slot, jnp.logical_not(in_prompt))[None, :],
        )
        prompt_ok = jnp.logical_and(in_prompt, is_response)[None, :]
        return jnp.logical_or(own_ok, prompt_ok)[:, None, :]

    def block_scores(number):
        start_row = number * block_len
        key_block = lax.dynamic_slice_in_dim(context_keys, start_row, block_len, 0)
        scores = (
            jnp.einsum("rgd,bd->rgb", query_rows, key_block, preferred_element_type=jnp.float32)
            * scaling
        )
        return (scores, allowed_block(start_row), start_row)

    def first_pass(number, carried):
        running_top, running_sum = carried
        scores, allowed, start_row = block_scores(number)
        masked = jnp.where(allowed, scores, NEG_FILL)
        new_top = jnp.maximum(running_top, jnp.max(masked, axis=-1))
        fresh = jnp.where(allowed, jnp.exp(masked - new_top[..., None]), 0.0)
        running_sum = running_sum * jnp.exp(running_top - new_top) + jnp.sum(fresh, axis=-1)
        return (new_top, running_sum)

    start_top = jnp.full((tok_rows, head_group), NEG_FILL, jnp.float32)
    start_sum = jnp.zeros((tok_rows, head_group), jnp.float32)
    running_top, running_sum = sweep(first_pass, (start_top, start_sum))
    log_total = running_top + jnp.log(running_sum)

    def second_pass(number, partial_out):
        scores, allowed, start_row = block_scores(number)
        weights = jnp.where(allowed, jnp.exp(scores - log_total[..., None]), 0.0).astype(
            jnp.bfloat16
        )
        value_block = lax.dynamic_slice_in_dim(context_values, start_row, block_len, 0)
        return partial_out + jnp.einsum(
            "rgb,bd->rgd", weights, value_block, preferred_element_type=jnp.float32
        )

    start_out = jnp.zeros((tok_rows, head_group, head_dim), jnp.float32)
    output = sweep(second_pass, start_out)
    row_delta = jnp.sum(grad_rows.astype(jnp.float32) * output, axis=-1)

    def third_pass(number, carried):
        partial_grad, grad_store = carried
        scores, allowed, start_row = block_scores(number)
        weights = jnp.where(allowed, jnp.exp(scores - log_total[..., None]), 0.0)
        rounded = weights.astype(jnp.bfloat16)
        key_block = lax.dynamic_slice_in_dim(context_keys, start_row, block_len, 0)
        value_block = lax.dynamic_slice_in_dim(context_values, start_row, block_len, 0)
        prob_grad = jnp.einsum(
            "rgd,bd->rgb", grad_rows, value_block, preferred_element_type=jnp.float32
        )
        score_grad = (weights * (prob_grad - row_delta[..., None]) * scaling).astype(jnp.bfloat16)
        partial_grad = partial_grad + jnp.einsum(
            "rgb,bd->rgd", score_grad, key_block, preferred_element_type=jnp.float32
        )
        key_block_grad = jnp.einsum(
            "rgb,rgd->bd", score_grad, query_rows, preferred_element_type=jnp.float32
        )
        value_block_grad = jnp.einsum(
            "rgb,rgd->bd", rounded, grad_rows, preferred_element_type=jnp.float32
        )
        block_grad = jnp.concatenate([key_block_grad, value_block_grad], axis=1)
        grad_store = lax.dynamic_update_slice_in_dim(grad_store, block_grad, start_row, 0)
        return (partial_grad, grad_store)

    empty_store = jnp.zeros((key_count, pair_width), jnp.float32)
    query_total, pieces = sweep(third_pass, (start_out, empty_store))
    prompt_part = pieces[:group_tok]
    own_part = pieces[group_tok:]
    row_index = jnp.arange(tok_rows * lax.axis_size(("seq", "grp")))
    block_id = row_index // tok_rows
    from_seq = block_id // group_count
    to_group = block_id % group_count
    source_row = from_seq * tok_rows + row_index % tok_rows
    own_rows = jnp.take(own_part, source_row, axis=0)
    prompt_rows = jnp.take(prompt_part, source_row, axis=0)
    own_term = jnp.where((to_group == group_index)[:, None], own_rows, 0.0)
    prompt_term = jnp.where((to_group == source_group)[:, None], prompt_rows, 0.0)
    summed = lax.psum_scatter(
        own_term + prompt_term, ("seq", "grp"), scatter_dimension=0, tiled=True
    )
    attended = (
        jnp.where(is_valid[:, None, None], output, 0.0)
        .reshape(tok_rows, -1)
        .astype(jnp.bfloat16)[None]
    )
    query_grad = query_total.reshape(tok_rows, -1).astype(jnp.bfloat16)[None]
    key_grad = summed[:, :head_dim].astype(jnp.bfloat16)[None]
    value_grad = summed[:, head_dim:].astype(jnp.bfloat16)[None]
    return (attended, query_grad, key_grad, value_grad, pair_loss)


def solution(mesh):
    in_specs = (
        P("grp", "seq", "head"),
        P("grp", "seq", "head"),
        P("grp", "seq", "head"),
        P("grp", "seq", "head"),
        P("grp", "seq"),
        P("grp", ("seq", "head")),
        P(),
        P(),
    )
    out_specs = (
        P("grp", "seq", "head"),
        P("grp", "seq", "head"),
        P("grp", "seq", "head"),
        P("grp", "seq", "head"),
        P(),
    )
    return jax.shard_map(body, mesh=mesh, in_specs=in_specs, out_specs=out_specs, check_vma=False)
```

profile of v0, /device:TPU:32, one launch (start us, length us, event | category | flops | bytes accessed | tf_op | source)
XLA Modules:
  0.0 307.4 jit_solution(11445562160718512161)
XLA Ops:
  7.2 1.4 pad_maximum_fusion.1
  8.7 1.2 dynamic_slice.78
  10.0 1.2 dynamic_slice.77
  11.8 0.7 bitcast_and_fusion
  12.4 1.3 fusion.158
  13.8 1.2 and_select_fusion.6
  15.0 79.8 %psum.7 = f32[8]{0:T(128)S(1)} all-reduce(f32[8]{0:T(128)S(1)} %and_select_fusion.6), channel_id=1, replica_groups=mesh['seq'=4,'grp'=8,'head'=8] {'seq','grp','head'}, use_global_device_ids=true, to_apply=%region_13.14 | all-reduce | flops 8 | bytes 64 | tf_op jit(solution)/shard_map/psum | solution.py:44
  97.4 1.1 copy.48
  99.1 1.1 copy.54
  102.7 8.4 %all-gather.3.cloned.1.call-done = bf16[4096,256]{1,0:T(8,128)(2,1)} async-done(((bf16[128,256]{1,0:T(8,128)(2,1)}), bf16[4096,256]{1,0:T(8,128)(2,1)}) %all-gather.3.cloned.1.call-update) | async-done | bytes 2097168 | tf_op jit(solution)/shard_map/all_gather | solution.py:57
  111.1 2.9 fusion.130
  114.0 2.9 fusion.127
  117.0 0.8 while.87
  117.8 0.8 while.89
  119.1 1.9 while.91
  121.1 1.3 copy.57
  122.4 1.3 fusion.161
  123.7 16.2 %gather_fusion.1 = f32[4096,256]{1,0:T(8,128)} fusion(f32[512,256]{1,0:T(8,128)S(1)} %get-tuple-element.1293, s32[4096]{0:T(1024)S(1)} %broadcast_clamp_fusion), kind=kCustom, calls=%fused_computation.1.clone | custom fusion | bytes 8404992 | tf_op jit(solution)/shard_map/jit(_take)/gather | solution.py:176
  139.8 16.1 %gather_fusion = f32[4096,256]{1,0:T(8,128)} fusion(f32[512,256]{1,0:T(8,128)S(1)} %get-tuple-element.1292, s32[4096]{0:T(1024)S(1)} %broadcast_clamp_fusion), kind=kCustom, calls=%fused_computation.clone | custom fusion | bytes 8404992 | tf_op jit(solution)/shard_map/jit(_take)/gather | solution.py:175
  156.0 8.8 %fusion.122 = f32[4096,256]{1,0:T(8,128)} fusion(f32[4096,256]{1,0:T(8,128)} %gather_fusion.1, f32[4096,256]{1,0:T(8,128)} %gather_fusion, pred[4096]{0:T(1024)(128)(4,1)S(1)} %compare_and_fusion, pred[4096]{0:T(1024)(128)(4,1)S(1)} %get-tuple-element.1302, pred[4096]{0:T(1024)(128)(4,1)S(1)} %get-tuple-element.1303), kind=kLoop, calls=%fused_computation.179 | loop fusion | flops 5242880 | bytes 12595200 | tf_op jit(solution)/shard_map/add | solution.py:180
  165.1 0.8 convert_element_type.89
  166.1 0.8 convert_element_type.95
  166.9 132.1 %reduce-scatter.2.cloned.1.call-done = f32[128,256]{1,0:T(8,128)} async-done(((f32[4096,256]{1,0:T(8,128)}), f32[128,256]{1,0:T(8,128)}) %reduce-scatter.2.cloned.1.call-update) | async-done | bytes 131088 | tf_op jit(solution)/shard_map/reduce_scatter | solution.py:179
  299.1 0.9 convert.5
  (60 shorter events, 6.9 us)
Async XLA Ops:
  7.2 103.9 %all-gather.3.cloned.1.call-start = ((), (), s32[]{:S(2)}) async-start(), calls=%async_computation.2 | async-start | bytes 2162688 | tf_op jit(solution)/shard_map/all_gather | solution.py:57
  8.6 290.4 %reduce-scatter.2.cloned.1.call-start = ((), (), s32[]{:S(2)}) async-start(), calls=%async_computation.1 | async-start | bytes 4325376 | tf_op jit(solution)/shard_map/reduce_scatter | solution.py:179
Sparse Core Ops, SparseCore 0:
  10.4 100.6 all-gather.2
  164.9 134.1 reduce-scatter.1
where the time goes:
time: 309 us; the launch traced here: 307 us
  waiting for transfers between devices  141 us (46%)
  blocking collectives  79.8 us (26%)
  local copies, waits for them, and re-layouts  43.8 us (14%)
  between operations  18.8 us (6%)
  other arithmetic  16 us (5%)
  matrix products  8.22 us (3%)
    reduce_scatter x1, waiting for transfers between devices, body(): lax.psum_scatter(own_term + prompt_term, ('seq', 'grp'), scatter_dimensio...  132 us
    psum x1, blocking collectives, body(): totals = lax.psum(ratio_terms, ('seq', 'grp', 'head'))  79.8 us
    gather x1, local copies, waits for them, and re-layouts, body(): prompt_rows = jnp.take(prompt_part, source_row, axis=0)  16.2 us
    gather x1, local copies, waits for them, and re-layouts, body(): own_rows = jnp.take(own_part, source_row, axis=0)  16.1 us
    add x1, other arithmetic, body(): own_term + prompt_term  8.78 us
    all_gather x1, waiting for transfers between devices, body(): lax.all_gather(local_pair[None], ('seq', 'grp'), axis=0, tiled=True)  8.36 us
  transfers between devices with their start and end apart: 2, of which 2 were waited for; matrix products, arithmetic and copies ran while one was open for 4% of the time, Pallas kernels for 0%

commit v1 on v0

v1 whole, which is shorter than its diff:
```python
import functools
import math

import jax
import jax.numpy as jnp
from jax import lax
from jax.experimental import pallas as pl
from jax.experimental.pallas import tpu as pltpu
from jax.sharding import PartitionSpec as P

LEN_BLOCK = 128
BETA = 0.1
NEG_FILL = -1e30
LOG2_E = math.log2(math.e)
TAIL = 16
F32 = jnp.float32
BF16 = jnp.bfloat16
VMEM_BYTES = 40 * 1024 * 1024

SMEM_SPEC = pl.BlockSpec(memory_space=pltpu.SMEM)
VMEM_SPEC = pl.BlockSpec(memory_space=pltpu.VMEM)


def dot(lhs, rhs, lhs_dim, rhs_dim):
    return lax.dot_general(
        lhs, rhs, (((lhs_dim,), (rhs_dim,)), ((), ())), preferred_element_type=F32
    )


def place():
    seq = lax.axis_index("seq")
    grp = lax.axis_index("grp")
    pairs = lax.axis_size("grp") // 2
    is_response = grp >= pairs
    first_slot = jnp.where(is_response, 2 * (grp - pairs), 0)
    return seq, grp, pairs, is_response, first_slot


def encode(totals):
    high = totals.astype(BF16).astype(F32)
    rest = totals - high
    middle = rest.astype(BF16).astype(F32)
    low = rest - middle
    left = jnp.concatenate([high, low], axis=0).astype(BF16)
    right = jnp.concatenate([middle, jnp.zeros_like(middle)], axis=0).astype(BF16)
    return left, right


def decode(ref, row):
    left = ref[row : row + TAIL, :128].astype(F32)
    right = ref[row : row + TAIL, 128:].astype(F32)
    return (left[:8] + right[:8]) + left[8:]


def store_tail(ref, row, totals):
    left, right = encode(totals)
    ref[row : row + TAIL, :128] = left
    ref[row : row + TAIL, 128:] = right


def pack_kernel(order_ref, counts_ref, key_ref, value_ref, mask_ref, ratio_ref, out_ref):
    seq, grp, pairs, is_response, first_slot = place()
    head = lax.axis_index("head")
    rows, dim = key_ref.shape
    piece = ratio_ref.shape[1]
    slot = first_slot + seq // 2
    valid = jnp.logical_and(is_response, seq % 2 < counts_ref[slot])
    lane = lax.broadcasted_iota(jnp.int32, (piece, 128), 1)
    spot = lax.broadcasted_iota(jnp.int32, (piece, 128), 0)
    place_at = (lane == spot + head * piece).astype(F32)
    spread = lax.dot_general(
        jnp.broadcast_to(ratio_ref[...], (8, piece)),
        place_at,
        (((1,), (0,)), ((), ())),
        precision=lax.Precision.HIGHEST,
        preferred_element_type=F32,
    )
    kept = mask_ref[...] > 0
    partial = jnp.sum(jnp.where(kept, spread[:1], 0.0), axis=1, keepdims=True)
    row = lax.broadcasted_iota(jnp.int32, (8, 128), 0)
    mine = jnp.where(valid, order_ref[slot], -1)
    totals = jnp.where(row == mine, jnp.broadcast_to(partial, (8, 128)), 0.0)
    out_ref[:rows, :dim] = key_ref[...]
    out_ref[:rows, dim:] = value_ref[...]
    store_tail(out_ref, rows, totals)


def route_kernel(order_ref, own_ref, far4, far5, far6, far7, near_ref, other_ref):
    seq, grp, pairs, is_response, first_slot = place()
    rows = own_ref.shape[0] - TAIL
    far = ((4, far4), (5, far5), (6, far6), (7, far7))
    own_pair = order_ref[first_slot + seq // 2] // 2
    other_pair = order_ref[first_slot + 1 - seq // 2] // 2
    near_ref[rows : 2 * rows] = own_ref[:rows]

    @pl.when(jnp.logical_not(is_response))
    def _():
        near_ref[:rows] = own_ref[:rows]
        other_ref[:rows] = own_ref[:rows]

    for turn, ref in far:
        source = grp ^ turn

        @pl.when(jnp.logical_and(is_response, own_pair == source))
        def _():
            near_ref[:rows] = ref[:rows]

        @pl.when(jnp.logical_and(is_response, other_pair == source))
        def _():
            other_ref[:rows] = ref[:rows]

    totals = (decode(far4, rows) + decode(far5, rows)) + (decode(far6, rows) + decode(far7, rows))
    store_tail(near_ref, 2 * rows, totals)
    store_tail(other_ref, rows, totals)


def totals_kernel(near_ref, seq1, seq2, seq3, out_ref):
    rows = seq2.shape[0] - TAIL
    out_ref[...] = (decode(near_ref, 2 * rows) + decode(seq1, 2 * rows)) + (
        decode(seq2, rows) + decode(seq3, rows)
    )


def attend_kernel(
    order_ref,
    counts_ref,
    query_ref,
    cot_ref,
    mask_ref,
    near_ref,
    seq1,
    seq2,
    seq3,
    attended_ref,
    query_grad_ref,
    back1,
    back2,
    back3,
    first_ref,
    own_ref,
    keys,
    values,
    keys_t,
    values_t,
    key_acc,
    value_acc,
):
    seq, grp, pairs, is_response, first_slot = place()
    rows = mask_ref.shape[1]
    dim = keys.shape[1]
    heads = query_ref.shape[1] // dim
    scaling = 1.0 / math.sqrt(dim)
    slot = first_slot + seq // 2
    valid = jnp.logical_or(jnp.logical_not(is_response), seq % 2 < counts_ref[slot])
    negative = jnp.logical_and(is_response, order_ref[slot] % 2 == 0)
    sign = jnp.where(valid, jnp.where(negative, -1.0, 1.0), 0.0).astype(F32)

    blocks = (
        (near_ref, 0),
        (seq1, 0),
        (seq2, 0),
        (seq3, 0),
        (seq1, rows),
        (near_ref, rows),
    )
    for number, (ref, start) in enumerate(blocks):
        part = slice(number * rows, (number + 1) * rows)
        key_part = ref[start : start + rows, :dim]
        value_part = ref[start : start + rows, dim:]
        keys[part] = key_part
        values[part] = value_part
        keys_t[:, part] = key_part.T
        values_t[:, part] = value_part.T

    open_blocks = [is_response]
    for turn in (1, 2, 3):
        open_blocks.append(jnp.logical_or(is_response, (seq ^ turn) < seq))
    open_blocks.append(jnp.logical_and(is_response, seq % 2 == 1))
    bias = [jnp.where(is_open, 0.0, NEG_FILL).astype(F32) for is_open in open_blocks]

    wide = 2 * rows
    key_id = lax.broadcasted_iota(jnp.int32, (rows, wide), 0)
    row_id = lax.broadcasted_iota(jnp.int32, (rows, wide), 1) % rows
    causal = key_id <= row_id
    kept = jnp.where(mask_ref[...] > 0, sign, 0.0)
    kept_rows = jnp.broadcast_to(kept, (rows, rows)).T
    shade = LOG2_E * scaling
    last = len(blocks) - 1

    for pair in range(heads // 2):
        spans = [slice((2 * pair + i) * dim, (2 * pair + i + 1) * dim) for i in (0, 1)]
        query = jnp.concatenate([query_ref[:, span] for span in spans], axis=0)
        grad = jnp.concatenate(
            [(cot_ref[:, span].astype(F32) * kept_rows).astype(BF16) for span in spans], axis=0
        )
        scores = dot(keys[...], query, 1, 1)
        pieces = [scores[i * rows : (i + 1) * rows] for i in range(last)]
        pieces.append(jnp.where(causal, scores[last * rows :], NEG_FILL))
        top = jnp.max(pieces[last], axis=0, keepdims=True)
        for i in range(last):
            top = jnp.maximum(top, jnp.max(pieces[i], axis=0, keepdims=True) + bias[i])
        shift = -shade * top
        powers = []
        total = jnp.zeros_like(top)
        for i in range(last + 1):
            lift = shift if i == last else shift + bias[i]
            power = jnp.exp2(pieces[i] * shade + lift)
            total = total + jnp.sum(power, axis=0, keepdims=True)
            powers.append(power)
        inverse = 1.0 / total
        probs = jnp.concatenate(powers, axis=0) * inverse
        rounded = probs.astype(BF16)
        output_t = dot(values_t[...], rounded, 1, 0)
        grad_t = grad.astype(F32).T
        delta = jnp.sum(grad_t * output_t, axis=0, keepdims=True)
        prob_grad = dot(values[...], grad, 1, 1)
        score_grad = (probs * (prob_grad - delta)).astype(BF16)
        query_grad_t = dot(keys_t[...], score_grad, 1, 0) * scaling
        key_part = dot(score_grad, query, 1, 0)
        value_part = dot(rounded, grad, 1, 0)
        if pair == 0:
            key_acc[...] = key_part
            value_acc[...] = value_part
        else:
            key_acc[...] += key_part
            value_acc[...] += value_part
        output = jnp.where(valid, output_t, 0.0).T
        query_grad = query_grad_t.T
        for i, span in enumerate(spans):
            part = slice(i * rows, (i + 1) * rows)
            attended_ref[:, span] = output[part].astype(BF16)
            query_grad_ref[:, span] = query_grad[part]

    def block(number):
        part = slice(number * rows, (number + 1) * rows)
        return key_acc[part] * scaling, value_acc[part]

    for number, ref, start in (
        (0, first_ref, 0),
        (1, back1, 0),
        (2, back2, 0),
        (3, back3, 0),
        (4, back1, rows),
        (5, own_ref, 0),
    ):
        key_part, value_part = block(number)
        ref[start : start + rows, :dim] = key_part.astype(ref.dtype)
        ref[start : start + rows, dim:] = value_part.astype(ref.dtype)


def return_kernel(
    order_ref, first_ref, own_ref, back1, back2, back3, totals_ref, local_ref, *pay_refs
):
    seq, grp, pairs, is_response, first_slot = place()
    rows = first_ref.shape[0]
    own_pair = order_ref[first_slot + seq // 2] // 2
    other_pair = order_ref[first_slot + 1 - seq // 2] // 2
    mate = back1[:rows].astype(F32)
    across = back2[...].astype(F32) + back3[...].astype(F32)
    as_prompt = jnp.where(is_response, 0.0, 1.0).astype(F32)
    local_ref[...] = own_ref[...] + back1[rows:].astype(F32) + (mate + across) * as_prompt
    own_sum = first_ref[...] + mate
    none = jnp.zeros((8, 128), F32)
    for turn, ref in zip((4, 5, 6, 7), pay_refs):
        target = grp ^ turn
        take_own = jnp.logical_and(is_response, own_pair == target)
        take_other = jnp.logical_and(is_response, other_pair == target)
        own_factor = jnp.where(take_own, 1.0, 0.0).astype(F32)
        other_factor = jnp.where(take_other, 1.0, 0.0).astype(F32)
        ref[:rows] = (own_sum * own_factor + across * other_factor).astype(BF16)
        store_tail(ref, rows, none if turn == 4 else totals_ref[...])


def add_kernel(left_ref, right_ref, out_ref):
    out_ref[...] = (left_ref[...].astype(F32) + right_ref[...].astype(F32)).astype(BF16)


def finish_kernel(
    order_ref,
    local_ref,
    far5,
    far6,
    far7,
    totals_ref,
    query_part_ref,
    query_grad_ref,
    key_grad_ref,
    value_grad_ref,
    loss_ref,
):
    seq, grp, pairs, is_response, first_slot = place()
    rows, dim = key_grad_ref.shape
    totals = totals_ref[...] + decode(far7, rows)
    margin = totals - jnp.concatenate([totals[1:], totals[:1]], axis=0)
    slope = -BETA * margin
    small = jnp.exp(-jnp.abs(slope))
    bigger = 1.0 + small
    gap = bigger - 1.0
    log_part = jnp.where(
        gap == 0.0, small, jnp.log(bigger) * (small / jnp.where(gap == 0.0, 1.0, gap))
    )
    loss = jnp.maximum(slope, 0.0) + log_part
    weight = jnp.where(slope >= 0.0, 1.0, small) / bigger
    row = lax.broadcasted_iota(jnp.int32, (8, 128), 0)
    lane = lax.broadcasted_iota(jnp.int32, (8, 128), 1)
    in_lanes = jnp.sum(jnp.where(row == 2 * lane, loss, 0.0), axis=0, keepdims=True)
    loss_ref[...] = in_lanes[:, : loss_ref.shape[1]]
    own_pair = order_ref[first_slot + seq // 2] // 2
    my_pair = jnp.where(is_response, own_pair, jnp.minimum(grp, pairs - 1))
    scale = jnp.sum(jnp.where(row == 2 * my_pair, weight, 0.0), axis=0, keepdims=True)
    as_prompt = jnp.where(is_response, 0.0, 1.0).astype(F32)
    far_sum = far5[:rows].astype(F32) + far6[:rows].astype(F32) + far7[:rows].astype(F32)
    total = local_ref[...] + far_sum * as_prompt
    key_grad_ref[...] = (total[:, :dim] * scale).astype(BF16)
    value_grad_ref[...] = (total[:, dim:] * scale).astype(BF16)
    for start in range(0, query_grad_ref.shape[1], dim):
        span = slice(start, start + dim)
        query_grad_ref[:, span] = (query_part_ref[:, span] * scale).astype(BF16)


def call(kernel, out_shapes, in_specs, scratch=(), flops=0, bytes_accessed=0):
    single = not isinstance(out_shapes, (list, tuple))
    return pl.pallas_call(
        kernel,
        out_shape=out_shapes,
        in_specs=in_specs,
        out_specs=VMEM_SPEC if single else [VMEM_SPEC] * len(out_shapes),
        scratch_shapes=list(scratch),
        compiler_params=pltpu.CompilerParams(vmem_limit_bytes=VMEM_BYTES),
        cost_estimate=pl.CostEstimate(
            flops=flops, bytes_accessed=bytes_accessed, transcendentals=0
        ),
    )


def swap(count, turn):
    return [(i, i ^ turn) for i in range(count)]


def body(
    queries, key_heads, value_heads, cotangent, loss_mask, log_ratio, block_counts, response_order
):
    seq_count = lax.axis_size("seq")
    group_count = lax.axis_size("grp")
    head_count = lax.axis_size("head")
    rows = queries.shape[1]
    dim = key_heads.shape[2]
    width = queries.shape[2]
    pair_width = 2 * dim
    blocks = seq_count + 2
    shape = jax.ShapeDtypeStruct
    packed = shape((rows + TAIL, pair_width), BF16)
    total_tile = shape((8, 128), F32)

    def along_grp(value, turn):
        return lax.ppermute(value, "grp", swap(group_count, turn))

    def along_seq(value, turn):
        return lax.ppermute(value, "seq", swap(seq_count, turn))

    own = call(pack_kernel, packed, [SMEM_SPEC] * 2 + [VMEM_SPEC] * 4)(
        response_order, block_counts, key_heads[0], value_heads[0], loss_mask, log_ratio
    )
    far5 = along_grp(own, 5)
    far6 = along_grp(own, 6)
    far7 = along_grp(own, 7)
    far4 = along_grp(far5, 1)
    near, other = call(
        route_kernel,
        [shape((2 * rows + TAIL, pair_width), BF16), packed],
        [SMEM_SPEC] + [VMEM_SPEC] * 5,
    )(response_order, own, far4, far5, far6, far7)
    seq1 = along_seq(near, 1)
    seq2 = along_seq(other, 2)
    seq3 = along_seq(other, 3)
    totals = call(totals_kernel, total_tile, [VMEM_SPEC] * 4)(near, seq1, seq2, seq3)
    half = head_count // 2
    turn_x1 = [(h, h ^ 2) for h in range(head_count)]
    turn_x2 = [(h, (3 - h // 2) * 2 + h % 2) for h in range(head_count)]
    turn_y = [
        (s * head_count + h, (s ^ 2) * head_count + (h ^ 1))
        for s in range(seq_count)
        for h in range(head_count)
    ]
    totals = totals + lax.ppermute(totals, "head", turn_x1)
    totals = totals + lax.ppermute(totals, "head", turn_x2)
    totals = totals + lax.ppermute(totals, ("seq", "head"), turn_y)

    grads = shape((rows, pair_width), BF16)
    grads_wide = shape((rows, pair_width), F32)
    attended, query_part, back1, back2, back3, first, local = call(
        attend_kernel,
        [
            shape((rows, width), BF16),
            shape((rows, width), F32),
            shape((2 * rows, pair_width), BF16),
            grads,
            grads,
            grads_wide,
            grads_wide,
        ],
        [SMEM_SPEC] * 2 + [VMEM_SPEC] * 7,
        scratch=[
            pltpu.VMEM((blocks * rows, dim), BF16),
            pltpu.VMEM((blocks * rows, dim), BF16),
            pltpu.VMEM((dim, blocks * rows), BF16),
            pltpu.VMEM((dim, blocks * rows), BF16),
            pltpu.VMEM((blocks * rows, dim), F32),
            pltpu.VMEM((blocks * rows, dim), F32),
        ],
        flops=12 * rows * width * blocks * rows,
        bytes_accessed=6 * rows * width * 2,
    )(
        response_order,
        block_counts,
        queries[0],
        cotangent[0],
        loss_mask,
        near,
        seq1,
        seq2,
        seq3,
    )
    back1 = along_seq(back1, 1)
    back2 = along_seq(back2, 2)
    back3 = along_seq(back3, 3)
    local, pay4, pay5, pay6, pay7 = call(
        return_kernel, [grads_wide] + [packed] * 4, [SMEM_SPEC] + [VMEM_SPEC] * 6
    )(response_order, first, local, back1, back2, back3, totals)
    pay4 = along_grp(pay4, 1)
    pay5 = call(add_kernel, packed, [VMEM_SPEC] * 2)(pay5, pay4)
    far7 = along_grp(pay7, 7)
    far6 = along_grp(pay6, 6)
    far5 = along_grp(pay5, 5)
    query_grad, key_grad, value_grad, loss = call(
        finish_kernel,
        [
            shape((rows, width), BF16),
            shape((rows, dim), BF16),
            shape((rows, dim), BF16),
            shape((1, group_count // 2), F32),
        ],
        [SMEM_SPEC] + [VMEM_SPEC] * 6,
    )(response_order, local, far5, far6, far7, totals, query_part)
    return attended[None], query_grad[None], key_grad[None], value_grad[None], loss[0]


def solution(mesh):
    spec = P("grp", "seq", "head")
    in_specs = (spec, spec, spec, spec, P("grp", "seq"), P("grp", ("seq", "head")), P(), P())
    out_specs = (spec, spec, spec, spec, P())
    return jax.shard_map(body, mesh=mesh, in_specs=in_specs, out_specs=out_specs, check_vma=False)
```

time: 309 us -> 67.9 us (0.22)
  waiting for transfers between devices: 141 us -> 18.9 us
  blocking collectives: 79.8 us -> 0 us
  local copies, waits for them, and re-layouts: 43.8 us -> 3.14 us
  starting transfers between devices: 0.08 us -> 35.3 us
  between operations: 18.8 us -> 0.72 us
  other arithmetic: 16 us -> 0.01 us
  Pallas kernels: 0 us -> 9.59 us
  matrix products: 8.22 us -> 0 us
    reduce_scatter x1 -> x0, waiting for transfers between devices: 132 us -> none  [body(): lax.psum_scatter(own_term + prompt_term, ('seq', 'grp'), scatter_dimensio...]
    psum x1 -> x0, blocking collectives: 79.8 us -> none  [body(): totals = lax.psum(ratio_terms, ('seq', 'grp', 'head'))]
    ppermute x0 -> x17, starting transfers between devices: none -> 35.3 us  [the longest x8 23.9 us: along_grp(): return lax.ppermute(value, 'grp', swap(group_count, turn))]
    gather x2 -> x0, local copies, waits for them, and re-layouts: 32.3 us -> none  [the longest x1 16.2 us: body(): prompt_rows = jnp.take(prompt_part, source_row, axis=0)]
    ppermute x0 -> x17, waiting for transfers between devices: none -> 18.9 us  [the longest x8 8.79 us: along_grp(): return lax.ppermute(value, 'grp', swap(group_count, turn))]
    pallas_call x0 -> x7, Pallas kernels: none -> 9.59 us  [the longest x1 6.15 us: body(): call(attend_kernel, [shape((rows, width), BF16), shape((rows, width), F32...]
    add x6 -> x3, other arithmetic: 8.81 us -> 0.01 us  [the longest x1 0.01 us: body(): totals = totals + lax.ppermute(totals, 'head', turn_x2)]
    all_gather x1 -> x0, waiting for transfers between devices: 8.36 us -> none  [body(): lax.all_gather(local_pair[None], ('seq', 'grp'), axis=0, tiled=True)]
  transfers between devices with their start and end apart: 2 -> 17, of which waited for: 2 -> 10; matrix products, arithmetic and copies ran while one was open for 4% -> 0% of each run, Pallas kernels for 0% -> 0%
where the time goes in v1:
time: 67.9 us; the launch traced here: 67.6 us
  starting transfers between devices  35.3 us (52%)
  waiting for transfers between devices  18.9 us (28%)
  Pallas kernels  9.59 us (14%)
  local copies, waits for them, and re-layouts  3.14 us (5%)
  between operations  0.72 us (1%)
    ppermute x8, starting transfers between devices, along_grp(): return lax.ppermute(value, 'grp', swap(group_count, turn))  23.9 us
    ppermute x8, waiting for transfers between devices, along_grp(): return lax.ppermute(value, 'grp', swap(group_count, turn))  8.79 us
    pallas_call x1, Pallas kernels, body(): call(attend_kernel, [shape((rows, width), BF16), shape((rows, width), F32...  6.15 us
    ppermute x6, starting transfers between devices, along_seq(): return lax.ppermute(value, 'seq', swap(seq_count, turn))  4.1 us
    ppermute x6, waiting for transfers between devices, along_seq(): return lax.ppermute(value, 'seq', swap(seq_count, turn))  4.1 us
    unnamed x16, local copies, waits for them, and re-layouts  3.14 us
    ppermute x1, starting transfers between devices, body(): totals = totals + lax.ppermute(totals, ('seq', 'head'), turn_y)  3 us
    ppermute x1, starting transfers between devices, body(): totals = totals + lax.ppermute(totals, 'head', turn_x2)  2.76 us
  transfers between devices with their start and end apart: 17, of which 10 were waited for; matrix products, arithmetic and copies ran while one was open for 0% of the time, Pallas kernels for 0%

profile of v1, /device:TPU:32, one launch (start us, length us, event | category | flops | bytes accessed | tf_op | source)
XLA Modules:
  0.0 67.6 jit_solution(17059257245334702783)
XLA Ops:
  3.6 5.9 %collective-permute-start = (bf16[144,256]{1,0:T(8,128)(2,1)S(1)}, bf16[144,256]{1,0:T(8,128)(2,1)S(1)}, u32[]{:S(2)}, u32[]{:S(2)}) collective-permute-start(bf16[144,256]{1,0:T(8,128)(2,1)S(1)} %shard_map.119.own_ref), channel_id=1, source_target_pairs={{0,40},{8,32},{16,56},{24,48},{32,8},{40,0},{48,24},{56,16},{1,41}... | collective-permute-start | bytes 221192 | tf_op jit(solution)/shard_map/ppermute | solution.py:356
  9.5 1.0 %collective-permute-start.3 = (bf16[144,256]{1,0:T(8,128)(2,1)S(1)}, bf16[144,256]{1,0:T(8,128)(2,1)S(1)}, u32[]{:S(2)}, u32[]{:S(2)}) collective-permute-start(bf16[144,256]{1,0:T(8,128)(2,1)S(1)} %shard_map.119.own_ref), channel_id=1, source_target_pairs={{0,56},{8,48},{16,40},{24,32},{32,24},{40,16},{48,8},{56,0},{1,57}... | collective-permute-start | bytes 221192 | tf_op jit(solution)/shard_map/ppermute | solution.py:356
  10.5 2.7 %collective-permute-start.2 = (bf16[144,256]{1,0:T(8,128)(2,1)S(1)}, bf16[144,256]{1,0:T(8,128)(2,1)S(1)}, u32[]{:S(2)}, u32[]{:S(2)}) collective-permute-start(bf16[144,256]{1,0:T(8,128)(2,1)S(1)} %shard_map.119.own_ref), channel_id=1, source_target_pairs={{0,48},{8,56},{16,32},{24,40},{32,16},{40,24},{48,0},{56,8},{1,49}... | collective-permute-start | bytes 221192 | tf_op jit(solution)/shard_map/ppermute | solution.py:356
  13.2 4.5 %collective-permute-start.1 = (bf16[144,256]{1,0:T(8,128)(2,1)S(1)}, bf16[144,256]{1,0:T(8,128)(2,1)S(1)}, u32[]{:S(2)}, u32[]{:S(2)}) collective-permute-start(bf16[144,256]{1,0:T(8,128)(2,1)S(1)} %collective-permute-done.far5), channel_id=1, source_target_pairs={{0,8},{8,0},{16,24},{24,16},{32,40},{40,32},{48,56},{56,48},{1,9},... | collective-permute-start | bytes 221192 | tf_op jit(solution)/shard_map/ppermute | solution.py:356
  17.7 2.4 %collective-permute-done.2.far6 = bf16[144,256]{1,0:T(8,128)(2,1)S(1)} collective-permute-done((bf16[144,256]{1,0:T(8,128)(2,1)S(1)}, bf16[144,256]{1,0:T(8,128)(2,1)S(1)}, u32[]{:S(2)}, u32[]{:S(2)}) %collective-permute-start.2) | collective-permute-done | bytes 73760 | tf_op jit(solution)/shard_map/ppermute | solution.py:356
  21.5 1.7 %collective-permute-start.6 = (bf16[144,256]{1,0:T(8,128)(2,1)S(1)}, bf16[144,256]{1,0:T(8,128)(2,1)S(1)}, u32[]{:S(2)}, u32[]{:S(2)}) collective-permute-start(bf16[144,256]{1,0:T(8,128)(2,1)S(1)} %get-tuple-element.24), channel_id=1, source_target_pairs={{0,192},{64,128},{128,64},{192,0},{1,193},{65,129},{129,65},{193,1... | collective-permute-start | bytes 221192 | tf_op jit(solution)/shard_map/ppermute | solution.py:359
  23.7 2.2 %collective-permute-done.6.seq3 = bf16[144,256]{1,0:T(8,128)(2,1)S(1)} collective-permute-done((bf16[144,256]{1,0:T(8,128)(2,1)S(1)}, bf16[144,256]{1,0:T(8,128)(2,1)S(1)}, u32[]{:S(2)}, u32[]{:S(2)}) %collective-permute-start.6) | collective-permute-done | bytes 73760 | tf_op jit(solution)/shard_map/ppermute | solution.py:359
  25.8 1.9 %collective-permute-done.5.seq2 = bf16[144,256]{1,0:T(8,128)(2,1)S(1)} collective-permute-done((bf16[144,256]{1,0:T(8,128)(2,1)S(1)}, bf16[144,256]{1,0:T(8,128)(2,1)S(1)}, u32[]{:S(2)}, u32[]{:S(2)}) %collective-permute-start.5) | collective-permute-done | bytes 73760 | tf_op jit(solution)/shard_map/ppermute | solution.py:359
  27.8 0.9 %copy-done.7 = bf16[1,128,1024]{2,1,0:T(8,128)(2,1)S(1)} copy-done((bf16[1,128,1024]{2,1,0:T(8,128)(2,1)S(1)}, bf16[1,128,1024]{2,1,0:T(8,128)(2,1)}, u32[]{:S(2)}) %copy-start.7) | copy-done | bytes 262168
  28.7 6.2 %shard_map.121 = (bf16[128,1024]{1,0:T(8,128)(2,1)}, f32[128,1024]{1,0:T(8,128)S(1)}, bf16[256,256]{1,0:T(8,128)(2,1)S(1)}, bf16[128,256]{1,0:T(8,128)(2,1)S(1)}...) custom-call(s32[8]{0:T(128)S(1)} %copy-done.2, s32[8]{0:T(128)S(1)} %copy-done.4, ...), custom_call_target="tpu_custom_call" | custom-call | flops 1207959552 | bytes 1572864 | tf_op jit(solution)/shard_map/pallas_call | solution.py:391
  34.9 1.6 %collective-permute-start.8 = (bf16[128,256]{1,0:T(8,128)(2,1)S(1)}, bf16[128,256]{1,0:T(8,128)(2,1)S(1)}, u32[]{:S(2)}, u32[]{:S(2)}) collective-permute-start(bf16[128,256]{1,0:T(8,128)(2,1)S(1)} %get-tuple-element.29), channel_id=1, source_target_pairs={{0,128},{64,192},{128,0},{192,64},{1,129},{65,193},{129,1},{193,65... | collective-permute-start | bytes 196616 | tf_op jit(solution)/shard_map/ppermute | solution.py:359
  36.7 1.5 %collective-permute-start.10 = (f32[8,128]{1,0:T(8,128)S(1)}, f32[8,128]{1,0:T(8,128)S(1)}, u32[]{:S(2)}, u32[]{:S(2)}) collective-permute-start(f32[8,128]{1,0:T(8,128)S(1)} %shard_map.122), channel_id=1, source_target_pairs={{0,2},{1,3},{2,0},{3,1},{4,6},{5,7},{6,4},{7,5},{8,10},{9,11},{10,... | collective-permute-start | bytes 12296 | tf_op jit(solution)/shard_map/ppermute | solution.py:385
  38.2 2.1 %collective-permute-done.10 = f32[8,128]{1,0:T(8,128)S(1)} collective-permute-done((f32[8,128]{1,0:T(8,128)S(1)}, f32[8,128]{1,0:T(8,128)S(1)}, u32[]{:S(2)}, u32[]{:S(2)}) %collective-permute-start.10) | collective-permute-done | bytes 4128 | tf_op jit(solution)/shard_map/ppermute | solution.py:385
  40.3 2.8 %collective-permute-start.11 = (f32[8,128]{1,0:T(8,128)S(1)}, f32[8,128]{1,0:T(8,128)S(1)}, u32[]{:S(2)}, u32[]{:S(2)}) collective-permute-start(f32[8,128]{1,0:T(8,128)S(1)} %add.9), channel_id=1, source_target_pairs={{0,6},{1,7},{2,4},{3,5},{4,2},{5,3},{6,0},{7,1},{8,14},{9,15},{10,... | collective-permute-start | bytes 12296 | tf_op jit(solution)/shard_map/ppermute | solution.py:386
  43.1 2.1 %collective-permute-done.11 = f32[8,128]{1,0:T(8,128)S(1)} collective-permute-done((f32[8,128]{1,0:T(8,128)S(1)}, f32[8,128]{1,0:T(8,128)S(1)}, u32[]{:S(2)}, u32[]{:S(2)}) %collective-permute-start.11) | collective-permute-done | bytes 4128 | tf_op jit(solution)/shard_map/ppermute | solution.py:386
  45.2 3.0 %collective-permute-start.12 = (f32[8,128]{1,0:T(8,128)S(1)}, f32[8,128]{1,0:T(8,128)S(1)}, u32[]{:S(2)}, u32[]{:S(2)}) collective-permute-start(f32[8,128]{1,0:T(8,128)S(1)} %add.10), channel_id=1, source_target_pairs={{0,129},{1,128},{2,131},{3,130},{4,133},{5,132},{6,135},{7,134},{6... | collective-permute-start | bytes 12296 | tf_op jit(solution)/shard_map/ppermute | solution.py:387
  48.2 1.8 %collective-permute-done.12 = f32[8,128]{1,0:T(8,128)S(1)} collective-permute-done((f32[8,128]{1,0:T(8,128)S(1)}, f32[8,128]{1,0:T(8,128)S(1)}, u32[]{:S(2)}, u32[]{:S(2)}) %collective-permute-start.12) | collective-permute-done | bytes 4128 | tf_op jit(solution)/shard_map/ppermute | solution.py:387
  50.7 1.4 %collective-permute-start.13 = (bf16[144,256]{1,0:T(8,128)(2,1)S(1)}, bf16[144,256]{1,0:T(8,128)(2,1)S(1)}, u32[]{:S(2)}, u32[]{:S(2)}) collective-permute-start(bf16[144,256]{1,0:T(8,128)(2,1)S(1)} %get-tuple-element.33), channel_id=1, source_target_pairs={{0,8},{8,0},{16,24},{24,16},{32,40},{40,32},{48,56},{56,48},{1,9},... | collective-permute-start | bytes 221192 | tf_op jit(solution)/shard_map/ppermute | solution.py:356
  52.0 4.8 %collective-permute-start.15 = (bf16[144,256]{1,0:T(8,128)(2,1)S(1)}, bf16[144,256]{1,0:T(8,128)(2,1)S(1)}, u32[]{:S(2)}, u32[]{:S(2)}) collective-permute-start(bf16[144,256]{1,0:T(8,128)(2,1)S(1)} %get-tuple-element.34), channel_id=1, source_target_pairs={{0,48},{8,56},{16,32},{24,40},{32,16},{40,24},{48,0},{56,8},{1,49}... | collective-permute-start | bytes 221192 | tf_op jit(solution)/shard_map/ppermute | solution.py:356
  56.8 3.7 %collective-permute-start.14 = (bf16[144,256]{1,0:T(8,128)(2,1)S(1)}, bf16[144,256]{1,0:T(8,128)(2,1)S(1)}, u32[]{:S(2)}, u32[]{:S(2)}) collective-permute-start(bf16[144,256]{1,0:T(8,128)(2,1)S(1)} %shard_map.124), channel_id=1, source_target_pairs={{0,40},{8,32},{16,56},{24,48},{32,8},{40,0},{48,24},{56,16},{1,41}... | collective-permute-start | bytes 221192 | tf_op jit(solution)/shard_map/ppermute | solution.py:356
  60.6 1.4 %collective-permute-done.15.far6 = bf16[144,256]{1,0:T(8,128)(2,1)S(1)} collective-permute-done((bf16[144,256]{1,0:T(8,128)(2,1)S(1)}, bf16[144,256]{1,0:T(8,128)(2,1)S(1)}, u32[]{:S(2)}, u32[]{:S(2)}) %collective-permute-start.15) | collective-permute-done | bytes 73760 | tf_op jit(solution)/shard_map/ppermute | solution.py:356
  62.0 2.3 %collective-permute-done.16.far7 = bf16[144,256]{1,0:T(8,128)(2,1)S(1)} collective-permute-done((bf16[144,256]{1,0:T(8,128)(2,1)S(1)}, bf16[144,256]{1,0:T(8,128)(2,1)S(1)}, u32[]{:S(2)}, u32[]{:S(2)}) %collective-permute-start.16) | collective-permute-done | bytes 73760 | tf_op jit(solution)/shard_map/ppermute | solution.py:356
  64.2 2.0 %collective-permute-done.14.far5 = bf16[144,256]{1,0:T(8,128)(2,1)S(1)} collective-permute-done((bf16[144,256]{1,0:T(8,128)(2,1)S(1)}, bf16[144,256]{1,0:T(8,128)(2,1)S(1)}, u32[]{:S(2)}, u32[]{:S(2)}) %collective-permute-start.14) | collective-permute-done | bytes 73760 | tf_op jit(solution)/shard_map/ppermute | solution.py:356
  66.3 1.4 %shard_map.125 = (bf16[128,1024]{1,0:T(8,128)(2,1)}, bf16[128,128]{1,0:T(8,128)(2,1)}, bf16[128,128]{1,0:T(8,128)(2,1)}, f32[1,4]{1,0:T(1,128)}) custom-call(s32[8]{0:T(128)S(1)} %copy-done.2, f32[128,256]{1,0:T(8,128)S(1)} %get-tuple-element.31.local_ref, bf16[144,256]{1,0:T(8,128)(2,1)S(1)} %collective-permute-done.14.far5, ...), custom_call_target="tpu_custom_call" | custom-call | tf_op jit(solution)/shard_map/pallas_call | solution.py:435
  (36 shorter events, 5.8 us)
Async XLA Ops:
  0.6 0.7 copy-start.2
  0.7 0.7 copy-start.3
  0.7 0.7 copy-start.4
  1.3 0.8 %copy-start = (bf16[1,128,128]{2,1,0:T(8,128)(2,1)S(1)}, bf16[1,128,128]{2,1,0:T(8,128)(2,1)}, u32[]{:S(2)}) copy-start(bf16[1,128,128]{2,1,0:T(8,128)(2,1)} %param.9) | copy-start | bytes 98308
  2.1 0.8 %copy-start.1 = (bf16[1,128,128]{2,1,0:T(8,128)(2,1)S(1)}, bf16[1,128,128]{2,1,0:T(8,128)(2,1)}, u32[]{:S(2)}) copy-start(bf16[1,128,128]{2,1,0:T(8,128)(2,1)} %param.10) | copy-start | bytes 98308
  2.9 24.9 %copy-start.6 = (bf16[1,128,1024]{2,1,0:T(8,128)(2,1)S(1)}, bf16[1,128,1024]{2,1,0:T(8,128)(2,1)}, u32[]{:S(2)}) copy-start(bf16[1,128,1024]{2,1,0:T(8,128)(2,1)} %param.8) | copy-start | bytes 786436
  3.6 9.5 %collective-permute-start = (bf16[144,256]{1,0:T(8,128)(2,1)S(1)}, bf16[144,256]{1,0:T(8,128)(2,1)S(1)}, u32[]{:S(2)}, u32[]{:S(2)}) collective-permute-start(bf16[144,256]{1,0:T(8,128)(2,1)S(1)} %shard_map.119.own_ref), channel_id=1, source_target_pairs={{0,40},{8,32},{16,56},{24,48},{32,8},{40,0},{48,24},{56,16},{1,41}... | collective-permute-start | bytes 221192 | tf_op jit(solution)/shard_map/ppermute | solution.py:356
  9.5 8.2 %collective-permute-start.3 = (bf16[144,256]{1,0:T(8,128)(2,1)S(1)}, bf16[144,256]{1,0:T(8,128)(2,1)S(1)}, u32[]{:S(2)}, u32[]{:S(2)}) collective-permute-start(bf16[144,256]{1,0:T(8,128)(2,1)S(1)} %shard_map.119.own_ref), channel_id=1, source_target_pairs={{0,56},{8,48},{16,40},{24,32},{32,24},{40,16},{48,8},{56,0},{1,57}... | collective-permute-start | bytes 221192 | tf_op jit(solution)/shard_map/ppermute | solution.py:356
  10.5 9.6 %collective-permute-start.2 = (bf16[144,256]{1,0:T(8,128)(2,1)S(1)}, bf16[144,256]{1,0:T(8,128)(2,1)S(1)}, u32[]{:S(2)}, u32[]{:S(2)}) collective-permute-start(bf16[144,256]{1,0:T(8,128)(2,1)S(1)} %shard_map.119.own_ref), channel_id=1, source_target_pairs={{0,48},{8,56},{16,32},{24,40},{32,16},{40,24},{48,0},{56,8},{1,49}... | collective-permute-start | bytes 221192 | tf_op jit(solution)/shard_map/ppermute | solution.py:356
  13.2 7.6 %collective-permute-start.1 = (bf16[144,256]{1,0:T(8,128)(2,1)S(1)}, bf16[144,256]{1,0:T(8,128)(2,1)S(1)}, u32[]{:S(2)}, u32[]{:S(2)}) collective-permute-start(bf16[144,256]{1,0:T(8,128)(2,1)S(1)} %collective-permute-done.far5), channel_id=1, source_target_pairs={{0,8},{8,0},{16,24},{24,16},{32,40},{40,32},{48,56},{56,48},{1,9},... | collective-permute-start | bytes 221192 | tf_op jit(solution)/shard_map/ppermute | solution.py:356
  21.4 6.3 %collective-permute-start.4 = (bf16[272,256]{1,0:T(8,128)(2,1)S(1)}, bf16[272,256]{1,0:T(8,128)(2,1)S(1)}, u32[]{:S(2)}, u32[]{:S(2)}) collective-permute-start(bf16[272,256]{1,0:T(8,128)(2,1)S(1)} %get-tuple-element.23.near_ref), channel_id=1, source_target_pairs={{0,64},{64,0},{128,192},{192,128},{1,65},{65,1},{129,193},{193,129... | collective-permute-start | bytes 417800 | tf_op jit(solution)/shard_map/ppermute | solution.py:359
  21.5 4.3 %collective-permute-start.6 = (bf16[144,256]{1,0:T(8,128)(2,1)S(1)}, bf16[144,256]{1,0:T(8,128)(2,1)S(1)}, u32[]{:S(2)}, u32[]{:S(2)}) collective-permute-start(bf16[144,256]{1,0:T(8,128)(2,1)S(1)} %get-tuple-element.24), channel_id=1, source_target_pairs={{0,192},{64,128},{128,64},{192,0},{1,193},{65,129},{129,65},{193,1... | collective-permute-start | bytes 221192 | tf_op jit(solution)/shard_map/ppermute | solution.py:359
  23.2 4.5 %collective-permute-start.5 = (bf16[144,256]{1,0:T(8,128)(2,1)S(1)}, bf16[144,256]{1,0:T(8,128)(2,1)S(1)}, u32[]{:S(2)}, u32[]{:S(2)}) collective-permute-start(bf16[144,256]{1,0:T(8,128)(2,1)S(1)} %get-tuple-element.24), channel_id=1, source_target_pairs={{0,128},{64,192},{128,0},{192,64},{1,129},{65,193},{129,1},{193,65... | collective-permute-start | bytes 221192 | tf_op jit(solution)/shard_map/ppermute | solution.py:359
  27.7 1.0 %copy-start.7 = (bf16[1,128,1024]{2,1,0:T(8,128)(2,1)S(1)}, bf16[1,128,1024]{2,1,0:T(8,128)(2,1)}, u32[]{:S(2)}) copy-start(bf16[1,128,1024]{2,1,0:T(8,128)(2,1)} %param.11) | copy-start | bytes 786436
  34.9 15.1 %collective-permute-start.7 = (bf16[256,256]{1,0:T(8,128)(2,1)S(1)}, bf16[256,256]{1,0:T(8,128)(2,1)S(1)}, u32[]{:S(2)}, u32[]{:S(2)}) collective-permute-start(bf16[256,256]{1,0:T(8,128)(2,1)S(1)} %get-tuple-element.28), channel_id=1, source_target_pairs={{0,64},{64,0},{128,192},{192,128},{1,65},{65,1},{129,193},{193,129... | collective-permute-start | bytes 393224 | tf_op jit(solution)/shard_map/ppermute | solution.py:359
  34.9 15.1 %collective-permute-start.8 = (bf16[128,256]{1,0:T(8,128)(2,1)S(1)}, bf16[128,256]{1,0:T(8,128)(2,1)S(1)}, u32[]{:S(2)}, u32[]{:S(2)}) collective-permute-start(bf16[128,256]{1,0:T(8,128)(2,1)S(1)} %get-tuple-element.29), channel_id=1, source_target_pairs={{0,128},{64,192},{128,0},{192,64},{1,129},{65,193},{129,1},{193,65... | collective-permute-start | bytes 196616 | tf_op jit(solution)/shard_map/ppermute | solution.py:359
  36.4 13.6 %collective-permute-start.9 = (bf16[128,256]{1,0:T(8,128)(2,1)S(1)}, bf16[128,256]{1,0:T(8,128)(2,1)S(1)}, u32[]{:S(2)}, u32[]{:S(2)}) collective-permute-start(bf16[128,256]{1,0:T(8,128)(2,1)S(1)} %get-tuple-element.30), channel_id=1, source_target_pairs={{0,192},{64,128},{128,64},{192,0},{1,193},{65,129},{129,65},{193,1... | collective-permute-start | bytes 196616 | tf_op jit(solution)/shard_map/ppermute | solution.py:359
  36.7 3.6 %collective-permute-start.10 = (f32[8,128]{1,0:T(8,128)S(1)}, f32[8,128]{1,0:T(8,128)S(1)}, u32[]{:S(2)}, u32[]{:S(2)}) collective-permute-start(f32[8,128]{1,0:T(8,128)S(1)} %shard_map.122), channel_id=1, source_target_pairs={{0,2},{1,3},{2,0},{3,1},{4,6},{5,7},{6,4},{7,5},{8,10},{9,11},{10,... | collective-permute-start | bytes 12296 | tf_op jit(solution)/shard_map/ppermute | solution.py:385
  40.3 4.8 %collective-permute-start.11 = (f32[8,128]{1,0:T(8,128)S(1)}, f32[8,128]{1,0:T(8,128)S(1)}, u32[]{:S(2)}, u32[]{:S(2)}) collective-permute-start(f32[8,128]{1,0:T(8,128)S(1)} %add.9), channel_id=1, source_target_pairs={{0,6},{1,7},{2,4},{3,5},{4,2},{5,3},{6,0},{7,1},{8,14},{9,15},{10,... | collective-permute-start | bytes 12296 | tf_op jit(solution)/shard_map/ppermute | solution.py:386
  45.2 4.8 %collective-permute-start.12 = (f32[8,128]{1,0:T(8,128)S(1)}, f32[8,128]{1,0:T(8,128)S(1)}, u32[]{:S(2)}, u32[]{:S(2)}) collective-permute-start(f32[8,128]{1,0:T(8,128)S(1)} %add.10), channel_id=1, source_target_pairs={{0,129},{1,128},{2,131},{3,130},{4,133},{5,132},{6,135},{7,134},{6... | collective-permute-start | bytes 12296 | tf_op jit(solution)/shard_map/ppermute | solution.py:387
  50.7 6.1 %collective-permute-start.13 = (bf16[144,256]{1,0:T(8,128)(2,1)S(1)}, bf16[144,256]{1,0:T(8,128)(2,1)S(1)}, u32[]{:S(2)}, u32[]{:S(2)}) collective-permute-start(bf16[144,256]{1,0:T(8,128)(2,1)S(1)} %get-tuple-element.33), channel_id=1, source_target_pairs={{0,8},{8,0},{16,24},{24,16},{32,40},{40,32},{48,56},{56,48},{1,9},... | collective-permute-start | bytes 221192 | tf_op jit(solution)/shard_map/ppermute | solution.py:356
  52.0 9.9 %collective-permute-start.15 = (bf16[144,256]{1,0:T(8,128)(2,1)S(1)}, bf16[144,256]{1,0:T(8,128)(2,1)S(1)}, u32[]{:S(2)}, u32[]{:S(2)}) collective-permute-start(bf16[144,256]{1,0:T(8,128)(2,1)S(1)} %get-tuple-element.34), channel_id=1, source_target_pairs={{0,48},{8,56},{16,32},{24,40},{32,16},{40,24},{48,0},{56,8},{1,49}... | collective-permute-start | bytes 221192 | tf_op jit(solution)/shard_map/ppermute | solution.py:356
  56.8 7.4 %collective-permute-start.16 = (bf16[144,256]{1,0:T(8,128)(2,1)S(1)}, bf16[144,256]{1,0:T(8,128)(2,1)S(1)}, u32[]{:S(2)}, u32[]{:S(2)}) collective-permute-start(bf16[144,256]{1,0:T(8,128)(2,1)S(1)} %get-tuple-element.35), channel_id=1, source_target_pairs={{0,56},{8,48},{16,40},{24,32},{32,24},{40,16},{48,8},{56,0},{1,57}... | collective-permute-start | bytes 221192 | tf_op jit(solution)/shard_map/ppermute | solution.py:356
  56.8 9.4 %collective-permute-start.14 = (bf16[144,256]{1,0:T(8,128)(2,1)S(1)}, bf16[144,256]{1,0:T(8,128)(2,1)S(1)}, u32[]{:S(2)}, u32[]{:S(2)}) collective-permute-start(bf16[144,256]{1,0:T(8,128)(2,1)S(1)} %shard_map.124), channel_id=1, source_target_pairs={{0,40},{8,32},{16,56},{24,48},{32,8},{40,0},{48,24},{56,16},{1,41}... | collective-permute-start | bytes 221192 | tf_op jit(solution)/shard_map/ppermute | solution.py:356
  (1 other events, 0.7 us)

commit v2 on v1

v2 whole, which is shorter than its diff:
```python
import functools
import math

import jax
import jax.numpy as jnp
from jax import lax
from jax.experimental import pallas as pl
from jax.experimental.pallas import tpu as pltpu
from jax.sharding import PartitionSpec as P

LEN_BLOCK = 128
BETA = 0.1
NEG_FILL = -1e30
LOG2_E = math.log2(math.e)
TAIL = 16
F32 = jnp.float32
BF16 = jnp.bfloat16
VMEM_BYTES = 40 * 1024 * 1024

VMEM_SPEC = pl.BlockSpec(memory_space=pltpu.VMEM)
HBM_SPEC = pl.BlockSpec(memory_space=pltpu.HBM)

FROM7, FROM5, IS_PROMPT, VALID, PAIR_ROW = 0, 4, 8, 9, 10
BIAS_FIRST, BIAS_MATE, BIAS_OVER, BIAS_CROSS, BIAS_OWN = 11, 12, 13, 14, 15
FACTS = 16


def dot(lhs, rhs, lhs_dim, rhs_dim):
    return lax.dot_general(
        lhs, rhs, (((lhs_dim,), (rhs_dim,)), ((), ())), preferred_element_type=F32
    )


def fact(facts_ref, row, width=None):
    return facts_ref[row : row + 1, :width]


def store_tail(ref, row, totals):
    high = totals.astype(BF16).astype(F32)
    rest = totals - high
    middle = rest.astype(BF16).astype(F32)
    low = rest - middle
    zero = jnp.zeros_like(middle)
    ref[row : row + TAIL, :128] = jnp.concatenate([high, low], axis=0).astype(BF16)
    ref[row : row + TAIL, 128:] = jnp.concatenate([middle, zero], axis=0).astype(BF16)


def decode(ref, row):
    left = ref[row : row + TAIL, :128].astype(F32)
    right = ref[row : row + TAIL, 128:].astype(F32)
    return (left[:8] + right[:8]) + left[8:]


def pack_kernel(key_ref, value_ref, out_ref, sems):
    dim = key_ref.shape[1]
    copies = [
        pltpu.make_async_copy(ref, out_ref.at[:, pl.ds(i * dim, dim)], sems.at[i])
        for i, ref in enumerate((key_ref, value_ref))
    ]
    for copy in copies:
        copy.start()
    for copy in copies:
        copy.wait()


def facts_kernel(
    order_hbm,
    counts_hbm,
    mask_hbm,
    ratio_hbm,
    facts_ref,
    totals_ref,
    kept_ref,
    order_ref,
    counts_ref,
    mask_ref,
    ratio_ref,
    sems,
):
    copies = [
        pltpu.make_async_copy(source, target, sems.at[i])
        for i, (source, target) in enumerate(
            (
                (order_hbm, order_ref),
                (counts_hbm, counts_ref),
                (mask_hbm, mask_ref),
                (ratio_hbm, ratio_ref),
            )
        )
    ]
    for copy in copies:
        copy.start()
    seq = lax.axis_index("seq")
    grp = lax.axis_index("grp")
    head = lax.axis_index("head")
    pairs = lax.axis_size("grp") // 2
    is_response = grp >= pairs
    for copy in copies:
        copy.wait()

    def pair_of(group, half):
        return order_ref[jnp.where(is_response, 2 * (group - pairs), 0) + half] // 2

    def put(row, value):
        facts_ref[row : row + 1, :] = jnp.full((1, facts_ref.shape[1]), value, F32)

    def flag(row, condition, yes=1.0, no=0.0):
        put(row, jnp.where(condition, yes, no).astype(F32))

    half = seq // 2
    slots = [pair_of(group, side) for side in (half, 1 - half) for group in (grp, grp ^ 1)]
    for number, pair in enumerate(slots):
        flag(FROM7 + number, jnp.logical_and(is_response, pair == (grp ^ 7)))
        flag(FROM5 + number, jnp.logical_and(is_response, pair == (grp ^ 5)))
    slot = jnp.where(is_response, 2 * (grp - pairs), 0) + half
    filled = seq % 2 < counts_ref[slot]
    valid = jnp.logical_or(jnp.logical_not(is_response), filled)
    my_pair = jnp.where(is_response, order_ref[slot] // 2, jnp.minimum(grp, pairs - 1))
    flag(IS_PROMPT, jnp.logical_not(is_response))
    flag(VALID, valid)
    put(PAIR_ROW, (2 * my_pair).astype(F32))
    flag(BIAS_FIRST, is_response, 0.0, NEG_FILL)
    flag(BIAS_MATE, jnp.logical_or(is_response, seq % 2 == 1), 0.0, NEG_FILL)
    flag(BIAS_OVER, jnp.logical_or(is_response, seq >= 2), 0.0, NEG_FILL)
    flag(BIAS_CROSS, jnp.logical_or(is_response, seq >= 2), 0.0, NEG_FILL)
    flag(BIAS_OWN, jnp.logical_and(is_response, seq % 2 == 1), 0.0, NEG_FILL)

    piece = ratio_ref.shape[1]
    lane = lax.broadcasted_iota(jnp.int32, (piece, 128), 1)
    spot = lax.broadcasted_iota(jnp.int32, (piece, 128), 0)
    place_at = (lane == spot + head * piece).astype(F32)
    spread = lax.dot_general(
        jnp.broadcast_to(ratio_ref[...], (8, piece)),
        place_at,
        (((1,), (0,)), ((), ())),
        precision=lax.Precision.HIGHEST,
        preferred_element_type=F32,
    )
    kept = mask_ref[...] > 0
    partial = jnp.sum(jnp.where(kept, spread[:1], 0.0), axis=1, keepdims=True)
    row = lax.broadcasted_iota(jnp.int32, (8, 128), 0)
    mine = jnp.where(jnp.logical_and(is_response, filled), order_ref[slot], -1)
    totals_ref[...] = jnp.where(row == mine, jnp.broadcast_to(partial, (8, 128)), 0.0)
    negative = jnp.logical_and(is_response, order_ref[slot] % 2 == 0)
    sign = jnp.where(valid, jnp.where(negative, -1.0, 1.0), 0.0).astype(F32)
    kept_ref[...] = jnp.where(kept, sign, 0.0)


def prepare_kernel(kept_ref, query_hbm, cot_hbm, query_ref, grad_ref, grad_t_ref, cots, sems):
    rows = kept_ref.shape[1]
    dim = query_ref.shape[1]
    heads = query_ref.shape[0] // rows
    copies = []
    for i in range(heads):
        for j, (source, target) in enumerate(((cot_hbm, cots), (query_hbm, query_ref))):
            copies.append(
                pltpu.make_async_copy(
                    source.at[:, pl.ds(i * dim, dim)],
                    target.at[pl.ds(i * rows, rows)],
                    sems.at[j, i],
                )
            )
    for copy in copies:
        copy.start()
    kept_rows = jnp.broadcast_to(kept_ref[...], (rows, rows)).T
    for copy in copies:
        copy.wait()
    for i in range(heads):
        part = slice(i * rows, (i + 1) * rows)
        grad = (cots[part].astype(F32) * kept_rows).astype(BF16)
        grad_ref[part] = grad
        grad_t_ref[:, part] = grad.T


def route_kernel(facts_ref, totals_ref, own_ref, far7, far5, group_ref, seq_ref, cross_ref):
    rows = own_ref.shape[0]
    for number, ref in ((1, group_ref), (2, seq_ref), (3, cross_ref)):
        picked = far7[...].astype(F32) * fact(facts_ref, FROM7 + number)
        picked = picked + far5[...].astype(F32) * fact(facts_ref, FROM5 + number)
        if number == 2:
            picked = picked + own_ref[...].astype(F32) * fact(facts_ref, IS_PROMPT)
        ref[:rows] = picked.astype(BF16)
        store_tail(ref, rows, totals_ref[...])


def select_kernel(
    facts_ref, totals_ref, own_ref, far7, far5, group_ref, seq_ref, cross_ref, near_ref, sum_ref
):
    rows = own_ref.shape[0]
    first = far7[...].astype(F32) * fact(facts_ref, FROM7)
    first = first + far5[...].astype(F32) * fact(facts_ref, FROM5)
    first = first + own_ref[...].astype(F32) * fact(facts_ref, IS_PROMPT)
    near_ref[:rows] = (first + group_ref[:rows].astype(F32)).astype(BF16)
    near_ref[rows:] = (seq_ref[:rows].astype(F32) + cross_ref[:rows].astype(F32)).astype(BF16)
    sum_ref[...] = (totals_ref[...] + decode(group_ref, rows)) + (
        decode(seq_ref, rows) + decode(cross_ref, rows)
    )


def load_blocks(blocks, keys, values, keys_t, values_t):
    dim = keys.shape[1]
    rows = keys.shape[0] // len(blocks)
    for number, (ref, start) in enumerate(blocks):
        part = slice(number * rows, (number + 1) * rows)
        key_part = ref[start : start + rows, :dim]
        value_part = ref[start : start + rows, dim:]
        keys[part] = key_part
        values[part] = value_part
        keys_t[:, part] = key_part.T
        values_t[:, part] = value_part.T


def early_kernel(
    biases,
    is_own,
    facts_ref,
    query_ref,
    grad_ref,
    left_ref,
    right_ref,
    powers_ref,
    prob_grad_ref,
    stats_ref,
    keys_t,
    values_t,
    keys,
    values,
):
    rows = keys.shape[0] // 2
    heads = query_ref.shape[0] // rows
    shade = LOG2_E / math.sqrt(keys.shape[1])
    start = 0 if is_own else rows
    load_blocks(((left_ref, 0), (right_ref, start)), keys, values, keys_t, values_t)
    wide = 2 * rows
    key_id = lax.broadcasted_iota(jnp.int32, (rows, wide), 0)
    row_id = lax.broadcasted_iota(jnp.int32, (rows, wide), 1) % rows
    causal = key_id <= row_id
    bias = [fact(facts_ref, row, wide) if row is not None else 0.0 for row in biases]
    for pair in range(heads // 2):
        both = slice(pair * wide, (pair + 1) * wide)
        scores = dot(keys[...], query_ref[both], 1, 1)
        prob_grad_ref[:, both] = dot(values[...], grad_ref[both], 1, 1)
        pieces = [scores[:rows], scores[rows:]]
        if is_own:
            pieces[1] = jnp.where(causal, pieces[1], NEG_FILL)
        tops = [jnp.max(piece, axis=0, keepdims=True) for piece in pieces]
        top = jnp.maximum(tops[0] + bias[0], tops[1] + bias[1])
        total = jnp.zeros_like(top)
        for i, piece in enumerate(pieces):
            power = jnp.exp2(piece * shade + (bias[i] - shade * top))
            total = total + jnp.sum(power, axis=0, keepdims=True)
            powers_ref[i * rows : (i + 1) * rows, both] = power
        stats_ref[0:1, both] = top
        stats_ref[1:2, both] = total


def late_kernel(
    facts_ref,
    query_ref,
    grad_ref,
    grad_t_ref,
    own_powers,
    own_prob_grad,
    own_stats,
    own_values_t,
    near_powers,
    near_prob_grad,
    near_stats,
    near_values_t,
    mate_ref,
    back_ref,
    first_ref,
    over_ref,
    own_ref,
    output_t_ref,
    own_score_grad,
    near_score_grad,
    mate_score_grad,
    keys_t,
    keys,
    values,
    values_t,
    own_key_acc,
    own_value_acc,
    near_key_acc,
    near_value_acc,
    mate_key_acc,
    mate_value_acc,
):
    rows, dim = keys.shape[0] // 2, keys.shape[1]
    heads = query_ref.shape[0] // rows
    scaling = 1.0 / math.sqrt(dim)
    shade = LOG2_E * scaling
    load_blocks(((mate_ref, 0), (mate_ref, rows)), keys, values, keys_t, values_t)
    wide = 2 * rows
    bias = [fact(facts_ref, row, wide) for row in (BIAS_MATE, BIAS_CROSS)]
    for pair in range(heads // 2):
        both = slice(pair * wide, (pair + 1) * wide)
        query = query_ref[both]
        grad = grad_ref[both]
        scores = dot(keys[...], query, 1, 1)
        prob_grad = dot(values[...], grad, 1, 1)
        pieces = [scores[:rows], scores[rows:]]
        tops = [jnp.max(pieces[i], axis=0, keepdims=True) + bias[i] for i in (0, 1)]
        own_top, near_top = own_stats[0:1, both], near_stats[0:1, both]
        top = jnp.maximum(jnp.maximum(own_top, near_top), jnp.maximum(tops[0], tops[1]))
        powers = [jnp.exp2(pieces[i] * shade + (bias[i] - shade * top)) for i in (0, 1)]
        own_fade = jnp.exp2((own_top - top) * shade)
        near_fade = jnp.exp2((near_top - top) * shade)
        total = own_stats[1:2, both] * own_fade + near_stats[1:2, both] * near_fade
        for power in powers:
            total = total + jnp.sum(power, axis=0, keepdims=True)
        inverse = 1.0 / total
        sets = (
            (own_powers[:, both] * (own_fade * inverse), own_prob_grad[:, both], own_values_t),
            (near_powers[:, both] * (near_fade * inverse), near_prob_grad[:, both], near_values_t),
            (jnp.concatenate(powers, axis=0) * inverse, prob_grad, values_t),
        )
        rounded = [probs.astype(BF16) for probs, _, _ in sets]
        output_t = sum(dot(item[2][...], part, 1, 0) for item, part in zip(sets, rounded))
        output_t_ref[:, both] = output_t
        delta = jnp.sum(grad_t_ref[:, both].astype(F32) * output_t, axis=0, keepdims=True)
        targets = (
            (own_score_grad, own_key_acc, own_value_acc),
            (near_score_grad, near_key_acc, near_value_acc),
            (mate_score_grad, mate_key_acc, mate_value_acc),
        )
        for (probs, part_grad, _), part, (target, key_acc, value_acc) in zip(
            sets, rounded, targets
        ):
            score_grad = (probs * (part_grad - delta)).astype(BF16)
            target[:, both] = score_grad
            key_part = dot(score_grad, query, 1, 0)
            value_part = dot(part, grad, 1, 0)
            if pair == 0:
                key_acc[...] = key_part
                value_acc[...] = value_part
            else:
                key_acc[...] += key_part
                value_acc[...] += value_part

    for key_acc, value_acc, number, ref, start in (
        (mate_key_acc, mate_value_acc, 0, back_ref, 0),
        (mate_key_acc, mate_value_acc, 1, back_ref, rows),
        (own_key_acc, own_value_acc, 0, back_ref, 2 * rows),
        (near_key_acc, near_value_acc, 0, first_ref, 0),
        (near_key_acc, near_value_acc, 1, over_ref, 0),
        (own_key_acc, own_value_acc, 1, own_ref, 0),
    ):
        part = slice(number * rows, (number + 1) * rows)
        ref[start : start + rows, :dim] = (key_acc[part] * scaling).astype(ref.dtype)
        ref[start : start + rows, dim:] = value_acc[part].astype(ref.dtype)


def query_kernel(
    facts_ref,
    output_t_ref,
    own_score_grad,
    near_score_grad,
    mate_score_grad,
    own_keys_t,
    near_keys_t,
    mate_keys_t,
    attended_ref,
    query_grad_ref,
):
    rows = attended_ref.shape[0]
    dim = output_t_ref.shape[0]
    scaling = 1.0 / math.sqrt(dim)
    wide = 2 * rows
    valid = fact(facts_ref, VALID, wide)
    for pair in range(output_t_ref.shape[1] // wide):
        both = slice(pair * wide, (pair + 1) * wide)
        grad_t = (
            dot(own_keys_t[...], own_score_grad[:, both], 1, 0)
            + dot(near_keys_t[...], near_score_grad[:, both], 1, 0)
            + dot(mate_keys_t[...], mate_score_grad[:, both], 1, 0)
        )
        query_grad = (grad_t * scaling).T
        output = (output_t_ref[:, both] * valid).T
        for i in (0, 1):
            span = slice((2 * pair + i) * dim, (2 * pair + i + 1) * dim)
            part = slice(i * rows, (i + 1) * rows)
            attended_ref[:, span] = output[part].astype(BF16)
            query_grad_ref[:, span] = query_grad[part]


def merge_kernel(first_ref, over_ref, own_ref, back_ref, near_out, over_out, local_ref):
    rows = first_ref.shape[0]
    near_out[...] = (first_ref[...] + back_ref[:rows].astype(F32)).astype(BF16)
    over_out[...] = (over_ref[...] + back_ref[rows : 2 * rows].astype(F32)).astype(BF16)
    local_ref[...] = own_ref[...] + back_ref[2 * rows :].astype(F32)


def return_kernel(
    facts_ref, totals_ref, near_ref, local_ref, group_ref, seq_ref, cross_ref, out_ref, pay7, pay5
):
    rows = near_ref.shape[0]
    sums = [ref[...].astype(F32) for ref in (near_ref, group_ref, seq_ref, cross_ref)]
    out_ref[...] = local_ref[...] + (sums[0] + sums[2]) * fact(facts_ref, IS_PROMPT)
    for ref, base in ((pay7, FROM7), (pay5, FROM5)):
        total = sum(part * fact(facts_ref, base + i) for i, part in enumerate(sums))
        ref[:rows] = total.astype(BF16)
        store_tail(ref, rows, totals_ref[...])


def finish_kernel(
    facts_ref,
    local_ref,
    far7,
    far5,
    totals_ref,
    rest_ref,
    query_part_ref,
    query_grad_ref,
    key_grad_ref,
    value_grad_ref,
    loss_ref,
):
    rows, dim = key_grad_ref.shape
    totals = (totals_ref[...] + rest_ref[...]) + (decode(far7, rows) + decode(far5, rows))
    margin = totals - jnp.concatenate([totals[1:], totals[:1]], axis=0)
    slope = -BETA * margin
    small = jnp.exp(-jnp.abs(slope))
    bigger = 1.0 + small
    gap = bigger - 1.0
    log_part = jnp.where(
        gap == 0.0, small, jnp.log(bigger) * (small / jnp.where(gap == 0.0, 1.0, gap))
    )
    loss = jnp.maximum(slope, 0.0) + log_part
    weight = jnp.where(slope >= 0.0, 1.0, small) / bigger
    row = lax.broadcasted_iota(jnp.int32, (8, 128), 0)
    lane = lax.broadcasted_iota(jnp.int32, (8, 128), 1)
    in_lanes = jnp.sum(jnp.where(row == 2 * lane, loss, 0.0), axis=0, keepdims=True)
    loss_ref[...] = in_lanes[:, : loss_ref.shape[1]]
    mine = row.astype(F32) == fact(facts_ref, PAIR_ROW, 128)
    scale = jnp.sum(jnp.where(mine, weight, 0.0), axis=0, keepdims=True)
    far_sum = far7[:rows].astype(F32) + far5[:rows].astype(F32)
    total = local_ref[...] + far_sum * fact(facts_ref, IS_PROMPT)
    key_grad_ref[...] = (total[:, :dim] * scale).astype(BF16)
    value_grad_ref[...] = (total[:, dim:] * scale).astype(BF16)
    for start in range(0, query_grad_ref.shape[1], dim):
        span = slice(start, start + dim)
        query_grad_ref[:, span] = (query_part_ref[:, span] * scale).astype(BF16)


def call(kernel, out_shapes, operands, scratch=(), in_hbm=0, flops=0):
    single = not isinstance(out_shapes, (list, tuple))
    plain = len(operands) - in_hbm
    held = [
        pltpu.with_memory_space_constraint(operand, pltpu.HBM) for operand in operands[plain:]
    ]
    return pl.pallas_call(
        kernel,
        out_shape=out_shapes,
        in_specs=[VMEM_SPEC] * plain + [HBM_SPEC] * in_hbm,
        out_specs=VMEM_SPEC if single else [VMEM_SPEC] * len(out_shapes),
        scratch_shapes=list(scratch),
        compiler_params=pltpu.CompilerParams(vmem_limit_bytes=VMEM_BYTES),
        cost_estimate=pl.CostEstimate(flops=flops, bytes_accessed=0, transcendentals=0),
    )(*operands[:plain], *held)


def swap(count, turn):
    return [(i, i ^ turn) for i in range(count)]


def body(
    queries, key_heads, value_heads, cotangent, loss_mask, log_ratio, block_counts, response_order
):
    seq_count = lax.axis_size("seq")
    group_count = lax.axis_size("grp")
    head_count = lax.axis_size("head")
    rows = queries.shape[1]
    dim = key_heads.shape[2]
    width = queries.shape[2]
    heads = width // dim
    both = 2 * dim
    every = heads * rows
    shape = jax.ShapeDtypeStruct
    dma = pltpu.SemaphoreType.DMA
    tie = lax.optimization_barrier
    packed = shape((rows + TAIL, both), BF16)
    total_tile = shape((8, 128), F32)
    grads = shape((rows, both), BF16)
    grads_wide = shape((rows, both), F32)

    def along_grp(value, turn):
        return lax.ppermute(value, "grp", swap(group_count, turn))

    def along_seq(value, turn):
        return lax.ppermute(value, "seq", swap(seq_count, turn))

    def across(value):
        turns = [
            (s * group_count + g, (s ^ 2) * group_count + (g ^ 1))
            for s in range(seq_count)
            for g in range(group_count)
        ]
        return lax.ppermute(value, ("seq", "grp"), turns)

    def along_x(value, step):
        near = [(h, h ^ 2) for h in range(head_count)]
        round_way = [(h, (3 - h // 2) * 2 + h % 2) for h in range(head_count)]
        return lax.ppermute(value, "head", round_way if step else near)

    def along_y(value):
        turns = [
            (s * head_count + h, (s ^ 2) * head_count + (h ^ 1))
            for s in range(seq_count)
            for h in range(head_count)
        ]
        return lax.ppermute(value, ("seq", "head"), turns)

    own = call(
        pack_kernel, grads, (key_heads[0], value_heads[0]), scratch=[dma((2,))], in_hbm=2
    )
    far7 = along_grp(own, 7)
    far5 = along_grp(own, 5)
    own, response_order = tie((own, response_order))
    facts, totals, kept = call(
        facts_kernel,
        [shape((FACTS, both), F32), total_tile, shape((1, rows), F32)],
        (response_order, block_counts, loss_mask, log_ratio),
        scratch=[
            pltpu.SMEM(response_order.shape, jnp.int32),
            pltpu.SMEM(block_counts.shape, jnp.int32),
            pltpu.VMEM(loss_mask.shape, jnp.int32),
            pltpu.VMEM(log_ratio.shape, F32),
            dma((4,)),
        ],
        in_hbm=4,
    )
    mate_own = along_seq(own, 1)
    stacked = shape((every, dim), BF16)
    query_rows, grad_rows, grad_cols = call(
        prepare_kernel,
        [stacked, stacked, shape((dim, every), BF16)],
        (kept, queries[0], cotangent[0]),
        scratch=[pltpu.VMEM((every, dim), BF16), dma((2, heads))],
        in_hbm=2,
    )
    totals = totals + along_seq(totals, 1)
    part = along_x(totals, 0)
    far7, far5, totals, query_rows = tie((far7, far5, totals, query_rows))
    totals = totals + part
    to_group, to_seq, to_cross = call(
        route_kernel, [packed] * 3, (facts, totals, own, far7, far5)
    )
    from_seq = along_seq(to_seq, 2)
    from_group = along_grp(to_group, 1)
    from_cross = across(to_cross)

    def early(biases, is_own, left, right):
        return call(
            functools.partial(early_kernel, biases, is_own),
            [
                shape((2 * rows, every), F32),
                shape((2 * rows, every), F32),
                shape((8, every), F32),
                shape((dim, 2 * rows), BF16),
                shape((dim, 2 * rows), BF16),
            ],
            (facts, query_rows, grad_rows, left, right),
            scratch=[pltpu.VMEM((2 * rows, dim), BF16)] * 2,
            flops=8 * rows * every * dim,
        )

    own_set = early((BIAS_OWN, None), True, mate_own, own)
    from_cross, own_powers = tie((from_cross, own_set[0]))
    near, totals = call(
        select_kernel,
        [shape((2 * rows, both), BF16), total_tile],
        (facts, totals, own, far7, far5, from_group, from_seq, from_cross),
    )
    mate = along_seq(near, 1)
    near_set = early((BIAS_FIRST, BIAS_OVER), False, near, near)
    near_powers, totals = tie((near_set[0], totals))
    part = along_x(totals, 1)
    mate, near_powers = tie((mate, near_powers))
    back, first, over, local, output_t, own_sg, near_sg, mate_sg, mate_keys_t = call(
        late_kernel,
        [
            shape((3 * rows, both), BF16),
            grads_wide,
            grads_wide,
            grads_wide,
            shape((dim, every), F32),
            shape((2 * rows, every), BF16),
            shape((2 * rows, every), BF16),
            shape((2 * rows, every), BF16),
            shape((dim, 2 * rows), BF16),
        ],
        (
            facts,
            query_rows,
            grad_rows,
            grad_cols,
            own_powers,
            own_set[1],
            own_set[2],
            own_set[4],
            near_powers,
            near_set[1],
            near_set[2],
            near_set[4],
            mate,
        ),
        scratch=[
            pltpu.VMEM((2 * rows, dim), BF16),
            pltpu.VMEM((2 * rows, dim), BF16),
            pltpu.VMEM((dim, 2 * rows), BF16),
        ]
        + [pltpu.VMEM((2 * rows, dim), F32)] * 6,
        flops=40 * rows * every * dim,
    )
    back, totals = tie((back, totals))
    back, totals = tie((back, totals + part))
    part = along_y(totals)
    back = along_seq(back, 1)
    near_sum, over_sum, local = call(
        merge_kernel, [grads, grads, grads_wide], (first, over, local, back)
    )
    from_seq = along_seq(over_sum, 2)
    from_group = along_grp(near_sum, 1)
    from_cross = across(over_sum)
    totals = totals + part
    attended, query_part = call(
        query_kernel,
        [shape((rows, width), BF16), shape((rows, width), F32)],
        (facts, output_t, own_sg, near_sg, mate_sg, own_set[3], near_set[3], mate_keys_t),
        flops=12 * rows * every * dim,
    )
    from_cross, query_part = tie((from_cross, query_part))
    local, pay7, pay5 = call(
        return_kernel,
        [grads_wide, packed, packed],
        (facts, totals, near_sum, local, from_group, from_seq, from_cross),
    )
    far7 = along_grp(pay7, 7)
    far5 = along_grp(pay5, 5)
    rest = along_grp(totals, 2)
    query_grad, key_grad, value_grad, loss = call(
        finish_kernel,
        [
            shape((rows, width), BF16),
            shape((rows, dim), BF16),
            shape((rows, dim), BF16),
            shape((1, group_count // 2), F32),
        ],
        (facts, local, far7, far5, totals, rest, query_part),
    )
    return attended[None], query_grad[None], key_grad[None], value_grad[None], loss[0]


def solution(mesh):
    spec = P("grp", "seq", "head")
    in_specs = (spec, spec, spec, spec, P("grp", "seq"), P("grp", ("seq", "head")), P(), P())
    out_specs = (spec, spec, spec, spec, P())
    return jax.shard_map(body, mesh=mesh, in_specs=in_specs, out_specs=out_specs, check_vma=False)
```

time: 67.9 us -> 51.8 us (0.76)
  starting transfers between devices: 35.3 us -> 28.2 us
  waiting for transfers between devices: 18.9 us -> 12.8 us
  local copies, waits for them, and re-layouts: 3.14 us -> 0 us
    ppermute x8 -> x7, starting transfers between devices: 23.9 us -> 17.5 us  [along_grp(): return lax.ppermute(value, 'grp', swap(group_count, turn))]
    ppermute x3 -> x5, waiting for transfers between devices: 5.99 us -> 2.72 us  [the longest x1 1.41 us: along_y(): return lax.ppermute(value, ('seq', 'head'), turns)]
    unnamed x16 -> x0, local copies, waits for them, and re-layouts: 3.14 us -> none
    ppermute x8 -> x7, waiting for transfers between devices: 8.79 us -> 6.98 us  [along_grp(): return lax.ppermute(value, 'grp', swap(group_count, turn))]
    ppermute x6, starting transfers between devices: 4.1 us -> 3.01 us  [along_seq(): return lax.ppermute(value, 'seq', swap(seq_count, turn))]
    ppermute x6, waiting for transfers between devices: 4.1 us -> 3.13 us  [along_seq(): return lax.ppermute(value, 'seq', swap(seq_count, turn))]
    ppermute x3 -> x5, starting transfers between devices: 7.26 us -> 7.66 us  [the longest x2 4.34 us: along_x(): return lax.ppermute(value, 'head', round_way if step else near)]
    pallas_call x7 -> x12, Pallas kernels: 9.59 us -> 9.75 us  [call(): pl.pallas_call(kernel, out_shape=out_shapes, in_specs=[VMEM_SPEC] * plain...]
  transfers between devices with their start and end apart: 17 -> 18, of which waited for: 10 -> 9; matrix products, arithmetic and copies ran while one was open for 0% -> 0% of each run, Pallas kernels for 0% -> 15%
where the time goes in v2:
time: 51.8 us; the launch traced here: 51.5 us
  starting transfers between devices  28.2 us (54%)
  waiting for transfers between devices  12.8 us (25%)
  Pallas kernels  9.75 us (19%)
  between operations  0.75 us (1%)
    ppermute x7, starting transfers between devices, along_grp(): return lax.ppermute(value, 'grp', swap(group_count, turn))  17.5 us
    pallas_call x12, Pallas kernels, call(): pl.pallas_call(kernel, out_shape=out_shapes, in_specs=[VMEM_SPEC] * plain...  9.75 us
    ppermute x7, waiting for transfers between devices, along_grp(): return lax.ppermute(value, 'grp', swap(group_count, turn))  6.98 us
    ppermute x2, starting transfers between devices, along_x(): return lax.ppermute(value, 'head', round_way if step else near)  4.34 us
    ppermute x6, waiting for transfers between devices, along_seq(): return lax.ppermute(value, 'seq', swap(seq_count, turn))  3.13 us
    ppermute x6, starting transfers between devices, along_seq(): return lax.ppermute(value, 'seq', swap(seq_count, turn))  3.01 us
    ppermute x1, starting transfers between devices, along_y(): return lax.ppermute(value, ('seq', 'head'), turns)  2.19 us
    ppermute x1, waiting for transfers between devices, along_y(): return lax.ppermute(value, ('seq', 'head'), turns)  1.41 us
  transfers between devices with their start and end apart: 18, of which 9 were waited for; matrix products, arithmetic and copies ran while one was open for 0% of the time, Pallas kernels for 15%

profile of v2, /device:TPU:32, one launch (start us, length us, event | category | flops | bytes accessed | tf_op | source)
XLA Modules:
  0.0 51.5 jit_solution(4662422302751247780)
XLA Ops:
  1.4 5.9 %collective-permute-start.1 = (bf16[128,256]{1,0:T(8,128)(2,1)S(1)}, bf16[128,256]{1,0:T(8,128)(2,1)S(1)}, u32[]{:S(2)}, u32[]{:S(2)}) collective-permute-start(bf16[128,256]{1,0:T(8,128)(2,1)S(1)} %shard_map.119.own_ref.right_ref), channel_id=1, source_target_pairs={{0,40},{8,32},{16,56},{24,48},{32,8},{40,0},{48,24},{56,16},{1,41}... | collective-permute-start | bytes 196616 | tf_op jit(solution)/shard_map/ppermute | solution.py:489
  7.4 1.0 %collective-permute-start = (bf16[128,256]{1,0:T(8,128)(2,1)S(1)}, bf16[128,256]{1,0:T(8,128)(2,1)S(1)}, u32[]{:S(2)}, u32[]{:S(2)}) collective-permute-start(bf16[128,256]{1,0:T(8,128)(2,1)S(1)} %shard_map.119.own_ref.right_ref), channel_id=1, source_target_pairs={{0,56},{8,48},{16,40},{24,32},{32,24},{40,16},{48,8},{56,0},{1,57}... | collective-permute-start | bytes 196616 | tf_op jit(solution)/shard_map/ppermute | solution.py:489
  8.4 0.9 %shard_map.120 = (f32[16,256]{1,0:T(8,128)S(1)}, f32[8,128]{1,0:T(8,128)S(1)}, f32[1,128]{1,0:T(1,128)S(1)}) custom-call(s32[8]{0:T(128)} %order_hbm, s32[8]{0:T(128)} %counts_hbm.1, s32[1,128]{1,0:T(1,128)} %mask_hbm.1, f32[1,16]{1,0:T(1,128)} %ratio_hbm.1), custom_call_target="tpu_custom_call" | custom-call | tf_op jit(solution)/shard_map/pallas_call | solution.py:453
  10.5 1.5 %collective-permute-start.3 = (f32[8,128]{1,0:T(8,128)S(1)}, f32[8,128]{1,0:T(8,128)S(1)}, u32[]{:S(2)}, u32[]{:S(2)}) collective-permute-start(f32[8,128]{1,0:T(8,128)S(1)} %add.12), channel_id=1, source_target_pairs={{0,2},{1,3},{2,0},{3,1},{4,6},{5,7},{6,4},{7,5},{8,10},{9,11},{10,... | collective-permute-start | bytes 12296 | tf_op jit(solution)/shard_map/ppermute | solution.py:505
  12.0 1.3 %shard_map.121 = (bf16[1024,128]{1,0:T(8,128)(2,1)S(1)}, bf16[1024,128]{1,0:T(8,128)(2,1)S(1)}, bf16[128,1024]{1,0:T(8,128)(2,1)S(1)}) custom-call(f32[1,128]{1,0:T(1,128)S(1)} %get-tuple-element.68.kept_ref, bf16[128,1024]{1,0:T(8,128)(2,1)} %bitcast.9, bf16[128,1024]{1,0:T(8,128)(2,1)} %bitcast.10), custom_call_target="tpu_custom_call" | custom-call | tf_op jit(solution)/shard_map/pallas_call | solution.py:453
  13.3 1.3 %collective-permute-done.far7 = bf16[128,256]{1,0:T(8,128)(2,1)S(1)} collective-permute-done((bf16[128,256]{1,0:T(8,128)(2,1)S(1)}, bf16[128,256]{1,0:T(8,128)(2,1)S(1)}, u32[]{:S(2)}, u32[]{:S(2)}) %collective-permute-start) | collective-permute-done | bytes 65568 | tf_op jit(solution)/shard_map/ppermute | solution.py:489
  14.7 0.9 %collective-permute-start.4 = (bf16[144,256]{1,0:T(8,128)(2,1)S(1)}, bf16[144,256]{1,0:T(8,128)(2,1)S(1)}, u32[]{:S(2)}, u32[]{:S(2)}) collective-permute-start(bf16[144,256]{1,0:T(8,128)(2,1)S(1)} %get-tuple-element.77), channel_id=1, source_target_pairs={{0,136},{8,128},{16,152},{24,144},{32,168},{40,160},{48,184},{56,1... | collective-permute-start | bytes 221192 | tf_op jit(solution)/shard_map/ppermute | solution.py:500
  15.7 2.2 %collective-permute-start.6 = (bf16[144,256]{1,0:T(8,128)(2,1)S(1)}, bf16[144,256]{1,0:T(8,128)(2,1)S(1)}, u32[]{:S(2)}, u32[]{:S(2)}) collective-permute-start(bf16[144,256]{1,0:T(8,128)(2,1)S(1)} %get-tuple-element.83), channel_id=1, source_target_pairs={{0,8},{8,0},{16,24},{24,16},{32,40},{40,32},{48,56},{56,48},{1,9},... | collective-permute-start | bytes 221192 | tf_op jit(solution)/shard_map/ppermute | solution.py:489
  18.9 1.3 %collective-permute-done.4.cross_ref = bf16[144,256]{1,0:T(8,128)(2,1)S(1)} collective-permute-done((bf16[144,256]{1,0:T(8,128)(2,1)S(1)}, bf16[144,256]{1,0:T(8,128)(2,1)S(1)}, u32[]{:S(2)}, u32[]{:S(2)}) %collective-permute-start.4) | collective-permute-done | bytes 73760 | tf_op jit(solution)/shard_map/ppermute | solution.py:500
  20.2 0.8 %collective-permute-done.6.group_ref = bf16[144,256]{1,0:T(8,128)(2,1)S(1)} collective-permute-done((bf16[144,256]{1,0:T(8,128)(2,1)S(1)}, bf16[144,256]{1,0:T(8,128)(2,1)S(1)}, u32[]{:S(2)}, u32[]{:S(2)}) %collective-permute-start.6) | collective-permute-done | bytes 73760 | tf_op jit(solution)/shard_map/ppermute | solution.py:489
  21.0 1.2 %collective-permute-done.7.seq_ref = bf16[144,256]{1,0:T(8,128)(2,1)S(1)} collective-permute-done((bf16[144,256]{1,0:T(8,128)(2,1)S(1)}, bf16[144,256]{1,0:T(8,128)(2,1)S(1)}, u32[]{:S(2)}, u32[]{:S(2)}) %collective-permute-start.7) | collective-permute-done | bytes 73760 | tf_op jit(solution)/shard_map/ppermute | solution.py:492
  23.0 2.8 %collective-permute-start.9 = (f32[8,128]{1,0:T(8,128)S(1)}, f32[8,128]{1,0:T(8,128)S(1)}, u32[]{:S(2)}, u32[]{:S(2)}) collective-permute-start(f32[8,128]{1,0:T(8,128)S(1)} %get-tuple-element.106), channel_id=1, source_target_pairs={{0,6},{1,7},{2,4},{3,5},{4,2},{5,3},{6,0},{7,1},{8,14},{9,15},{10,... | collective-permute-start | bytes 12296 | tf_op jit(solution)/shard_map/ppermute | solution.py:505
  25.8 3.3 %shard_map.126 = (bf16[384,256]{1,0:T(8,128)(2,1)S(1)}, f32[128,256]{1,0:T(8,128)S(1)}, f32[128,256]{1,0:T(8,128)S(1)}, f32[128,256]{1,0:T(8,128)S(1)}, f32[128,...) custom-call(f32[16,256]{1,0:T(8,128)S(1)} %get-tuple-element.66.fact, ...), custom_call_target="tpu_custom_call" | custom-call | flops 671088640 | tf_op jit(solution)/shard_map/pallas_call | solution.py:453
  29.4 1.2 %collective-permute-done.11.back_ref = bf16[384,256]{1,0:T(8,128)(2,1)S(1)} collective-permute-done((bf16[384,256]{1,0:T(8,128)(2,1)S(1)}, bf16[384,256]{1,0:T(8,128)(2,1)S(1)}, u32[]{:S(2)}, u32[]{:S(2)}) %collective-permute-start.11) | collective-permute-done | bytes 196640 | tf_op jit(solution)/shard_map/ppermute | solution.py:492
  30.9 1.8 %collective-permute-start.12 = (bf16[128,256]{1,0:T(8,128)(2,1)S(1)}, bf16[128,256]{1,0:T(8,128)(2,1)S(1)}, u32[]{:S(2)}, u32[]{:S(2)}) collective-permute-start(bf16[128,256]{1,0:T(8,128)(2,1)S(1)} %get-tuple-element.112.near_ref), channel_id=1, source_target_pairs={{0,8},{8,0},{16,24},{24,16},{32,40},{40,32},{48,56},{56,48},{1,9},... | collective-permute-start | bytes 196616 | tf_op jit(solution)/shard_map/ppermute | solution.py:489
  32.7 1.6 %collective-permute-start.13 = (bf16[128,256]{1,0:T(8,128)(2,1)S(1)}, bf16[128,256]{1,0:T(8,128)(2,1)S(1)}, u32[]{:S(2)}, u32[]{:S(2)}) collective-permute-start(bf16[128,256]{1,0:T(8,128)(2,1)S(1)} %get-tuple-element.114), channel_id=1, source_target_pairs={{0,128},{64,192},{128,0},{192,64},{1,129},{65,193},{129,1},{193,65... | collective-permute-start | bytes 196616 | tf_op jit(solution)/shard_map/ppermute | solution.py:492
  34.3 2.2 %collective-permute-start.10 = (f32[8,128]{1,0:T(8,128)S(1)}, f32[8,128]{1,0:T(8,128)S(1)}, u32[]{:S(2)}, u32[]{:S(2)}) collective-permute-start(f32[8,128]{1,0:T(8,128)S(1)} %add.14), channel_id=1, source_target_pairs={{0,129},{1,128},{2,131},{3,130},{4,133},{5,132},{6,135},{7,134},{6... | collective-permute-start | bytes 12296 | tf_op jit(solution)/shard_map/ppermute | solution.py:513
  36.5 1.2 %shard_map.127 = (bf16[128,1024]{1,0:T(8,128)(2,1)}, f32[128,1024]{1,0:T(8,128)S(1)}) custom-call(f32[16,256]{1,0:T(8,128)S(1)} %get-tuple-element.66.facts_ref, f32[128,1024]{1,0:T(8,128)S(1)} %get-tuple-element.95.output_t_ref, bf16[256,1024]{1,0:T(8,128)(2,1)S(1)} %get-tuple-element.96.own_score_grad, ...), custom_call_target="tpu_custom_call" | custom-call | flops 201326592 | tf_op jit(solution)/shard_map/pallas_call | solution.py:453
  37.7 1.4 %collective-permute-done.10 = f32[8,128]{1,0:T(8,128)S(1)} collective-permute-done((f32[8,128]{1,0:T(8,128)S(1)}, f32[8,128]{1,0:T(8,128)S(1)}, u32[]{:S(2)}, u32[]{:S(2)}) %collective-permute-start.10) | collective-permute-done | bytes 4128 | tf_op jit(solution)/shard_map/ppermute | solution.py:513
  39.2 3.6 %collective-permute-start.15 = (bf16[144,256]{1,0:T(8,128)(2,1)S(1)}, bf16[144,256]{1,0:T(8,128)(2,1)S(1)}, u32[]{:S(2)}, u32[]{:S(2)}) collective-permute-start(bf16[144,256]{1,0:T(8,128)(2,1)S(1)} %get-tuple-element.118), channel_id=1, source_target_pairs={{0,56},{8,48},{16,40},{24,32},{32,24},{40,16},{48,8},{56,0},{1,57}... | collective-permute-start | bytes 221192 | tf_op jit(solution)/shard_map/ppermute | solution.py:489
  42.9 2.9 %collective-permute-start.17 = (f32[8,128]{1,0:T(8,128)S(1)}, f32[8,128]{1,0:T(8,128)S(1)}, u32[]{:S(2)}, u32[]{:S(2)}) collective-permute-start(f32[8,128]{1,0:T(8,128)S(1)} %add.15.totals_ref), channel_id=1, source_target_pairs={{0,16},{8,24},{16,0},{24,8},{32,48},{40,56},{48,32},{56,40},{1,17}... | collective-permute-start | bytes 12296 | tf_op jit(solution)/shard_map/ppermute | solution.py:489
  45.8 2.0 %collective-permute-done.17.rest_ref = f32[8,128]{1,0:T(8,128)S(1)} collective-permute-done((f32[8,128]{1,0:T(8,128)S(1)}, f32[8,128]{1,0:T(8,128)S(1)}, u32[]{:S(2)}, u32[]{:S(2)}) %collective-permute-start.17) | collective-permute-done | bytes 4128 | tf_op jit(solution)/shard_map/ppermute | solution.py:489
  47.8 2.9 %collective-permute-done.16.far5 = bf16[144,256]{1,0:T(8,128)(2,1)S(1)} collective-permute-done((bf16[144,256]{1,0:T(8,128)(2,1)S(1)}, bf16[144,256]{1,0:T(8,128)(2,1)S(1)}, u32[]{:S(2)}, u32[]{:S(2)}) %collective-permute-start.16) | collective-permute-done | bytes 73760 | tf_op jit(solution)/shard_map/ppermute | solution.py:489
  50.7 0.8 %shard_map.130 = (bf16[128,1024]{1,0:T(8,128)(2,1)}, bf16[128,128]{1,0:T(8,128)(2,1)}, bf16[128,128]{1,0:T(8,128)(2,1)}, f32[1,4]{1,0:T(1,128)}) custom-call(f32[16,256]{1,0:T(8,128)S(1)} %get-tuple-element.66.facts_ref, f32[128,256]{1,0:T(8,128)S(1)} %get-tuple-element.117.local_ref, bf16[144,256]{1,0:T(8,128)(2,1)S(1)} %collective-permute-done.15.far7, ...), custom_call_target="tpu_custom_call" | custom-call | tf_op jit(solution)/shard_map/pallas_call | solution.py:453
  (28 shorter events, 4.5 us)
Async XLA Ops:
  1.4 11.9 %collective-permute-start.1 = (bf16[128,256]{1,0:T(8,128)(2,1)S(1)}, bf16[128,256]{1,0:T(8,128)(2,1)S(1)}, u32[]{:S(2)}, u32[]{:S(2)}) collective-permute-start(bf16[128,256]{1,0:T(8,128)(2,1)S(1)} %shard_map.119.own_ref.right_ref), channel_id=1, source_target_pairs={{0,40},{8,32},{16,56},{24,48},{32,8},{40,0},{48,24},{56,16},{1,41}... | collective-permute-start | bytes 196616 | tf_op jit(solution)/shard_map/ppermute | solution.py:489
  7.4 7.3 %collective-permute-start = (bf16[128,256]{1,0:T(8,128)(2,1)S(1)}, bf16[128,256]{1,0:T(8,128)(2,1)S(1)}, u32[]{:S(2)}, u32[]{:S(2)}) collective-permute-start(bf16[128,256]{1,0:T(8,128)(2,1)S(1)} %shard_map.119.own_ref.right_ref), channel_id=1, source_target_pairs={{0,56},{8,48},{16,40},{24,32},{32,24},{40,16},{48,8},{56,0},{1,57}... | collective-permute-start | bytes 196616 | tf_op jit(solution)/shard_map/ppermute | solution.py:489
  9.3 1.3 %collective-permute-start.2 = (f32[8,128]{1,0:T(8,128)S(1)}, f32[8,128]{1,0:T(8,128)S(1)}, u32[]{:S(2)}, u32[]{:S(2)}) collective-permute-start(f32[8,128]{1,0:T(8,128)S(1)} %get-tuple-element.67), channel_id=1, source_target_pairs={{0,64},{64,0},{128,192},{192,128},{1,65},{65,1},{129,193},{193,129... | collective-permute-start | bytes 12296 | tf_op jit(solution)/shard_map/ppermute | solution.py:492
  9.4 8.9 %collective-permute-start.5 = (bf16[128,256]{1,0:T(8,128)(2,1)S(1)}, bf16[128,256]{1,0:T(8,128)(2,1)S(1)}, u32[]{:S(2)}, u32[]{:S(2)}) collective-permute-start(bf16[128,256]{1,0:T(8,128)(2,1)S(1)} %shard_map.119.own_ref.right_ref), channel_id=1, source_target_pairs={{0,64},{64,0},{128,192},{192,128},{1,65},{65,1},{129,193},{193,129... | collective-permute-start | bytes 196616 | tf_op jit(solution)/shard_map/ppermute | solution.py:492
  10.5 4.1 %collective-permute-start.3 = (f32[8,128]{1,0:T(8,128)S(1)}, f32[8,128]{1,0:T(8,128)S(1)}, u32[]{:S(2)}, u32[]{:S(2)}) collective-permute-start(f32[8,128]{1,0:T(8,128)S(1)} %add.12), channel_id=1, source_target_pairs={{0,2},{1,3},{2,0},{3,1},{4,6},{5,7},{6,4},{7,5},{8,10},{9,11},{10,... | collective-permute-start | bytes 12296 | tf_op jit(solution)/shard_map/ppermute | solution.py:505
  14.7 5.4 %collective-permute-start.4 = (bf16[144,256]{1,0:T(8,128)(2,1)S(1)}, bf16[144,256]{1,0:T(8,128)(2,1)S(1)}, u32[]{:S(2)}, u32[]{:S(2)}) collective-permute-start(bf16[144,256]{1,0:T(8,128)(2,1)S(1)} %get-tuple-element.77), channel_id=1, source_target_pairs={{0,136},{8,128},{16,152},{24,144},{32,168},{40,160},{48,184},{56,1... | collective-permute-start | bytes 221192 | tf_op jit(solution)/shard_map/ppermute | solution.py:500
  15.7 5.3 %collective-permute-start.6 = (bf16[144,256]{1,0:T(8,128)(2,1)S(1)}, bf16[144,256]{1,0:T(8,128)(2,1)S(1)}, u32[]{:S(2)}, u32[]{:S(2)}) collective-permute-start(bf16[144,256]{1,0:T(8,128)(2,1)S(1)} %get-tuple-element.83), channel_id=1, source_target_pairs={{0,8},{8,0},{16,24},{24,16},{32,40},{40,32},{48,56},{56,48},{1,9},... | collective-permute-start | bytes 221192 | tf_op jit(solution)/shard_map/ppermute | solution.py:489
  17.9 4.4 %collective-permute-start.7 = (bf16[144,256]{1,0:T(8,128)(2,1)S(1)}, bf16[144,256]{1,0:T(8,128)(2,1)S(1)}, u32[]{:S(2)}, u32[]{:S(2)}) collective-permute-start(bf16[144,256]{1,0:T(8,128)(2,1)S(1)} %get-tuple-element.84), channel_id=1, source_target_pairs={{0,128},{64,192},{128,0},{192,64},{1,129},{65,193},{129,1},{193,65... | collective-permute-start | bytes 221192 | tf_op jit(solution)/shard_map/ppermute | solution.py:492
  22.3 3.5 %collective-permute-start.8 = (bf16[256,256]{1,0:T(8,128)(2,1)S(1)}, bf16[256,256]{1,0:T(8,128)(2,1)S(1)}, u32[]{:S(2)}, u32[]{:S(2)}) collective-permute-start(bf16[256,256]{1,0:T(8,128)(2,1)S(1)} %get-tuple-element.86.left_ref.right_ref), channel_id=1, source_target_pairs={{0,64},{64,0},{128,192},{192,128},{1,65},{65,1},{129,193},{193,129... | collective-permute-start | bytes 393224 | tf_op jit(solution)/shard_map/ppermute | solution.py:492
  23.0 6.2 %collective-permute-start.9 = (f32[8,128]{1,0:T(8,128)S(1)}, f32[8,128]{1,0:T(8,128)S(1)}, u32[]{:S(2)}, u32[]{:S(2)}) collective-permute-start(f32[8,128]{1,0:T(8,128)S(1)} %get-tuple-element.106), channel_id=1, source_target_pairs={{0,6},{1,7},{2,4},{3,5},{4,2},{5,3},{6,0},{7,1},{8,14},{9,15},{10,... | collective-permute-start | bytes 12296 | tf_op jit(solution)/shard_map/ppermute | solution.py:505
  29.1 1.5 %collective-permute-start.11 = (bf16[384,256]{1,0:T(8,128)(2,1)S(1)}, bf16[384,256]{1,0:T(8,128)(2,1)S(1)}, u32[]{:S(2)}, u32[]{:S(2)}) collective-permute-start(bf16[384,256]{1,0:T(8,128)(2,1)S(1)} %get-tuple-element.111), channel_id=1, source_target_pairs={{0,64},{64,0},{128,192},{192,128},{1,65},{65,1},{129,193},{193,129... | collective-permute-start | bytes 589832 | tf_op jit(solution)/shard_map/ppermute | solution.py:492
  30.7 8.4 %collective-permute-start.14 = (bf16[128,256]{1,0:T(8,128)(2,1)S(1)}, bf16[128,256]{1,0:T(8,128)(2,1)S(1)}, u32[]{:S(2)}, u32[]{:S(2)}) collective-permute-start(bf16[128,256]{1,0:T(8,128)(2,1)S(1)} %get-tuple-element.114), channel_id=1, source_target_pairs={{0,136},{8,128},{16,152},{24,144},{32,168},{40,160},{48,184},{56,1... | collective-permute-start | bytes 196616 | tf_op jit(solution)/shard_map/ppermute | solution.py:500
  30.9 8.2 %collective-permute-start.12 = (bf16[128,256]{1,0:T(8,128)(2,1)S(1)}, bf16[128,256]{1,0:T(8,128)(2,1)S(1)}, u32[]{:S(2)}, u32[]{:S(2)}) collective-permute-start(bf16[128,256]{1,0:T(8,128)(2,1)S(1)} %get-tuple-element.112.near_ref), channel_id=1, source_target_pairs={{0,8},{8,0},{16,24},{24,16},{32,40},{40,32},{48,56},{56,48},{1,9},... | collective-permute-start | bytes 196616 | tf_op jit(solution)/shard_map/ppermute | solution.py:489
  32.7 6.4 %collective-permute-start.13 = (bf16[128,256]{1,0:T(8,128)(2,1)S(1)}, bf16[128,256]{1,0:T(8,128)(2,1)S(1)}, u32[]{:S(2)}, u32[]{:S(2)}) collective-permute-start(bf16[128,256]{1,0:T(8,128)(2,1)S(1)} %get-tuple-element.114), channel_id=1, source_target_pairs={{0,128},{64,192},{128,0},{192,64},{1,129},{65,193},{129,1},{193,65... | collective-permute-start | bytes 196616 | tf_op jit(solution)/shard_map/ppermute | solution.py:492
  34.3 4.8 %collective-permute-start.10 = (f32[8,128]{1,0:T(8,128)S(1)}, f32[8,128]{1,0:T(8,128)S(1)}, u32[]{:S(2)}, u32[]{:S(2)}) collective-permute-start(f32[8,128]{1,0:T(8,128)S(1)} %add.14), channel_id=1, source_target_pairs={{0,129},{1,128},{2,131},{3,130},{4,133},{5,132},{6,135},{7,134},{6... | collective-permute-start | bytes 12296 | tf_op jit(solution)/shard_map/ppermute | solution.py:513
  39.2 8.6 %collective-permute-start.15 = (bf16[144,256]{1,0:T(8,128)(2,1)S(1)}, bf16[144,256]{1,0:T(8,128)(2,1)S(1)}, u32[]{:S(2)}, u32[]{:S(2)}) collective-permute-start(bf16[144,256]{1,0:T(8,128)(2,1)S(1)} %get-tuple-element.118), channel_id=1, source_target_pairs={{0,56},{8,48},{16,40},{24,32},{32,24},{40,16},{48,8},{56,0},{1,57}... | collective-permute-start | bytes 221192 | tf_op jit(solution)/shard_map/ppermute | solution.py:489
  42.9 7.8 %collective-permute-start.16 = (bf16[144,256]{1,0:T(8,128)(2,1)S(1)}, bf16[144,256]{1,0:T(8,128)(2,1)S(1)}, u32[]{:S(2)}, u32[]{:S(2)}) collective-permute-start(bf16[144,256]{1,0:T(8,128)(2,1)S(1)} %get-tuple-element.119), channel_id=1, source_target_pairs={{0,40},{8,32},{16,56},{24,48},{32,8},{40,0},{48,24},{56,16},{1,41}... | collective-permute-start | bytes 221192 | tf_op jit(solution)/shard_map/ppermute | solution.py:489
  42.9 4.9 %collective-permute-start.17 = (f32[8,128]{1,0:T(8,128)S(1)}, f32[8,128]{1,0:T(8,128)S(1)}, u32[]{:S(2)}, u32[]{:S(2)}) collective-permute-start(f32[8,128]{1,0:T(8,128)S(1)} %add.15.totals_ref), channel_id=1, source_target_pairs={{0,16},{8,24},{16,0},{24,8},{32,48},{40,56},{48,32},{56,40},{1,17}... | collective-permute-start | bytes 12296 | tf_op jit(solution)/shard_map/ppermute | solution.py:489

commit v3 on v2

--- a/solution.py
+++ b/solution.py
@@ -172,29 +172,22 @@
         grad_t_ref[:, part] = grad.T
 
 
-def route_kernel(facts_ref, totals_ref, own_ref, far7, far5, group_ref, seq_ref, cross_ref):
-    rows = own_ref.shape[0]
+def route_kernel(facts_ref, own_ref, far7, far5, group_ref, seq_ref, cross_ref):
     for number, ref in ((1, group_ref), (2, seq_ref), (3, cross_ref)):
         picked = far7[...].astype(F32) * fact(facts_ref, FROM7 + number)
         picked = picked + far5[...].astype(F32) * fact(facts_ref, FROM5 + number)
         if number == 2:
             picked = picked + own_ref[...].astype(F32) * fact(facts_ref, IS_PROMPT)
-        ref[:rows] = picked.astype(BF16)
-        store_tail(ref, rows, totals_ref[...])
-
-
-def select_kernel(
-    facts_ref, totals_ref, own_ref, far7, far5, group_ref, seq_ref, cross_ref, near_ref, sum_ref
-):
+        ref[...] = picked.astype(BF16)
+
+
+def select_kernel(facts_ref, own_ref, far7, far5, group_ref, seq_ref, cross_ref, near_ref):
     rows = own_ref.shape[0]
     first = far7[...].astype(F32) * fact(facts_ref, FROM7)
     first = first + far5[...].astype(F32) * fact(facts_ref, FROM5)
     first = first + own_ref[...].astype(F32) * fact(facts_ref, IS_PROMPT)
-    near_ref[:rows] = (first + group_ref[:rows].astype(F32)).astype(BF16)
-    near_ref[rows:] = (seq_ref[:rows].astype(F32) + cross_ref[:rows].astype(F32)).astype(BF16)
-    sum_ref[...] = (totals_ref[...] + decode(group_ref, rows)) + (
-        decode(seq_ref, rows) + decode(cross_ref, rows)
-    )
+    near_ref[:rows] = (first + group_ref[...].astype(F32)).astype(BF16)
+    near_ref[rows:] = (seq_ref[...].astype(F32) + cross_ref[...].astype(F32)).astype(BF16)
 
 
 def load_blocks(blocks, keys, values, keys_t, values_t):
@@ -271,8 +264,8 @@
     back_ref,
     first_ref,
     over_ref,
-    own_ref,
     output_t_ref,
+    own_rounded,
     own_score_grad,
     near_score_grad,
     mate_score_grad,
@@ -280,12 +273,12 @@
     keys,
     values,
     values_t,
-    own_key_acc,
-    own_value_acc,
-    near_key_acc,
-    near_value_acc,
-    mate_key_acc,
-    mate_value_acc,
+    powers,
+    prob_grad,
+    stats,
+    factors,
+    near_rounded,
+    mate_rounded,
 ):
     rows, dim = keys.shape[0] // 2, keys.shape[1]
     heads = query_ref.shape[0] // rows
@@ -293,63 +286,62 @@
     shade = LOG2_E * scaling
     load_blocks(((mate_ref, 0), (mate_ref, rows)), keys, values, keys_t, values_t)
     wide = 2 * rows
+    spans = [slice(pair * wide, (pair + 1) * wide) for pair in range(heads // 2)]
     bias = [fact(facts_ref, row, wide) for row in (BIAS_MATE, BIAS_CROSS)]
-    for pair in range(heads // 2):
-        both = slice(pair * wide, (pair + 1) * wide)
-        query = query_ref[both]
-        grad = grad_ref[both]
-        scores = dot(keys[...], query, 1, 1)
-        prob_grad = dot(values[...], grad, 1, 1)
+    for both in spans:
+        scores = dot(keys[...], query_ref[both], 1, 1)
+        prob_grad[:, both] = dot(values[...], grad_ref[both], 1, 1)
         pieces = [scores[:rows], scores[rows:]]
         tops = [jnp.max(pieces[i], axis=0, keepdims=True) + bias[i] for i in (0, 1)]
-        own_top, near_top = own_stats[0:1, both], near_stats[0:1, both]
-        top = jnp.maximum(jnp.maximum(own_top, near_top), jnp.maximum(tops[0], tops[1]))
-        powers = [jnp.exp2(pieces[i] * shade + (bias[i] - shade * top)) for i in (0, 1)]
-        own_fade = jnp.exp2((own_top - top) * shade)
-        near_fade = jnp.exp2((near_top - top) * shade)
-        total = own_stats[1:2, both] * own_fade + near_stats[1:2, both] * near_fade
-        for power in powers:
+        top = jnp.maximum(tops[0], tops[1])
+        total = jnp.zeros_like(top)
+        for i, piece in enumerate(pieces):
+            power = jnp.exp2(piece * shade + (bias[i] - shade * top))
             total = total + jnp.sum(power, axis=0, keepdims=True)
+            powers[i * rows : (i + 1) * rows, both] = power
+        stats[0:1, both] = top
+        stats[1:2, both] = total
+
+    sets = (
+        (own_powers, own_prob_grad, own_stats, own_values_t, own_rounded, own_score_grad),
+        (near_powers, near_prob_grad, near_stats, near_values_t, near_rounded, near_score_grad),
+        (powers, prob_grad, stats, values_t, mate_rounded, mate_score_grad),
+    )
+    for both in spans:
+        tops = [item[2][0:1, both] for item in sets]
+        top = jnp.maximum(jnp.maximum(tops[0], tops[1]), tops[2])
+        fades = [jnp.exp2((part - top) * shade) for part in tops]
+        total = sum(item[2][1:2, both] * fade for item, fade in zip(sets, fades))
         inverse = 1.0 / total
-        sets = (
-            (own_powers[:, both] * (own_fade * inverse), own_prob_grad[:, both], own_values_t),
-            (near_powers[:, both] * (near_fade * inverse), near_prob_grad[:, both], near_values_t),
-            (jnp.concatenate(powers, axis=0) * inverse, prob_grad, values_t),
+        output_t = None
+        for i, item in enumerate(sets):
+            factor = fades[i] * inverse
+            factors[i : i + 1, both] = factor
+            rounded = (item[0][:, both] * factor).astype(BF16)
+            item[4][:, both] = rounded
+            part = dot(item[3][...], rounded, 1, 0)
+            output_t = part if output_t is None else output_t + part
+        output_t_ref[:, both] = output_t
+        factors[3:4, both] = jnp.sum(
+            grad_t_ref[:, both].astype(F32) * output_t, axis=0, keepdims=True
         )
-        rounded = [probs.astype(BF16) for probs, _, _ in sets]
-        output_t = sum(dot(item[2][...], part, 1, 0) for item, part in zip(sets, rounded))
-        output_t_ref[:, both] = output_t
-        delta = jnp.sum(grad_t_ref[:, both].astype(F32) * output_t, axis=0, keepdims=True)
-        targets = (
-            (own_score_grad, own_key_acc, own_value_acc),
-            (near_score_grad, near_key_acc, near_value_acc),
-            (mate_score_grad, mate_key_acc, mate_value_acc),
-        )
-        for (probs, part_grad, _), part, (target, key_acc, value_acc) in zip(
-            sets, rounded, targets
-        ):
-            score_grad = (probs * (part_grad - delta)).astype(BF16)
-            target[:, both] = score_grad
-            key_part = dot(score_grad, query, 1, 0)
-            value_part = dot(part, grad, 1, 0)
-            if pair == 0:
-                key_acc[...] = key_part
-                value_acc[...] = value_part
-            else:
-                key_acc[...] += key_part
-                value_acc[...] += value_part
-
-    for key_acc, value_acc, number, ref, start in (
-        (mate_key_acc, mate_value_acc, 0, back_ref, 0),
-        (mate_key_acc, mate_value_acc, 1, back_ref, rows),
-        (own_key_acc, own_value_acc, 0, back_ref, 2 * rows),
-        (near_key_acc, near_value_acc, 0, first_ref, 0),
-        (near_key_acc, near_value_acc, 1, over_ref, 0),
-        (own_key_acc, own_value_acc, 1, own_ref, 0),
+
+    for both in spans:
+        delta = factors[3:4, both]
+        for i, item in enumerate(sets):
+            probs = item[0][:, both] * factors[i : i + 1, both]
+            item[5][:, both] = (probs * (item[1][:, both] - delta)).astype(BF16)
+
+    for item, near_out, over_out in (
+        (sets[2], (back_ref, 0), (back_ref, rows)),
+        (sets[1], (first_ref, 0), (over_ref, 0)),
     ):
-        part = slice(number * rows, (number + 1) * rows)
-        ref[start : start + rows, :dim] = (key_acc[part] * scaling).astype(ref.dtype)
-        ref[start : start + rows, dim:] = value_acc[part].astype(ref.dtype)
+        key_part = dot(item[5][...], query_ref[...], 1, 0) * scaling
+        value_part = dot(item[4][...], grad_ref[...], 1, 0)
+        for number, (ref, start) in enumerate((near_out, over_out)):
+            part = slice(number * rows, (number + 1) * rows)
+            ref[start : start + rows, :dim] = key_part[part].astype(ref.dtype)
+            ref[start : start + rows, dim:] = value_part[part].astype(ref.dtype)
 
 
 def query_kernel(
@@ -361,8 +353,15 @@
     own_keys_t,
     near_keys_t,
     mate_keys_t,
+    own_rounded,
+    query_ref,
+    grad_ref,
     attended_ref,
     query_grad_ref,
+    back_ref,
+    local_ref,
+    key_acc,
+    value_acc,
 ):
     rows = attended_ref.shape[0]
     dim = output_t_ref.shape[0]
@@ -376,6 +375,14 @@
             + dot(near_keys_t[...], near_score_grad[:, both], 1, 0)
             + dot(mate_keys_t[...], mate_score_grad[:, both], 1, 0)
         )
+        key_part = dot(own_score_grad[:, both], query_ref[both], 1, 0)
+        value_part = dot(own_rounded[:, both], grad_ref[both], 1, 0)
+        if pair == 0:
+            key_acc[...] = key_part
+            value_acc[...] = value_part
+        else:
+            key_acc[...] += key_part
+            value_acc[...] += value_part
         query_grad = (grad_t * scaling).T
         output = (output_t_ref[:, both] * valid).T
         for i in (0, 1):
@@ -383,30 +390,51 @@
             part = slice(i * rows, (i + 1) * rows)
             attended_ref[:, span] = output[part].astype(BF16)
             query_grad_ref[:, span] = query_grad[part]
-
-
-def merge_kernel(first_ref, over_ref, own_ref, back_ref, near_out, over_out, local_ref):
+    for number, ref in ((0, back_ref), (1, local_ref)):
+        part = slice(number * rows, (number + 1) * rows)
+        ref[:, :dim] = (key_acc[part] * scaling).astype(ref.dtype)
+        ref[:, dim:] = value_acc[part].astype(ref.dtype)
+
+
+def merge_kernel(totals_ref, first_ref, over_ref, back_ref, near_out, over_out):
     rows = first_ref.shape[0]
-    near_out[...] = (first_ref[...] + back_ref[:rows].astype(F32)).astype(BF16)
-    over_out[...] = (over_ref[...] + back_ref[rows : 2 * rows].astype(F32)).astype(BF16)
-    local_ref[...] = own_ref[...] + back_ref[2 * rows :].astype(F32)
+    near_out[:rows] = (first_ref[...] + back_ref[:rows].astype(F32)).astype(BF16)
+    over_out[:rows] = (over_ref[...] + back_ref[rows:].astype(F32)).astype(BF16)
+    store_tail(near_out, rows, totals_ref[...])
+    store_tail(over_out, rows, totals_ref[...])
 
 
 def return_kernel(
-    facts_ref, totals_ref, near_ref, local_ref, group_ref, seq_ref, cross_ref, out_ref, pay7, pay5
+    facts_ref,
+    totals_ref,
+    near_ref,
+    group_ref,
+    seq_ref,
+    cross_ref,
+    prompt_ref,
+    pay7,
+    pay5,
+    sum_ref,
 ):
-    rows = near_ref.shape[0]
-    sums = [ref[...].astype(F32) for ref in (near_ref, group_ref, seq_ref, cross_ref)]
-    out_ref[...] = local_ref[...] + (sums[0] + sums[2]) * fact(facts_ref, IS_PROMPT)
+    rows = prompt_ref.shape[0]
+    refs = (near_ref, group_ref, seq_ref, cross_ref)
+    sums = [ref[:rows].astype(F32) for ref in refs]
+    prompt_ref[...] = (sums[0] + sums[2]) * fact(facts_ref, IS_PROMPT)
+    totals = (totals_ref[...] + decode(group_ref, rows)) + (
+        decode(seq_ref, rows) + decode(cross_ref, rows)
+    )
+    sum_ref[...] = totals
     for ref, base in ((pay7, FROM7), (pay5, FROM5)):
         total = sum(part * fact(facts_ref, base + i) for i, part in enumerate(sums))
         ref[:rows] = total.astype(BF16)
-        store_tail(ref, rows, totals_ref[...])
+        store_tail(ref, rows, totals)
 
 
 def finish_kernel(
     facts_ref,
     local_ref,
+    mate_ref,
+    prompt_ref,
     far7,
     far5,
     totals_ref,
@@ -436,7 +464,8 @@
     mine = row.astype(F32) == fact(facts_ref, PAIR_ROW, 128)
     scale = jnp.sum(jnp.where(mine, weight, 0.0), axis=0, keepdims=True)
     far_sum = far7[:rows].astype(F32) + far5[:rows].astype(F32)
-    total = local_ref[...] + far_sum * fact(facts_ref, IS_PROMPT)
+    total = local_ref[...] + mate_ref[...].astype(F32) + prompt_ref[...]
+    total = total + far_sum * fact(facts_ref, IS_PROMPT)
     key_grad_ref[...] = (total[:, :dim] * scale).astype(BF16)
     value_grad_ref[...] = (total[:, dim:] * scale).astype(BF16)
     for start in range(0, query_grad_ref.shape[1], dim):
@@ -505,12 +534,7 @@
         return lax.ppermute(value, "head", round_way if step else near)
 
     def along_y(value):
-        turns = [
-            (s * head_count + h, (s ^ 2) * head_count + (h ^ 1))
-            for s in range(seq_count)
-            for h in range(head_count)
-        ]
-        return lax.ppermute(value, ("seq", "head"), turns)
+        return lax.ppermute(value, "head", swap(head_count, 1))
 
     own = call(
         pack_kernel, grads, (key_heads[0], value_heads[0]), scratch=[dma((2,))], in_hbm=2
@@ -540,13 +564,11 @@
         scratch=[pltpu.VMEM((every, dim), BF16), dma((2, heads))],
         in_hbm=2,
     )
-    totals = totals + along_seq(totals, 1)
-    part = along_x(totals, 0)
+    part = along_y(totals)
     far7, far5, totals, query_rows = tie((far7, far5, totals, query_rows))
     totals = totals + part
-    to_group, to_seq, to_cross = call(
-        route_kernel, [packed] * 3, (facts, totals, own, far7, far5)
-    )
+    far7, far5, totals = tie((far7, far5, totals))
+    to_group, to_seq, to_cross = call(route_kernel, [grads] * 3, (facts, own, far7, far5))
     from_seq = along_seq(to_seq, 2)
     from_group = along_grp(to_group, 1)
     from_cross = across(to_cross)
@@ -567,25 +589,26 @@
         )
 
     own_set = early((BIAS_OWN, None), True, mate_own, own)
-    from_cross, own_powers = tie((from_cross, own_set[0]))
-    near, totals = call(
+    totals = totals + along_x(totals, 1)
+    from_cross, own_powers, totals = tie((from_cross, own_set[0], totals))
+    near = call(
         select_kernel,
-        [shape((2 * rows, both), BF16), total_tile],
-        (facts, totals, own, far7, far5, from_group, from_seq, from_cross),
+        shape((2 * rows, both), BF16),
+        (facts, own, far7, far5, from_group, from_seq, from_cross),
     )
     mate = along_seq(near, 1)
     near_set = early((BIAS_FIRST, BIAS_OVER), False, near, near)
     near_powers, totals = tie((near_set[0], totals))
-    part = along_x(totals, 1)
+    part = along_x(totals, 0)
     mate, near_powers = tie((mate, near_powers))
-    back, first, over, local, output_t, own_sg, near_sg, mate_sg, mate_keys_t = call(
+    back, first, over, output_t, own_rounded, own_sg, near_sg, mate_sg, mate_keys_t = call(
         late_kernel,
         [
-            shape((3 * rows, both), BF16),
-            grads_wide,
+            shape((2 * rows, both), BF16),
             grads_wide,
             grads_wide,
             shape((dim, every), F32),
+            shape((2 * rows, every), BF16),
             shape((2 * rows, every), BF16),
             shape((2 * rows, every), BF16),
             shape((2 * rows, every), BF16),
@@ -611,34 +634,47 @@
             pltpu.VMEM((2 * rows, dim), BF16),
             pltpu.VMEM((dim, 2 * rows), BF16),
         ]
-        + [pltpu.VMEM((2 * rows, dim), F32)] * 6,
+        + [pltpu.VMEM((2 * rows, every), F32)] * 2
+        + [pltpu.VMEM((8, every), F32)] * 2
+        + [pltpu.VMEM((2 * rows, every), BF16)] * 2,
         flops=40 * rows * every * dim,
     )
     back, totals = tie((back, totals))
     back, totals = tie((back, totals + part))
-    part = along_y(totals)
     back = along_seq(back, 1)
-    near_sum, over_sum, local = call(
-        merge_kernel, [grads, grads, grads_wide], (first, over, local, back)
-    )
+    totals = totals + along_seq(totals, 1)
+    near_sum, over_sum = call(merge_kernel, [packed, packed], (totals, first, over, back))
     from_seq = along_seq(over_sum, 2)
     from_group = along_grp(near_sum, 1)
     from_cross = across(over_sum)
-    totals = totals + part
-    attended, query_part = call(
+    attended, query_part, own_back, local = call(
         query_kernel,
-        [shape((rows, width), BF16), shape((rows, width), F32)],
-        (facts, output_t, own_sg, near_sg, mate_sg, own_set[3], near_set[3], mate_keys_t),
-        flops=12 * rows * every * dim,
+        [shape((rows, width), BF16), shape((rows, width), F32), grads, grads_wide],
+        (
+            facts,
+            output_t,
+            own_sg,
+            near_sg,
+            mate_sg,
+            own_set[3],
+            near_set[3],
+            mate_keys_t,
+            own_rounded,
+            query_rows,
+            grad_rows,
+        ),
+        scratch=[pltpu.VMEM((2 * rows, dim), F32)] * 2,
+        flops=20 * rows * every * dim,
     )
     from_cross, query_part = tie((from_cross, query_part))
-    local, pay7, pay5 = call(
+    from_prompt, pay7, pay5, totals = call(
         return_kernel,
-        [grads_wide, packed, packed],
-        (facts, totals, near_sum, local, from_group, from_seq, from_cross),
+        [grads_wide, packed, packed, total_tile],
+        (facts, totals, near_sum, from_group, from_seq, from_cross),
     )
     far7 = along_grp(pay7, 7)
     far5 = along_grp(pay5, 5)
+    own_back = along_seq(own_back, 1)
     rest = along_grp(totals, 2)
     query_grad, key_grad, value_grad, loss = call(
         finish_kernel,
@@ -648,7 +684,7 @@
             shape((rows, dim), BF16),
             shape((1, group_count // 2), F32),
         ],
-        (facts, local, far7, far5, totals, rest, query_part),
+        (facts, local, own_back, from_prompt, far7, far5, totals, rest, query_part),
     )
     return attended[None], query_grad[None], key_grad[None], value_grad[None], loss[0]
 

time: 51.8 us -> 49 us (0.946)
  waiting for transfers between devices: 12.8 us -> 11.4 us
  Pallas kernels: 9.75 us -> 8.7 us
    ppermute x2, waiting for transfers between devices: 0.01 us -> 2.32 us  [along_x(): return lax.ppermute(value, 'head', round_way if step else near)]
    ppermute x6 -> x7, waiting for transfers between devices: 3.13 us -> 1.38 us  [along_seq(): return lax.ppermute(value, 'seq', swap(seq_count, turn))]
    ppermute x6 -> x7, starting transfers between devices: 3.01 us -> 1.51 us  [along_seq(): return lax.ppermute(value, 'seq', swap(seq_count, turn))]
    ppermute x1, waiting for transfers between devices: 1.41 us -> 0.01 us  [along_y(): return lax.ppermute(value, 'head', swap(head_count, 1))]
    ppermute x1, starting transfers between devices: 2.19 us -> 3.28 us  [along_y(): return lax.ppermute(value, 'head', swap(head_count, 1))]
    pallas_call x12, Pallas kernels: 9.75 us -> 8.7 us  [call(): pl.pallas_call(kernel, out_shape=out_shapes, in_specs=[VMEM_SPEC] * plain...]
    ppermute x2, starting transfers between devices: 4.34 us -> 3.31 us  [along_x(): return lax.ppermute(value, 'head', round_way if step else near)]
    ppermute x2, starting transfers between devices: 1.14 us -> 2.07 us  [across(): return lax.ppermute(value, ('seq', 'grp'), turns)]
  transfers between devices with their start and end apart: 18 -> 19, of which waited for: 9 -> 10; matrix products, arithmetic and copies ran while one was open for 0% -> 0% of each run, Pallas kernels for 15% -> 14%
where the time goes in v3:
time: 49 us; the launch traced here: 48.7 us
  starting transfers between devices  27.9 us (57%)
  waiting for transfers between devices  11.4 us (23%)
  Pallas kernels  8.7 us (18%)
  between operations  0.73 us (1%)
    ppermute x7, starting transfers between devices, along_grp(): return lax.ppermute(value, 'grp', swap(group_count, turn))  17.7 us
    pallas_call x12, Pallas kernels, call(): pl.pallas_call(kernel, out_shape=out_shapes, in_specs=[VMEM_SPEC] * plain...  8.7 us
    ppermute x7, waiting for transfers between devices, along_grp(): return lax.ppermute(value, 'grp', swap(group_count, turn))  6.61 us
    ppermute x2, starting transfers between devices, along_x(): return lax.ppermute(value, 'head', round_way if step else near)  3.31 us
    ppermute x1, starting transfers between devices, along_y(): return lax.ppermute(value, 'head', swap(head_count, 1))  3.28 us
    ppermute x2, waiting for transfers between devices, along_x(): return lax.ppermute(value, 'head', round_way if step else near)  2.32 us
    ppermute x2, starting transfers between devices, across(): return lax.ppermute(value, ('seq', 'grp'), turns)  2.07 us
    ppermute x7, starting transfers between devices, along_seq(): return lax.ppermute(value, 'seq', swap(seq_count, turn))  1.51 us
  transfers between devices with their start and end apart: 19, of which 10 were waited for; matrix products, arithmetic and copies ran while one was open for 0% of the time, Pallas kernels for 14%

profile of v3, /device:TPU:32, one launch (start us, length us, event | category | flops | bytes accessed | tf_op | source)
XLA Modules:
  0.0 48.7 jit_solution(11015505973308137447)
XLA Ops:
  0.6 0.8 %shard_map.119.own_ref.right_ref = bf16[128,256]{1,0:T(8,128)(2,1)S(1)} custom-call(bf16[128,128]{1,0:T(8,128)(2,1)} %bitcast.11, bf16[128,128]{1,0:T(8,128)(2,1)} %bitcast.12), custom_call_target="tpu_custom_call" | custom-call | tf_op jit(solution)/shard_map/pallas_call | solution.py:482
  1.4 5.9 %collective-permute-start.1 = (bf16[128,256]{1,0:T(8,128)(2,1)S(1)}, bf16[128,256]{1,0:T(8,128)(2,1)S(1)}, u32[]{:S(2)}, u32[]{:S(2)}) collective-permute-start(bf16[128,256]{1,0:T(8,128)(2,1)S(1)} %shard_map.119.own_ref.right_ref), channel_id=1, source_target_pairs={{0,40},{8,32},{16,56},{24,48},{32,8},{40,0},{48,24},{56,16},{1,41}... | collective-permute-start | bytes 196616 | tf_op jit(solution)/shard_map/ppermute | solution.py:518
  7.4 1.0 %collective-permute-start = (bf16[128,256]{1,0:T(8,128)(2,1)S(1)}, bf16[128,256]{1,0:T(8,128)(2,1)S(1)}, u32[]{:S(2)}, u32[]{:S(2)}) collective-permute-start(bf16[128,256]{1,0:T(8,128)(2,1)S(1)} %shard_map.119.own_ref.right_ref), channel_id=1, source_target_pairs={{0,56},{8,48},{16,40},{24,32},{32,24},{40,16},{48,8},{56,0},{1,57}... | collective-permute-start | bytes 196616 | tf_op jit(solution)/shard_map/ppermute | solution.py:518
  8.4 0.9 %shard_map.120 = (f32[16,256]{1,0:T(8,128)S(1)}, f32[8,128]{1,0:T(8,128)S(1)}, f32[1,128]{1,0:T(1,128)S(1)}) custom-call(s32[8]{0:T(128)} %order_hbm, s32[8]{0:T(128)} %counts_hbm.1, s32[1,128]{1,0:T(1,128)} %mask_hbm.1, f32[1,16]{1,0:T(1,128)} %ratio_hbm.1), custom_call_target="tpu_custom_call" | custom-call | tf_op jit(solution)/shard_map/pallas_call | solution.py:482
  9.3 3.3 %collective-permute-start.2 = (f32[8,128]{1,0:T(8,128)S(1)}, f32[8,128]{1,0:T(8,128)S(1)}, u32[]{:S(2)}, u32[]{:S(2)}) collective-permute-start(f32[8,128]{1,0:T(8,128)S(1)} %get-tuple-element.80), channel_id=1, source_target_pairs={{0,1},{1,0},{2,3},{3,2},{4,5},{5,4},{6,7},{7,6},{8,9},{9,8},{10,11... | collective-permute-start | bytes 12296 | tf_op jit(solution)/shard_map/ppermute | solution.py:537
  12.6 1.3 %shard_map.121 = (bf16[1024,128]{1,0:T(8,128)(2,1)S(1)}, bf16[1024,128]{1,0:T(8,128)(2,1)S(1)}, bf16[128,1024]{1,0:T(8,128)(2,1)S(1)}) custom-call(f32[1,128]{1,0:T(1,128)S(1)} %get-tuple-element.72.kept_ref, bf16[128,1024]{1,0:T(8,128)(2,1)} %bitcast.9, bf16[128,1024]{1,0:T(8,128)(2,1)} %bitcast.10), custom_call_target="tpu_custom_call" | custom-call | tf_op jit(solution)/shard_map/pallas_call | solution.py:482
  13.9 0.8 %collective-permute-done.far7 = bf16[128,256]{1,0:T(8,128)(2,1)S(1)} collective-permute-done((bf16[128,256]{1,0:T(8,128)(2,1)S(1)}, bf16[128,256]{1,0:T(8,128)(2,1)S(1)}, u32[]{:S(2)}, u32[]{:S(2)}) %collective-permute-start) | collective-permute-done | bytes 65568 | tf_op jit(solution)/shard_map/ppermute | solution.py:518
  14.7 1.0 %collective-permute-start.3 = (bf16[128,256]{1,0:T(8,128)(2,1)S(1)}, bf16[128,256]{1,0:T(8,128)(2,1)S(1)}, u32[]{:S(2)}, u32[]{:S(2)}) collective-permute-start(bf16[128,256]{1,0:T(8,128)(2,1)S(1)} %get-tuple-element.83), channel_id=1, source_target_pairs={{0,136},{8,128},{16,152},{24,144},{32,168},{40,160},{48,184},{56,1... | collective-permute-start | bytes 196616 | tf_op jit(solution)/shard_map/ppermute | solution.py:529
  15.7 2.2 %collective-permute-start.6 = (bf16[128,256]{1,0:T(8,128)(2,1)S(1)}, bf16[128,256]{1,0:T(8,128)(2,1)S(1)}, u32[]{:S(2)}, u32[]{:S(2)}) collective-permute-start(bf16[128,256]{1,0:T(8,128)(2,1)S(1)} %get-tuple-element.90), channel_id=1, source_target_pairs={{0,8},{8,0},{16,24},{24,16},{32,40},{40,32},{48,56},{56,48},{1,9},... | collective-permute-start | bytes 196616 | tf_op jit(solution)/shard_map/ppermute | solution.py:518
  18.3 2.8 %collective-permute-start.5 = (f32[8,128]{1,0:T(8,128)S(1)}, f32[8,128]{1,0:T(8,128)S(1)}, u32[]{:S(2)}, u32[]{:S(2)}) collective-permute-start(f32[8,128]{1,0:T(8,128)S(1)} %add.12), channel_id=1, source_target_pairs={{0,6},{1,7},{2,4},{3,5},{4,2},{5,3},{6,0},{7,1},{8,14},{9,15},{10,... | collective-permute-start | bytes 12296 | tf_op jit(solution)/shard_map/ppermute | solution.py:534
  21.6 1.5 %collective-permute-done.5 = f32[8,128]{1,0:T(8,128)S(1)} collective-permute-done((f32[8,128]{1,0:T(8,128)S(1)}, f32[8,128]{1,0:T(8,128)S(1)}, u32[]{:S(2)}, u32[]{:S(2)}) %collective-permute-start.5) | collective-permute-done | bytes 4128 | tf_op jit(solution)/shard_map/ppermute | solution.py:534
  24.7 2.1 %shard_map.126 = (bf16[256,256]{1,0:T(8,128)(2,1)S(1)}, f32[128,256]{1,0:T(8,128)S(1)}, f32[128,256]{1,0:T(8,128)S(1)}, f32[128,1024]{1,0:T(8,128)S(1)}, bf16[25...) custom-call(f32[16,256]{1,0:T(8,128)S(1)} %get-tuple-element.70.fact, ...), custom_call_target="tpu_custom_call" | custom-call | flops 671088640 | tf_op jit(solution)/shard_map/pallas_call | solution.py:482
  26.8 0.8 %collective-permute-done.10 = f32[8,128]{1,0:T(8,128)S(1)} collective-permute-done((f32[8,128]{1,0:T(8,128)S(1)}, f32[8,128]{1,0:T(8,128)S(1)}, u32[]{:S(2)}, u32[]{:S(2)}) %collective-permute-start.10) | collective-permute-done | bytes 4128 | tf_op jit(solution)/shard_map/ppermute | solution.py:534
  28.1 0.8 %collective-permute-done.11 = f32[8,128]{1,0:T(8,128)S(1)} collective-permute-done((f32[8,128]{1,0:T(8,128)S(1)}, f32[8,128]{1,0:T(8,128)S(1)}, u32[]{:S(2)}, u32[]{:S(2)}) %collective-permute-start.11) | collective-permute-done | bytes 4128 | tf_op jit(solution)/shard_map/ppermute | solution.py:521
  29.0 1.1 %collective-permute-start.15 = (bf16[144,256]{1,0:T(8,128)(2,1)S(1)}, bf16[144,256]{1,0:T(8,128)(2,1)S(1)}, u32[]{:S(2)}, u32[]{:S(2)}) collective-permute-start(bf16[144,256]{1,0:T(8,128)(2,1)S(1)} %get-tuple-element.121), channel_id=1, source_target_pairs={{0,136},{8,128},{16,152},{24,144},{32,168},{40,160},{48,184},{56,1... | collective-permute-start | bytes 221192 | tf_op jit(solution)/shard_map/ppermute | solution.py:529
  30.1 2.0 %collective-permute-start.13 = (bf16[144,256]{1,0:T(8,128)(2,1)S(1)}, bf16[144,256]{1,0:T(8,128)(2,1)S(1)}, u32[]{:S(2)}, u32[]{:S(2)}) collective-permute-start(bf16[144,256]{1,0:T(8,128)(2,1)S(1)} %get-tuple-element.120.near_ref), channel_id=1, source_target_pairs={{0,8},{8,0},{16,24},{24,16},{32,40},{40,32},{48,56},{56,48},{1,9},... | collective-permute-start | bytes 221192 | tf_op jit(solution)/shard_map/ppermute | solution.py:518
  32.6 1.4 %shard_map.127 = (bf16[128,1024]{1,0:T(8,128)(2,1)}, f32[128,1024]{1,0:T(8,128)S(1)}, bf16[128,256]{1,0:T(8,128)(2,1)S(1)}, f32[128,256]{1,0:T(8,128)S(1)}) custom-call(f32[16,256]{1,0:T(8,128)S(1)} %get-tuple-element.70.facts_ref, f32[128,1024]{1,0:T(8,128)S(1)} %get-tuple-element.101.output_t_ref, bf16[256,1024]{1,0:T(8,128)(2,1)S(1)} %get-tuple-element.102.own_score_grad, ...), custom_call_target="tpu_custom_call" | custom-call | flops 335544320 | tf_op jit(solution)/shard_map/pallas_call | solution.py:482
  33.9 1.1 %collective-permute-done.15.cross_ref = bf16[144,256]{1,0:T(8,128)(2,1)S(1)} collective-permute-done((bf16[144,256]{1,0:T(8,128)(2,1)S(1)}, bf16[144,256]{1,0:T(8,128)(2,1)S(1)}, u32[]{:S(2)}, u32[]{:S(2)}) %collective-permute-start.15) | collective-permute-done | bytes 73760 | tf_op jit(solution)/shard_map/ppermute | solution.py:529
  35.1 1.1 %collective-permute-done.13.group_ref = bf16[144,256]{1,0:T(8,128)(2,1)S(1)} collective-permute-done((bf16[144,256]{1,0:T(8,128)(2,1)S(1)}, bf16[144,256]{1,0:T(8,128)(2,1)S(1)}, u32[]{:S(2)}, u32[]{:S(2)}) %collective-permute-start.13) | collective-permute-done | bytes 73760 | tf_op jit(solution)/shard_map/ppermute | solution.py:518
  36.6 4.0 %collective-permute-start.16 = (bf16[144,256]{1,0:T(8,128)(2,1)S(1)}, bf16[144,256]{1,0:T(8,128)(2,1)S(1)}, u32[]{:S(2)}, u32[]{:S(2)}) collective-permute-start(bf16[144,256]{1,0:T(8,128)(2,1)S(1)} %get-tuple-element.125), channel_id=1, source_target_pairs={{0,56},{8,48},{16,40},{24,32},{32,24},{40,16},{48,8},{56,0},{1,57}... | collective-permute-start | bytes 221192 | tf_op jit(solution)/shard_map/ppermute | solution.py:518
  40.6 2.6 %collective-permute-start.18 = (f32[8,128]{1,0:T(8,128)S(1)}, f32[8,128]{1,0:T(8,128)S(1)}, u32[]{:S(2)}, u32[]{:S(2)}) collective-permute-start(f32[8,128]{1,0:T(8,128)S(1)} %get-tuple-element.127.totals_ref), channel_id=1, source_target_pairs={{0,16},{8,24},{16,0},{24,8},{32,48},{40,56},{48,32},{56,40},{1,17}... | collective-permute-start | bytes 12296 | tf_op jit(solution)/shard_map/ppermute | solution.py:518
  43.2 1.9 %collective-permute-done.18.rest_ref = f32[8,128]{1,0:T(8,128)S(1)} collective-permute-done((f32[8,128]{1,0:T(8,128)S(1)}, f32[8,128]{1,0:T(8,128)S(1)}, u32[]{:S(2)}, u32[]{:S(2)}) %collective-permute-start.18) | collective-permute-done | bytes 4128 | tf_op jit(solution)/shard_map/ppermute | solution.py:518
  45.1 2.8 %collective-permute-done.17.far5 = bf16[144,256]{1,0:T(8,128)(2,1)S(1)} collective-permute-done((bf16[144,256]{1,0:T(8,128)(2,1)S(1)}, bf16[144,256]{1,0:T(8,128)(2,1)S(1)}, u32[]{:S(2)}, u32[]{:S(2)}) %collective-permute-start.17) | collective-permute-done | bytes 73760 | tf_op jit(solution)/shard_map/ppermute | solution.py:518
  47.9 0.8 %shard_map.130 = (bf16[128,1024]{1,0:T(8,128)(2,1)}, bf16[128,128]{1,0:T(8,128)(2,1)}, bf16[128,128]{1,0:T(8,128)(2,1)}, f32[1,4]{1,0:T(1,128)}) custom-call(f32[16,256]{1,0:T(8,128)S(1)} %get-tuple-element.70.facts_ref, f32[128,256]{1,0:T(8,128)S(1)} %get-tuple-element.110.local_ref, bf16[128,256]{1,0:T(8,128)(2,1)S(1)} %collective-permute-done.9.mate_ref, ...), custom_call_target="tpu_custom_call" | custom-call | tf_op jit(solution)/shard_map/pallas_call | solution.py:482
  (30 shorter events, 4.0 us)
Async XLA Ops:
  1.4 12.4 %collective-permute-start.1 = (bf16[128,256]{1,0:T(8,128)(2,1)S(1)}, bf16[128,256]{1,0:T(8,128)(2,1)S(1)}, u32[]{:S(2)}, u32[]{:S(2)}) collective-permute-start(bf16[128,256]{1,0:T(8,128)(2,1)S(1)} %shard_map.119.own_ref.right_ref), channel_id=1, source_target_pairs={{0,40},{8,32},{16,56},{24,48},{32,8},{40,0},{48,24},{56,16},{1,41}... | collective-permute-start | bytes 196616 | tf_op jit(solution)/shard_map/ppermute | solution.py:518
  7.4 7.3 %collective-permute-start = (bf16[128,256]{1,0:T(8,128)(2,1)S(1)}, bf16[128,256]{1,0:T(8,128)(2,1)S(1)}, u32[]{:S(2)}, u32[]{:S(2)}) collective-permute-start(bf16[128,256]{1,0:T(8,128)(2,1)S(1)} %shard_map.119.own_ref.right_ref), channel_id=1, source_target_pairs={{0,56},{8,48},{16,40},{24,32},{32,24},{40,16},{48,8},{56,0},{1,57}... | collective-permute-start | bytes 196616 | tf_op jit(solution)/shard_map/ppermute | solution.py:518
  8.4 12.7 %collective-permute-start.4 = (bf16[128,256]{1,0:T(8,128)(2,1)S(1)}, bf16[128,256]{1,0:T(8,128)(2,1)S(1)}, u32[]{:S(2)}, u32[]{:S(2)}) collective-permute-start(bf16[128,256]{1,0:T(8,128)(2,1)S(1)} %shard_map.119.own_ref.right_ref), channel_id=1, source_target_pairs={{0,64},{64,0},{128,192},{192,128},{1,65},{65,1},{129,193},{193,129... | collective-permute-start | bytes 196616 | tf_op jit(solution)/shard_map/ppermute | solution.py:521
  9.3 5.3 %collective-permute-start.2 = (f32[8,128]{1,0:T(8,128)S(1)}, f32[8,128]{1,0:T(8,128)S(1)}, u32[]{:S(2)}, u32[]{:S(2)}) collective-permute-start(f32[8,128]{1,0:T(8,128)S(1)} %get-tuple-element.80), channel_id=1, source_target_pairs={{0,1},{1,0},{2,3},{3,2},{4,5},{5,4},{6,7},{7,6},{8,9},{9,8},{10,11... | collective-permute-start | bytes 12296 | tf_op jit(solution)/shard_map/ppermute | solution.py:537
  14.7 8.4 %collective-permute-start.3 = (bf16[128,256]{1,0:T(8,128)(2,1)S(1)}, bf16[128,256]{1,0:T(8,128)(2,1)S(1)}, u32[]{:S(2)}, u32[]{:S(2)}) collective-permute-start(bf16[128,256]{1,0:T(8,128)(2,1)S(1)} %get-tuple-element.83), channel_id=1, source_target_pairs={{0,136},{8,128},{16,152},{24,144},{32,168},{40,160},{48,184},{56,1... | collective-permute-start | bytes 196616 | tf_op jit(solution)/shard_map/ppermute | solution.py:529
  15.7 7.4 %collective-permute-start.6 = (bf16[128,256]{1,0:T(8,128)(2,1)S(1)}, bf16[128,256]{1,0:T(8,128)(2,1)S(1)}, u32[]{:S(2)}, u32[]{:S(2)}) collective-permute-start(bf16[128,256]{1,0:T(8,128)(2,1)S(1)} %get-tuple-element.90), channel_id=1, source_target_pairs={{0,8},{8,0},{16,24},{24,16},{32,40},{40,32},{48,56},{56,48},{1,9},... | collective-permute-start | bytes 196616 | tf_op jit(solution)/shard_map/ppermute | solution.py:518
  17.9 5.3 %collective-permute-start.7 = (bf16[128,256]{1,0:T(8,128)(2,1)S(1)}, bf16[128,256]{1,0:T(8,128)(2,1)S(1)}, u32[]{:S(2)}, u32[]{:S(2)}) collective-permute-start(bf16[128,256]{1,0:T(8,128)(2,1)S(1)} %get-tuple-element.91), channel_id=1, source_target_pairs={{0,128},{64,192},{128,0},{192,64},{1,129},{65,193},{129,1},{193,65... | collective-permute-start | bytes 196616 | tf_op jit(solution)/shard_map/ppermute | solution.py:521
  18.3 4.8 %collective-permute-start.5 = (f32[8,128]{1,0:T(8,128)S(1)}, f32[8,128]{1,0:T(8,128)S(1)}, u32[]{:S(2)}, u32[]{:S(2)}) collective-permute-start(f32[8,128]{1,0:T(8,128)S(1)} %add.12), channel_id=1, source_target_pairs={{0,6},{1,7},{2,4},{3,5},{4,2},{5,3},{6,0},{7,1},{8,14},{9,15},{10,... | collective-permute-start | bytes 12296 | tf_op jit(solution)/shard_map/ppermute | solution.py:534
  23.2 1.4 %collective-permute-start.8 = (bf16[256,256]{1,0:T(8,128)(2,1)S(1)}, bf16[256,256]{1,0:T(8,128)(2,1)S(1)}, u32[]{:S(2)}, u32[]{:S(2)}) collective-permute-start(bf16[256,256]{1,0:T(8,128)(2,1)S(1)} %shard_map.124.left_ref.right_ref), channel_id=1, source_target_pairs={{0,64},{64,0},{128,192},{192,128},{1,65},{65,1},{129,193},{193,129... | collective-permute-start | bytes 393224 | tf_op jit(solution)/shard_map/ppermute | solution.py:521
  23.9 3.7 %collective-permute-start.10 = (f32[8,128]{1,0:T(8,128)S(1)}, f32[8,128]{1,0:T(8,128)S(1)}, u32[]{:S(2)}, u32[]{:S(2)}) collective-permute-start(f32[8,128]{1,0:T(8,128)S(1)} %add.13), channel_id=1, source_target_pairs={{0,2},{1,3},{2,0},{3,1},{4,6},{5,7},{6,4},{7,5},{8,10},{9,11},{10,... | collective-permute-start | bytes 12296 | tf_op jit(solution)/shard_map/ppermute | solution.py:534
  27.6 1.4 %collective-permute-start.12 = (bf16[256,256]{1,0:T(8,128)(2,1)S(1)}, bf16[256,256]{1,0:T(8,128)(2,1)S(1)}, u32[]{:S(2)}, u32[]{:S(2)}) collective-permute-start(bf16[256,256]{1,0:T(8,128)(2,1)S(1)} %get-tuple-element.119), channel_id=1, source_target_pairs={{0,64},{64,0},{128,192},{192,128},{1,65},{65,1},{129,193},{193,129... | collective-permute-start | bytes 393224 | tf_op jit(solution)/shard_map/ppermute | solution.py:521
  27.6 1.4 %collective-permute-start.11 = (f32[8,128]{1,0:T(8,128)S(1)}, f32[8,128]{1,0:T(8,128)S(1)}, u32[]{:S(2)}, u32[]{:S(2)}) collective-permute-start(f32[8,128]{1,0:T(8,128)S(1)} %add.14), channel_id=1, source_target_pairs={{0,64},{64,0},{128,192},{192,128},{1,65},{65,1},{129,193},{193,129... | collective-permute-start | bytes 12296 | tf_op jit(solution)/shard_map/ppermute | solution.py:521
  29.0 6.1 %collective-permute-start.15 = (bf16[144,256]{1,0:T(8,128)(2,1)S(1)}, bf16[144,256]{1,0:T(8,128)(2,1)S(1)}, u32[]{:S(2)}, u32[]{:S(2)}) collective-permute-start(bf16[144,256]{1,0:T(8,128)(2,1)S(1)} %get-tuple-element.121), channel_id=1, source_target_pairs={{0,136},{8,128},{16,152},{24,144},{32,168},{40,160},{48,184},{56,1... | collective-permute-start | bytes 221192 | tf_op jit(solution)/shard_map/ppermute | solution.py:529
  30.1 6.1 %collective-permute-start.13 = (bf16[144,256]{1,0:T(8,128)(2,1)S(1)}, bf16[144,256]{1,0:T(8,128)(2,1)S(1)}, u32[]{:S(2)}, u32[]{:S(2)}) collective-permute-start(bf16[144,256]{1,0:T(8,128)(2,1)S(1)} %get-tuple-element.120.near_ref), channel_id=1, source_target_pairs={{0,8},{8,0},{16,24},{24,16},{32,40},{40,32},{48,56},{56,48},{1,9},... | collective-permute-start | bytes 221192 | tf_op jit(solution)/shard_map/ppermute | solution.py:518
  32.1 4.4 %collective-permute-start.14 = (bf16[144,256]{1,0:T(8,128)(2,1)S(1)}, bf16[144,256]{1,0:T(8,128)(2,1)S(1)}, u32[]{:S(2)}, u32[]{:S(2)}) collective-permute-start(bf16[144,256]{1,0:T(8,128)(2,1)S(1)} %get-tuple-element.121), channel_id=1, source_target_pairs={{0,128},{64,192},{128,0},{192,64},{1,129},{65,193},{129,1},{193,65... | collective-permute-start | bytes 221192 | tf_op jit(solution)/shard_map/ppermute | solution.py:521
  36.6 8.5 %collective-permute-start.16 = (bf16[144,256]{1,0:T(8,128)(2,1)S(1)}, bf16[144,256]{1,0:T(8,128)(2,1)S(1)}, u32[]{:S(2)}, u32[]{:S(2)}) collective-permute-start(bf16[144,256]{1,0:T(8,128)(2,1)S(1)} %get-tuple-element.125), channel_id=1, source_target_pairs={{0,56},{8,48},{16,40},{24,32},{32,24},{40,16},{48,8},{56,0},{1,57}... | collective-permute-start | bytes 221192 | tf_op jit(solution)/shard_map/ppermute | solution.py:518
  40.6 7.4 %collective-permute-start.17 = (bf16[144,256]{1,0:T(8,128)(2,1)S(1)}, bf16[144,256]{1,0:T(8,128)(2,1)S(1)}, u32[]{:S(2)}, u32[]{:S(2)}) collective-permute-start(bf16[144,256]{1,0:T(8,128)(2,1)S(1)} %get-tuple-element.126), channel_id=1, source_target_pairs={{0,40},{8,32},{16,56},{24,48},{32,8},{40,0},{48,24},{56,16},{1,41}... | collective-permute-start | bytes 221192 | tf_op jit(solution)/shard_map/ppermute | solution.py:518
  40.6 2.6 %collective-permute-start.9 = (bf16[128,256]{1,0:T(8,128)(2,1)S(1)}, bf16[128,256]{1,0:T(8,128)(2,1)S(1)}, u32[]{:S(2)}, u32[]{:S(2)}) collective-permute-start(bf16[128,256]{1,0:T(8,128)(2,1)S(1)} %get-tuple-element.111), channel_id=1, source_target_pairs={{0,64},{64,0},{128,192},{192,128},{1,65},{65,1},{129,193},{193,129... | collective-permute-start | bytes 196616 | tf_op jit(solution)/shard_map/ppermute | solution.py:521
  40.6 4.5 %collective-permute-start.18 = (f32[8,128]{1,0:T(8,128)S(1)}, f32[8,128]{1,0:T(8,128)S(1)}, u32[]{:S(2)}, u32[]{:S(2)}) collective-permute-start(f32[8,128]{1,0:T(8,128)S(1)} %get-tuple-element.127.totals_ref), channel_id=1, source_target_pairs={{0,16},{8,24},{16,0},{24,8},{32,48},{40,56},{48,32},{56,40},{1,17}... | collective-permute-start | bytes 12296 | tf_op jit(solution)/shard_map/ppermute | solution.py:518

commit v4 on v3

--- a/solution.py
+++ b/solution.py
@@ -20,7 +20,7 @@
 VMEM_SPEC = pl.BlockSpec(memory_space=pltpu.VMEM)
 HBM_SPEC = pl.BlockSpec(memory_space=pltpu.HBM)
 
-FROM7, FROM5, IS_PROMPT, VALID, PAIR_ROW = 0, 4, 8, 9, 10
+FROM6, FROM5, IS_PROMPT, VALID, PAIR_ROW = 0, 4, 8, 9, 10
 BIAS_FIRST, BIAS_MATE, BIAS_OVER, BIAS_CROSS, BIAS_OWN = 11, 12, 13, 14, 15
 FACTS = 16
 
@@ -110,7 +110,7 @@
     half = seq // 2
     slots = [pair_of(group, side) for side in (half, 1 - half) for group in (grp, grp ^ 1)]
     for number, pair in enumerate(slots):
-        flag(FROM7 + number, jnp.logical_and(is_response, pair == (grp ^ 7)))
+        flag(FROM6 + number, jnp.logical_and(is_response, pair == (grp ^ 6)))
         flag(FROM5 + number, jnp.logical_and(is_response, pair == (grp ^ 5)))
     slot = jnp.where(is_response, 2 * (grp - pairs), 0) + half
     filled = seq % 2 < counts_ref[slot]
@@ -146,7 +146,9 @@
     kept_ref[...] = jnp.where(kept, sign, 0.0)
 
 
-def prepare_kernel(kept_ref, query_hbm, cot_hbm, query_ref, grad_ref, grad_t_ref, cots, sems):
+def prepare_kernel(
+    kept_ref, query_hbm, cot_hbm, query_ref, query_t_ref, grad_ref, grad_t_ref, cots, sems
+):
     rows = kept_ref.shape[1]
     dim = query_ref.shape[1]
     heads = query_ref.shape[0] // rows
@@ -170,24 +172,33 @@
         grad = (cots[part].astype(F32) * kept_rows).astype(BF16)
         grad_ref[part] = grad
         grad_t_ref[:, part] = grad.T
-
-
-def route_kernel(facts_ref, own_ref, far7, far5, group_ref, seq_ref, cross_ref):
+        query_t_ref[:, part] = query_ref[part].T
+
+
+def route_kernel(facts_ref, totals_ref, own_ref, far6, far5, group_ref, seq_ref, cross_ref):
+    rows = own_ref.shape[0]
     for number, ref in ((1, group_ref), (2, seq_ref), (3, cross_ref)):
-        picked = far7[...].astype(F32) * fact(facts_ref, FROM7 + number)
+        picked = far6[...].astype(F32) * fact(facts_ref, FROM6 + number)
         picked = picked + far5[...].astype(F32) * fact(facts_ref, FROM5 + number)
         if number == 2:
             picked = picked + own_ref[...].astype(F32) * fact(facts_ref, IS_PROMPT)
-        ref[...] = picked.astype(BF16)
-
-
-def select_kernel(facts_ref, own_ref, far7, far5, group_ref, seq_ref, cross_ref, near_ref):
+        ref[:rows] = picked.astype(BF16)
+        store_tail(ref, rows, totals_ref[...])
+
+
+def select_kernel(
+    facts_ref, totals_ref, own_ref, far6, far5, group_ref, seq_ref, cross_ref, near_ref, sum_ref
+):
     rows = own_ref.shape[0]
-    first = far7[...].astype(F32) * fact(facts_ref, FROM7)
+    first = far6[...].astype(F32) * fact(facts_ref, FROM6)
     first = first + far5[...].astype(F32) * fact(facts_ref, FROM5)
     first = first + own_ref[...].astype(F32) * fact(facts_ref, IS_PROMPT)
-    near_ref[:rows] = (first + group_ref[...].astype(F32)).astype(BF16)
-    near_ref[rows:] = (seq_ref[...].astype(F32) + cross_ref[...].astype(F32)).astype(BF16)
+    near_ref[:rows] = (first + group_ref[:rows].astype(F32)).astype(BF16)
+    near_ref[rows:] = (seq_ref[:rows].astype(F32) + cross_ref[:rows].astype(F32)).astype(BF16)
+    totals = (totals_ref[...] + decode(group_ref, rows)) + (
+        decode(seq_ref, rows) + decode(cross_ref, rows)
+    )
+    sum_ref[...] = jnp.concatenate([totals] * (sum_ref.shape[0] // 8), axis=0)
 
 
 def load_blocks(blocks, keys, values, keys_t, values_t):
@@ -242,43 +253,45 @@
         for i, piece in enumerate(pieces):
             power = jnp.exp2(piece * shade + (bias[i] - shade * top))
             total = total + jnp.sum(power, axis=0, keepdims=True)
-            powers_ref[i * rows : (i + 1) * rows, both] = power
+            powers_ref[i * rows : (i + 1) * rows, both] = power.astype(BF16)
         stats_ref[0:1, both] = top
         stats_ref[1:2, both] = total
+
+
+def scaled(ref, scales_ref, row):
+    return (ref[...].astype(F32) * scales_ref[row : row + 1, :]).astype(BF16)
+
+
+def store_grads(ref, score_grad, powers, query_t, grad_t, scaling):
+    dim = query_t.shape[0]
+    ref[:, :dim] = (dot(score_grad, query_t, 1, 1) * scaling).astype(ref.dtype)
+    ref[:, dim:] = dot(powers, grad_t, 1, 1).astype(ref.dtype)
 
 
 def late_kernel(
     facts_ref,
     query_ref,
+    query_t_ref,
     grad_ref,
     grad_t_ref,
     own_powers,
-    own_prob_grad,
     own_stats,
     own_values_t,
     near_powers,
-    near_prob_grad,
     near_stats,
     near_values_t,
     mate_ref,
     back_ref,
-    first_ref,
-    over_ref,
     output_t_ref,
-    own_rounded,
-    own_score_grad,
-    near_score_grad,
-    mate_score_grad,
+    score_grad,
     keys_t,
+    scales_ref,
     keys,
     values,
     values_t,
     powers,
     prob_grad,
     stats,
-    factors,
-    near_rounded,
-    mate_rounded,
 ):
     rows, dim = keys.shape[0] // 2, keys.shape[1]
     heads = query_ref.shape[0] // rows
@@ -298,70 +311,78 @@
         for i, piece in enumerate(pieces):
             power = jnp.exp2(piece * shade + (bias[i] - shade * top))
             total = total + jnp.sum(power, axis=0, keepdims=True)
-            powers[i * rows : (i + 1) * rows, both] = power
+            powers[i * rows : (i + 1) * rows, both] = power.astype(BF16)
         stats[0:1, both] = top
         stats[1:2, both] = total
 
     sets = (
-        (own_powers, own_prob_grad, own_stats, own_values_t, own_rounded, own_score_grad),
-        (near_powers, near_prob_grad, near_stats, near_values_t, near_rounded, near_score_grad),
-        (powers, prob_grad, stats, values_t, mate_rounded, mate_score_grad),
-    )
+        (own_powers, own_stats, own_values_t),
+        (near_powers, near_stats, near_values_t),
+        (powers, stats, values_t),
+    )
+    tops = [item[1][0:1, :] for item in sets]
+    top = jnp.maximum(jnp.maximum(tops[0], tops[1]), tops[2])
+    fades = [jnp.exp2((part - top) * shade) for part in tops]
+    total = sum(item[1][1:2, :] * fade for item, fade in zip(sets, fades))
+    inverse = 1.0 / total
+    for i, fade in enumerate(fades):
+        scales_ref[i : i + 1, :] = fade * inverse
     for both in spans:
-        tops = [item[2][0:1, both] for item in sets]
-        top = jnp.maximum(jnp.maximum(tops[0], tops[1]), tops[2])
-        fades = [jnp.exp2((part - top) * shade) for part in tops]
-        total = sum(item[2][1:2, both] * fade for item, fade in zip(sets, fades))
-        inverse = 1.0 / total
-        output_t = None
-        for i, item in enumerate(sets):
-            factor = fades[i] * inverse
-            factors[i : i + 1, both] = factor
-            rounded = (item[0][:, both] * factor).astype(BF16)
-            item[4][:, both] = rounded
-            part = dot(item[3][...], rounded, 1, 0)
-            output_t = part if output_t is None else output_t + part
+        output_t = sum(
+            dot(item[2][...], item[0][:, both], 1, 0) * scales_ref[i : i + 1, both]
+            for i, item in enumerate(sets)
+        )
         output_t_ref[:, both] = output_t
-        factors[3:4, both] = jnp.sum(
-            grad_t_ref[:, both].astype(F32) * output_t, axis=0, keepdims=True
-        )
-
-    for both in spans:
-        delta = factors[3:4, both]
-        for i, item in enumerate(sets):
-            probs = item[0][:, both] * factors[i : i + 1, both]
-            item[5][:, both] = (probs * (item[1][:, both] - delta)).astype(BF16)
-
-    for item, near_out, over_out in (
-        (sets[2], (back_ref, 0), (back_ref, rows)),
-        (sets[1], (first_ref, 0), (over_ref, 0)),
-    ):
-        key_part = dot(item[5][...], query_ref[...], 1, 0) * scaling
-        value_part = dot(item[4][...], grad_ref[...], 1, 0)
-        for number, (ref, start) in enumerate((near_out, over_out)):
-            part = slice(number * rows, (number + 1) * rows)
-            ref[start : start + rows, :dim] = key_part[part].astype(ref.dtype)
-            ref[start : start + rows, dim:] = value_part[part].astype(ref.dtype)
+        delta = jnp.sum(grad_t_ref[:, both].astype(F32) * output_t, axis=0, keepdims=True)
+        scales_ref[3:4, both] = delta
+        score_grad[:, both] = (
+            powers[:, both].astype(F32) * (prob_grad[:, both] - delta)
+        ).astype(BF16)
+    store_grads(
+        back_ref,
+        score_grad[...],
+        powers[...],
+        scaled(query_t_ref, scales_ref, 2),
+        scaled(grad_t_ref, scales_ref, 2),
+        scaling,
+    )
+
+
+def near_kernel(
+    query_t_ref, grad_t_ref, powers, prob_grad, scales_ref, near_ref, score_grad
+):
+    scaling = 1.0 / math.sqrt(query_t_ref.shape[0])
+    delta = scales_ref[3:4, :]
+    score_grad[...] = (powers[...].astype(F32) * (prob_grad[...] - delta)).astype(BF16)
+    store_grads(
+        near_ref,
+        score_grad[...],
+        powers[...],
+        scaled(query_t_ref, scales_ref, 1),
+        scaled(grad_t_ref, scales_ref, 1),
+        scaling,
+    )
 
 
 def query_kernel(
     facts_ref,
+    query_t_ref,
+    grad_t_ref,
     output_t_ref,
-    own_score_grad,
+    scales_ref,
+    own_powers,
+    own_prob_grad,
     near_score_grad,
     mate_score_grad,
     own_keys_t,
     near_keys_t,
     mate_keys_t,
-    own_rounded,
-    query_ref,
-    grad_ref,
     attended_ref,
     query_grad_ref,
     back_ref,
     local_ref,
-    key_acc,
-    value_acc,
+    own_score_grad,
+    grads_ref,
 ):
     rows = attended_ref.shape[0]
     dim = output_t_ref.shape[0]
@@ -370,19 +391,19 @@
     valid = fact(facts_ref, VALID, wide)
     for pair in range(output_t_ref.shape[1] // wide):
         both = slice(pair * wide, (pair + 1) * wide)
-        grad_t = (
-            dot(own_keys_t[...], own_score_grad[:, both], 1, 0)
-            + dot(near_keys_t[...], near_score_grad[:, both], 1, 0)
-            + dot(mate_keys_t[...], mate_score_grad[:, both], 1, 0)
+        delta = scales_ref[3:4, both]
+        own_score_grad[:, both] = (
+            own_powers[:, both].astype(F32) * (own_prob_grad[:, both] - delta)
+        ).astype(BF16)
+        sets = (
+            (own_keys_t, own_score_grad),
+            (near_keys_t, near_score_grad),
+            (mate_keys_t, mate_score_grad),
         )
-        key_part = dot(own_score_grad[:, both], query_ref[both], 1, 0)
-        value_part = dot(own_rounded[:, both], grad_ref[both], 1, 0)
-        if pair == 0:
-            key_acc[...] = key_part
-            value_acc[...] = value_part
-        else:
-            key_acc[...] += key_part
-            value_acc[...] += value_part
+        grad_t = sum(
+            dot(part_t[...], part[:, both], 1, 0) * scales_ref[i : i + 1, both]
+            for i, (part_t, part) in enumerate(sets)
+        )
         query_grad = (grad_t * scaling).T
         output = (output_t_ref[:, both] * valid).T
         for i in (0, 1):
@@ -390,44 +411,34 @@
             part = slice(i * rows, (i + 1) * rows)
             attended_ref[:, span] = output[part].astype(BF16)
             query_grad_ref[:, span] = query_grad[part]
-    for number, ref in ((0, back_ref), (1, local_ref)):
-        part = slice(number * rows, (number + 1) * rows)
-        ref[:, :dim] = (key_acc[part] * scaling).astype(ref.dtype)
-        ref[:, dim:] = value_acc[part].astype(ref.dtype)
-
-
-def merge_kernel(totals_ref, first_ref, over_ref, back_ref, near_out, over_out):
-    rows = first_ref.shape[0]
-    near_out[:rows] = (first_ref[...] + back_ref[:rows].astype(F32)).astype(BF16)
-    over_out[:rows] = (over_ref[...] + back_ref[rows:].astype(F32)).astype(BF16)
-    store_tail(near_out, rows, totals_ref[...])
-    store_tail(over_out, rows, totals_ref[...])
+    store_grads(
+        grads_ref,
+        own_score_grad[...],
+        own_powers[...],
+        scaled(query_t_ref, scales_ref, 0),
+        scaled(grad_t_ref, scales_ref, 0),
+        scaling,
+    )
+    back_ref[...] = grads_ref[:rows].astype(BF16)
+    local_ref[...] = grads_ref[rows:]
+
+
+def merge_kernel(first_ref, back_ref, near_out, over_out):
+    rows = first_ref.shape[0] // 2
+    near_out[...] = (first_ref[:rows] + back_ref[:rows].astype(F32)).astype(BF16)
+    over_out[...] = (first_ref[rows:] + back_ref[rows:].astype(F32)).astype(BF16)
 
 
 def return_kernel(
-    facts_ref,
-    totals_ref,
-    near_ref,
-    group_ref,
-    seq_ref,
-    cross_ref,
-    prompt_ref,
-    pay7,
-    pay5,
-    sum_ref,
+    facts_ref, totals_ref, near_ref, group_ref, seq_ref, cross_ref, prompt_ref, pay6, pay5
 ):
     rows = prompt_ref.shape[0]
-    refs = (near_ref, group_ref, seq_ref, cross_ref)
-    sums = [ref[:rows].astype(F32) for ref in refs]
+    sums = [ref[...].astype(F32) for ref in (near_ref, group_ref, seq_ref, cross_ref)]
     prompt_ref[...] = (sums[0] + sums[2]) * fact(facts_ref, IS_PROMPT)
-    totals = (totals_ref[...] + decode(group_ref, rows)) + (
-        decode(seq_ref, rows) + decode(cross_ref, rows)
-    )
-    sum_ref[...] = totals
-    for ref, base in ((pay7, FROM7), (pay5, FROM5)):
+    for ref, base in ((pay6, FROM6), (pay5, FROM5)):
         total = sum(part * fact(facts_ref, base + i) for i, part in enumerate(sums))
         ref[:rows] = total.astype(BF16)
-        store_tail(ref, rows, totals)
+        store_tail(ref, rows, totals_ref[...])
 
 
 def finish_kernel(
@@ -435,8 +446,8 @@
     local_ref,
     mate_ref,
     prompt_ref,
-    far7,
     far5,
+    far6,
     totals_ref,
     rest_ref,
     query_part_ref,
@@ -446,7 +457,7 @@
     loss_ref,
 ):
     rows, dim = key_grad_ref.shape
-    totals = (totals_ref[...] + rest_ref[...]) + (decode(far7, rows) + decode(far5, rows))
+    totals = (totals_ref[...] + rest_ref[...]) + (decode(far6, rows) + decode(far5, rows))
     margin = totals - jnp.concatenate([totals[1:], totals[:1]], axis=0)
     slope = -BETA * margin
     small = jnp.exp(-jnp.abs(slope))
@@ -463,7 +474,7 @@
     loss_ref[...] = in_lanes[:, : loss_ref.shape[1]]
     mine = row.astype(F32) == fact(facts_ref, PAIR_ROW, 128)
     scale = jnp.sum(jnp.where(mine, weight, 0.0), axis=0, keepdims=True)
-    far_sum = far7[:rows].astype(F32) + far5[:rows].astype(F32)
+    far_sum = far6[:rows].astype(F32) + far5[:rows].astype(F32)
     total = local_ref[...] + mate_ref[...].astype(F32) + prompt_ref[...]
     total = total + far_sum * fact(facts_ref, IS_PROMPT)
     key_grad_ref[...] = (total[:, :dim] * scale).astype(BF16)
@@ -539,7 +550,7 @@
     own = call(
         pack_kernel, grads, (key_heads[0], value_heads[0]), scratch=[dma((2,))], in_hbm=2
     )
-    far7 = along_grp(own, 7)
+    far6 = along_grp(own, 6)
     far5 = along_grp(own, 5)
     own, response_order = tie((own, response_order))
     facts, totals, kept = call(
@@ -557,18 +568,20 @@
     )
     mate_own = along_seq(own, 1)
     stacked = shape((every, dim), BF16)
-    query_rows, grad_rows, grad_cols = call(
+    query_rows, query_cols, grad_rows, grad_cols = call(
         prepare_kernel,
-        [stacked, stacked, shape((dim, every), BF16)],
+        [stacked, shape((dim, every), BF16), stacked, shape((dim, every), BF16)],
         (kept, queries[0], cotangent[0]),
         scratch=[pltpu.VMEM((every, dim), BF16), dma((2, heads))],
         in_hbm=2,
     )
     part = along_y(totals)
-    far7, far5, totals, query_rows = tie((far7, far5, totals, query_rows))
+    far6, far5, totals, query_rows = tie((far6, far5, totals, query_rows))
     totals = totals + part
-    far7, far5, totals = tie((far7, far5, totals))
-    to_group, to_seq, to_cross = call(route_kernel, [grads] * 3, (facts, own, far7, far5))
+    far6, far5, totals = tie((far6, far5, totals))
+    to_group, to_seq, to_cross = call(
+        route_kernel, [packed] * 3, (facts, totals, own, far6, far5)
+    )
     from_seq = along_seq(to_seq, 2)
     from_group = along_grp(to_group, 1)
     from_cross = across(to_cross)
@@ -577,7 +590,7 @@
         return call(
             functools.partial(early_kernel, biases, is_own),
             [
-                shape((2 * rows, every), F32),
+                shape((2 * rows, every), BF16),
                 shape((2 * rows, every), F32),
                 shape((8, every), F32),
                 shape((dim, 2 * rows), BF16),
@@ -589,42 +602,35 @@
         )
 
     own_set = early((BIAS_OWN, None), True, mate_own, own)
-    totals = totals + along_x(totals, 1)
-    from_cross, own_powers, totals = tie((from_cross, own_set[0], totals))
-    near = call(
+    from_cross, own_powers = tie((from_cross, own_set[0]))
+    near, totals = call(
         select_kernel,
-        shape((2 * rows, both), BF16),
-        (facts, own, far7, far5, from_group, from_seq, from_cross),
+        [shape((2 * rows, both), BF16), shape((rows, 128), F32)],
+        (facts, totals, own, far6, far5, from_group, from_seq, from_cross),
     )
     mate = along_seq(near, 1)
     near_set = early((BIAS_FIRST, BIAS_OVER), False, near, near)
-    near_powers, totals = tie((near_set[0], totals))
-    part = along_x(totals, 0)
-    mate, near_powers = tie((mate, near_powers))
-    back, first, over, output_t, own_rounded, own_sg, near_sg, mate_sg, mate_keys_t = call(
+    part = along_seq(totals, 1)
+    mate, near_powers = tie((mate, near_set[0]))
+    back, output_t, mate_sg, mate_keys_t, scales = call(
         late_kernel,
         [
             shape((2 * rows, both), BF16),
-            grads_wide,
-            grads_wide,
             shape((dim, every), F32),
             shape((2 * rows, every), BF16),
-            shape((2 * rows, every), BF16),
-            shape((2 * rows, every), BF16),
-            shape((2 * rows, every), BF16),
             shape((dim, 2 * rows), BF16),
+            shape((8, every), F32),
         ],
         (
             facts,
             query_rows,
+            query_cols,
             grad_rows,
             grad_cols,
             own_powers,
-            own_set[1],
             own_set[2],
             own_set[4],
             near_powers,
-            near_set[1],
             near_set[2],
             near_set[4],
             mate,
@@ -633,47 +639,59 @@
             pltpu.VMEM((2 * rows, dim), BF16),
             pltpu.VMEM((2 * rows, dim), BF16),
             pltpu.VMEM((dim, 2 * rows), BF16),
-        ]
-        + [pltpu.VMEM((2 * rows, every), F32)] * 2
-        + [pltpu.VMEM((8, every), F32)] * 2
-        + [pltpu.VMEM((2 * rows, every), BF16)] * 2,
-        flops=40 * rows * every * dim,
+            pltpu.VMEM((2 * rows, every), BF16),
+            pltpu.VMEM((2 * rows, every), F32),
+            pltpu.VMEM((8, every), F32),
+        ],
+        flops=24 * rows * every * dim,
     )
     back, totals = tie((back, totals))
     back, totals = tie((back, totals + part))
     back = along_seq(back, 1)
-    totals = totals + along_seq(totals, 1)
-    near_sum, over_sum = call(merge_kernel, [packed, packed], (totals, first, over, back))
+    part = along_x(totals, 0)
+    first, near_sg = call(
+        near_kernel,
+        [shape((2 * rows, both), F32), shape((2 * rows, every), BF16)],
+        (query_cols, grad_cols, near_powers, near_set[1], scales),
+        flops=8 * rows * every * dim,
+    )
+    near_sum, over_sum = call(merge_kernel, [grads, grads], (first, back))
     from_seq = along_seq(over_sum, 2)
     from_group = along_grp(near_sum, 1)
     from_cross = across(over_sum)
+    totals = (totals + part)[:8]
+    totals = totals + along_x(totals, 1)
     attended, query_part, own_back, local = call(
         query_kernel,
         [shape((rows, width), BF16), shape((rows, width), F32), grads, grads_wide],
         (
             facts,
+            query_cols,
+            grad_cols,
             output_t,
-            own_sg,
+            scales,
+            own_powers,
+            own_set[1],
             near_sg,
             mate_sg,
             own_set[3],
             near_set[3],
             mate_keys_t,
-            own_rounded,
-            query_rows,
-            grad_rows,
         ),
-        scratch=[pltpu.VMEM((2 * rows, dim), F32)] * 2,
+        scratch=[
+            pltpu.VMEM((2 * rows, every), BF16),
+            pltpu.VMEM((2 * rows, both), F32),
+        ],
         flops=20 * rows * every * dim,
     )
     from_cross, query_part = tie((from_cross, query_part))
-    from_prompt, pay7, pay5, totals = call(
+    from_prompt, pay6, pay5 = call(
         return_kernel,
-        [grads_wide, packed, packed, total_tile],
+        [grads_wide, packed, packed],
         (facts, totals, near_sum, from_group, from_seq, from_cross),
     )
-    far7 = along_grp(pay7, 7)
     far5 = along_grp(pay5, 5)
+    far6 = along_grp(pay6, 6)
     own_back = along_seq(own_back, 1)
     rest = along_grp(totals, 2)
     query_grad, key_grad, value_grad, loss = call(
@@ -684,7 +702,7 @@
             shape((rows, dim), BF16),
             shape((1, group_count // 2), F32),
         ],
-        (facts, local, own_back, from_prompt, far7, far5, totals, rest, query_part),
+        (facts, local, own_back, from_prompt, far5, far6, totals, rest, query_part),
     )
     return attended[None], query_grad[None], key_grad[None], value_grad[None], loss[0]
 

time: 49 us -> 47.7 us (0.973)
  starting transfers between devices: 27.9 us -> 26.8 us
    ppermute x7, starting transfers between devices: 17.7 us -> 14.4 us  [along_grp(): return lax.ppermute(value, 'grp', swap(group_count, turn))]
    ppermute x7, starting transfers between devices: 1.51 us -> 2.85 us  [along_seq(): return lax.ppermute(value, 'seq', swap(seq_count, turn))]
    ppermute x2, waiting for transfers between devices: 2.32 us -> 1.35 us  [along_x(): return lax.ppermute(value, 'head', round_way if step else near)]
    ppermute x2, starting transfers between devices: 2.07 us -> 2.73 us  [across(): return lax.ppermute(value, ('seq', 'grp'), turns)]
    ppermute x7, waiting for transfers between devices: 6.61 us -> 7.15 us  [along_grp(): return lax.ppermute(value, 'grp', swap(group_count, turn))]
    pallas_call x12 -> x13, Pallas kernels: 8.7 us -> 8.43 us  [call(): pl.pallas_call(kernel, out_shape=out_shapes, in_specs=[VMEM_SPEC] * plain...]
  transfers between devices with their start and end apart: 19 -> 19, of which waited for: 10 -> 9; matrix products, arithmetic and copies ran while one was open for 0% -> 0% of each run, Pallas kernels for 14% -> 14%
where the time goes in v4:
time: 47.7 us; the launch traced here: 47.5 us
  starting transfers between devices  26.8 us (56%)
  waiting for transfers between devices  11.4 us (24%)
  Pallas kernels  8.43 us (18%)
  between operations  0.76 us (2%)
    ppermute x7, starting transfers between devices, along_grp(): return lax.ppermute(value, 'grp', swap(group_count, turn))  14.4 us
    pallas_call x13, Pallas kernels, call(): pl.pallas_call(kernel, out_shape=out_shapes, in_specs=[VMEM_SPEC] * plain...  8.43 us
    ppermute x7, waiting for transfers between devices, along_grp(): return lax.ppermute(value, 'grp', swap(group_count, turn))  7.15 us
    ppermute x2, starting transfers between devices, along_x(): return lax.ppermute(value, 'head', round_way if step else near)  3.6 us
    ppermute x1, starting transfers between devices, along_y(): return lax.ppermute(value, 'head', swap(head_count, 1))  3.28 us
    ppermute x7, starting transfers between devices, along_seq(): return lax.ppermute(value, 'seq', swap(seq_count, turn))  2.85 us
    ppermute x2, starting transfers between devices, across(): return lax.ppermute(value, ('seq', 'grp'), turns)  2.73 us
    ppermute x7, waiting for transfers between devices, along_seq(): return lax.ppermute(value, 'seq', swap(seq_count, turn))  1.48 us
  transfers between devices with their start and end apart: 19, of which 9 were waited for; matrix products, arithmetic and copies ran while one was open for 0% of the time, Pallas kernels for 14%

profile of v4, /device:TPU:32, one launch (start us, length us, event | category | flops | bytes accessed | tf_op | source)
XLA Modules:
  0.0 47.5 jit_solution(10733371233089417782)
XLA Ops:
  0.6 0.8 %shard_map.119.own_ref.right_ref = bf16[128,256]{1,0:T(8,128)(2,1)S(1)} custom-call(bf16[128,128]{1,0:T(8,128)(2,1)} %bitcast.11, bf16[128,128]{1,0:T(8,128)(2,1)} %bitcast.12), custom_call_target="tpu_custom_call" | custom-call | tf_op jit(solution)/shard_map/pallas_call | solution.py:493
  1.4 5.5 %collective-permute-start = (bf16[128,256]{1,0:T(8,128)(2,1)S(1)}, bf16[128,256]{1,0:T(8,128)(2,1)S(1)}, u32[]{:S(2)}, u32[]{:S(2)}) collective-permute-start(bf16[128,256]{1,0:T(8,128)(2,1)S(1)} %shard_map.119.own_ref.right_ref), channel_id=1, source_target_pairs={{0,48},{8,56},{16,32},{24,40},{32,16},{40,24},{48,0},{56,8},{1,49}... | collective-permute-start | bytes 196616 | tf_op jit(solution)/shard_map/ppermute | solution.py:529
  7.5 0.9 %shard_map.120 = (f32[16,256]{1,0:T(8,128)S(1)}, f32[8,128]{1,0:T(8,128)S(1)}, f32[1,128]{1,0:T(1,128)S(1)}) custom-call(s32[8]{0:T(128)} %order_hbm, s32[8]{0:T(128)} %counts_hbm.1, s32[1,128]{1,0:T(1,128)} %mask_hbm.1, f32[1,16]{1,0:T(1,128)} %ratio_hbm.1), custom_call_target="tpu_custom_call" | custom-call | tf_op jit(solution)/shard_map/pallas_call | solution.py:493
  8.4 3.3 %collective-permute-start.2 = (f32[8,128]{1,0:T(8,128)S(1)}, f32[8,128]{1,0:T(8,128)S(1)}, u32[]{:S(2)}, u32[]{:S(2)}) collective-permute-start(f32[8,128]{1,0:T(8,128)S(1)} %get-tuple-element.77), channel_id=1, source_target_pairs={{0,1},{1,0},{2,3},{3,2},{4,5},{5,4},{6,7},{7,6},{8,9},{9,8},{10,11... | collective-permute-start | bytes 12296 | tf_op jit(solution)/shard_map/ppermute | solution.py:548
  11.7 1.4 %shard_map.121 = (bf16[1024,128]{1,0:T(8,128)(2,1)S(1)}, bf16[128,1024]{1,0:T(8,128)(2,1)S(1)}, bf16[1024,128]{1,0:T(8,128)(2,1)S(1)}, bf16[128,1024]{1,0:T(8,128)(2,1)S(1)}) custom-call(f32[1,128]{1,0:T(1,128)S(1)} %get-tuple-element.68.kept_ref, bf16[128,1024]{1,0:T(8,128)(2,1)} %bitcast.9, bf16[128,1024]{1,0:T(8,128)(2,1)} %bitcast.10), custom_call_target="tpu_custom_call" | custom-call | tf_op jit(solution)/shard_map/pallas_call | solution.py:493
  13.0 1.3 %collective-permute-done.1.far5 = bf16[128,256]{1,0:T(8,128)(2,1)S(1)} collective-permute-done((bf16[128,256]{1,0:T(8,128)(2,1)S(1)}, bf16[128,256]{1,0:T(8,128)(2,1)S(1)}, u32[]{:S(2)}, u32[]{:S(2)}) %collective-permute-start.1) | collective-permute-done | bytes 65568 | tf_op jit(solution)/shard_map/ppermute | solution.py:529
  14.5 1.9 %collective-permute-start.3 = (bf16[144,256]{1,0:T(8,128)(2,1)S(1)}, bf16[144,256]{1,0:T(8,128)(2,1)S(1)}, u32[]{:S(2)}, u32[]{:S(2)}) collective-permute-start(bf16[144,256]{1,0:T(8,128)(2,1)S(1)} %get-tuple-element.82), channel_id=1, source_target_pairs={{0,136},{8,128},{16,152},{24,144},{32,168},{40,160},{48,184},{56,1... | collective-permute-start | bytes 221192 | tf_op jit(solution)/shard_map/ppermute | solution.py:540
  16.4 1.2 %collective-permute-start.5 = (bf16[144,256]{1,0:T(8,128)(2,1)S(1)}, bf16[144,256]{1,0:T(8,128)(2,1)S(1)}, u32[]{:S(2)}, u32[]{:S(2)}) collective-permute-start(bf16[144,256]{1,0:T(8,128)(2,1)S(1)} %get-tuple-element.87), channel_id=1, source_target_pairs={{0,8},{8,0},{16,24},{24,16},{32,40},{40,32},{48,56},{56,48},{1,9},... | collective-permute-start | bytes 221192 | tf_op jit(solution)/shard_map/ppermute | solution.py:529
  18.6 1.4 %collective-permute-done.3.cross_ref = bf16[144,256]{1,0:T(8,128)(2,1)S(1)} collective-permute-done((bf16[144,256]{1,0:T(8,128)(2,1)S(1)}, bf16[144,256]{1,0:T(8,128)(2,1)S(1)}, u32[]{:S(2)}, u32[]{:S(2)}) %collective-permute-start.3) | collective-permute-done | bytes 73760 | tf_op jit(solution)/shard_map/ppermute | solution.py:540
  20.8 1.2 %collective-permute-done.6.seq_ref = bf16[144,256]{1,0:T(8,128)(2,1)S(1)} collective-permute-done((bf16[144,256]{1,0:T(8,128)(2,1)S(1)}, bf16[144,256]{1,0:T(8,128)(2,1)S(1)}, u32[]{:S(2)}, u32[]{:S(2)}) %collective-permute-start.6) | collective-permute-done | bytes 73760 | tf_op jit(solution)/shard_map/ppermute | solution.py:532
  23.5 1.3 %shard_map.126 = (bf16[256,256]{1,0:T(8,128)(2,1)S(1)}, f32[128,1024]{1,0:T(8,128)S(1)}, bf16[256,1024]{1,0:T(8,128)(2,1)S(1)}, bf16[128,256]{1,0:T(8,128)(2,1)S(1)}, f32[8,1024]{1,0:T(8,128)S(1)}) custom-call(f32[16,256]{1,0:T(8,128)S(1)} %get-tuple-element.67.facts_ref, bf16[1024,128]{1,0:T(8,128)(2,1)S(1)} %get-tuple-element.73.query_ref, ...), custom_call_target="tpu_custom_call" | custom-call | flops 402653184 | tf_op jit(solution)/shard_map/pallas_call | solution.py:493
  25.0 1.5 %collective-permute-start.10 = (f32[128,128]{1,0:T(8,128)S(1)}, f32[128,128]{1,0:T(8,128)S(1)}, u32[]{:S(2)}, u32[]{:S(2)}) collective-permute-start(f32[128,128]{1,0:T(8,128)S(1)} %add.13), channel_id=1, source_target_pairs={{0,2},{1,3},{2,0},{3,1},{4,6},{5,7},{6,4},{7,5},{8,10},{9,11},{10,... | collective-permute-start | bytes 196616 | tf_op jit(solution)/shard_map/ppermute | solution.py:545
  27.0 0.8 %collective-permute-start.15 = (bf16[128,256]{1,0:T(8,128)(2,1)S(1)}, bf16[128,256]{1,0:T(8,128)(2,1)S(1)}, u32[]{:S(2)}, u32[]{:S(2)}) collective-permute-start(bf16[128,256]{1,0:T(8,128)(2,1)S(1)} %get-tuple-element.116), channel_id=1, source_target_pairs={{0,136},{8,128},{16,152},{24,144},{32,168},{40,160},{48,184},{56,1... | collective-permute-start | bytes 196616 | tf_op jit(solution)/shard_map/ppermute | solution.py:540
  27.8 1.6 %collective-permute-start.14 = (bf16[128,256]{1,0:T(8,128)(2,1)S(1)}, bf16[128,256]{1,0:T(8,128)(2,1)S(1)}, u32[]{:S(2)}, u32[]{:S(2)}) collective-permute-start(bf16[128,256]{1,0:T(8,128)(2,1)S(1)} %get-tuple-element.116), channel_id=1, source_target_pairs={{0,128},{64,192},{128,0},{192,64},{1,129},{65,193},{129,1},{193,65... | collective-permute-start | bytes 196616 | tf_op jit(solution)/shard_map/ppermute | solution.py:532
  29.4 1.2 %collective-permute-start.13 = (bf16[128,256]{1,0:T(8,128)(2,1)S(1)}, bf16[128,256]{1,0:T(8,128)(2,1)S(1)}, u32[]{:S(2)}, u32[]{:S(2)}) collective-permute-start(bf16[128,256]{1,0:T(8,128)(2,1)S(1)} %get-tuple-element.115.near_ref), channel_id=1, source_target_pairs={{0,8},{8,0},{16,24},{24,16},{32,40},{40,32},{48,56},{56,48},{1,9},... | collective-permute-start | bytes 196616 | tf_op jit(solution)/shard_map/ppermute | solution.py:529
  30.6 2.1 %collective-permute-start.11 = (f32[8,128]{1,0:T(8,128)S(1)}, f32[8,128]{1,0:T(8,128)S(1)}, u32[]{:S(2)}, u32[]{:S(2)}) collective-permute-start(f32[8,128]{1,0:T(8,128)S(1)} %slice_add_fusion), channel_id=1, source_target_pairs={{0,6},{1,7},{2,4},{3,5},{4,2},{5,3},{6,0},{7,1},{8,14},{9,15},{10,... | collective-permute-start | bytes 12296 | tf_op jit(solution)/shard_map/ppermute | solution.py:545
  32.7 1.4 %shard_map.128 = (bf16[128,1024]{1,0:T(8,128)(2,1)}, f32[128,1024]{1,0:T(8,128)S(1)}, bf16[128,256]{1,0:T(8,128)(2,1)S(1)}, f32[128,256]{1,0:T(8,128)S(1)}) custom-call(f32[16,256]{1,0:T(8,128)S(1)} %get-tuple-element.67.facts_ref, bf16[128,1024]{1,0:T(8,128)(2,1)S(1)} %get-tuple-element.69.query_t_ref, bf16[128,1024]{1,0:T(8,128)(2,1)S(1)} %get-tuple-element.70.grad_t_ref, ...), custom_call_target="tpu_custom_call" | custom-call | flops 335544320 | tf_op jit(solution)/shard_map/pallas_call | solution.py:493
  34.1 1.3 %collective-permute-done.11 = f32[8,128]{1,0:T(8,128)S(1)} collective-permute-done((f32[8,128]{1,0:T(8,128)S(1)}, f32[8,128]{1,0:T(8,128)S(1)}, u32[]{:S(2)}, u32[]{:S(2)}) %collective-permute-start.11) | collective-permute-done | bytes 4128 | tf_op jit(solution)/shard_map/ppermute | solution.py:545
  35.6 3.8 %collective-permute-start.16 = (bf16[144,256]{1,0:T(8,128)(2,1)S(1)}, bf16[144,256]{1,0:T(8,128)(2,1)S(1)}, u32[]{:S(2)}, u32[]{:S(2)}) collective-permute-start(bf16[144,256]{1,0:T(8,128)(2,1)S(1)} %get-tuple-element.120), channel_id=1, source_target_pairs={{0,40},{8,32},{16,56},{24,48},{32,8},{40,0},{48,24},{56,16},{1,41}... | collective-permute-start | bytes 221192 | tf_op jit(solution)/shard_map/ppermute | solution.py:529
  39.4 0.9 %collective-permute-start.17 = (bf16[144,256]{1,0:T(8,128)(2,1)S(1)}, bf16[144,256]{1,0:T(8,128)(2,1)S(1)}, u32[]{:S(2)}, u32[]{:S(2)}) collective-permute-start(bf16[144,256]{1,0:T(8,128)(2,1)S(1)} %get-tuple-element.121), channel_id=1, source_target_pairs={{0,48},{8,56},{16,32},{24,40},{32,16},{40,24},{48,0},{56,8},{1,49}... | collective-permute-start | bytes 221192 | tf_op jit(solution)/shard_map/ppermute | solution.py:529
  40.3 1.3 %collective-permute-start.18 = (f32[8,128]{1,0:T(8,128)S(1)}, f32[8,128]{1,0:T(8,128)S(1)}, u32[]{:S(2)}, u32[]{:S(2)}) collective-permute-start(f32[8,128]{1,0:T(8,128)S(1)} %add.15.totals_ref), channel_id=1, source_target_pairs={{0,16},{8,24},{16,0},{24,8},{32,48},{40,56},{48,32},{56,40},{1,17}... | collective-permute-start | bytes 12296 | tf_op jit(solution)/shard_map/ppermute | solution.py:529
  41.5 3.6 %collective-permute-done.18.rest_ref = f32[8,128]{1,0:T(8,128)S(1)} collective-permute-done((f32[8,128]{1,0:T(8,128)S(1)}, f32[8,128]{1,0:T(8,128)S(1)}, u32[]{:S(2)}, u32[]{:S(2)}) %collective-permute-start.18) | collective-permute-done | bytes 4128 | tf_op jit(solution)/shard_map/ppermute | solution.py:529
  45.4 1.2 %collective-permute-done.17.far6 = bf16[144,256]{1,0:T(8,128)(2,1)S(1)} collective-permute-done((bf16[144,256]{1,0:T(8,128)(2,1)S(1)}, bf16[144,256]{1,0:T(8,128)(2,1)S(1)}, u32[]{:S(2)}, u32[]{:S(2)}) %collective-permute-start.17) | collective-permute-done | bytes 73760 | tf_op jit(solution)/shard_map/ppermute | solution.py:529
  46.6 0.8 %shard_map.131 = (bf16[128,1024]{1,0:T(8,128)(2,1)}, bf16[128,128]{1,0:T(8,128)(2,1)}, bf16[128,128]{1,0:T(8,128)(2,1)}, f32[1,4]{1,0:T(1,128)}) custom-call(f32[16,256]{1,0:T(8,128)S(1)} %get-tuple-element.67.facts_ref, f32[128,256]{1,0:T(8,128)S(1)} %get-tuple-element.106.local_ref, bf16[128,256]{1,0:T(8,128)(2,1)S(1)} %collective-permute-done.8.mate_ref, ...), custom_call_target="tpu_custom_call" | custom-call | tf_op jit(solution)/shard_map/pallas_call | solution.py:493
  (31 shorter events, 5.0 us)
Async XLA Ops:
  1.4 11.6 %collective-permute-start = (bf16[128,256]{1,0:T(8,128)(2,1)S(1)}, bf16[128,256]{1,0:T(8,128)(2,1)S(1)}, u32[]{:S(2)}, u32[]{:S(2)}) collective-permute-start(bf16[128,256]{1,0:T(8,128)(2,1)S(1)} %shard_map.119.own_ref.right_ref), channel_id=1, source_target_pairs={{0,48},{8,56},{16,32},{24,40},{32,16},{40,24},{48,0},{56,8},{1,49}... | collective-permute-start | bytes 196616 | tf_op jit(solution)/shard_map/ppermute | solution.py:529
  6.9 7.5 %collective-permute-start.1 = (bf16[128,256]{1,0:T(8,128)(2,1)S(1)}, bf16[128,256]{1,0:T(8,128)(2,1)S(1)}, u32[]{:S(2)}, u32[]{:S(2)}) collective-permute-start(bf16[128,256]{1,0:T(8,128)(2,1)S(1)} %shard_map.119.own_ref.right_ref), channel_id=1, source_target_pairs={{0,40},{8,32},{16,56},{24,48},{32,8},{40,0},{48,24},{56,16},{1,41}... | collective-permute-start | bytes 196616 | tf_op jit(solution)/shard_map/ppermute | solution.py:529
  8.4 6.0 %collective-permute-start.2 = (f32[8,128]{1,0:T(8,128)S(1)}, f32[8,128]{1,0:T(8,128)S(1)}, u32[]{:S(2)}, u32[]{:S(2)}) collective-permute-start(f32[8,128]{1,0:T(8,128)S(1)} %get-tuple-element.77), channel_id=1, source_target_pairs={{0,1},{1,0},{2,3},{3,2},{4,5},{5,4},{6,7},{7,6},{8,9},{9,8},{10,11... | collective-permute-start | bytes 12296 | tf_op jit(solution)/shard_map/ppermute | solution.py:548
  11.7 6.4 %collective-permute-start.4 = (bf16[128,256]{1,0:T(8,128)(2,1)S(1)}, bf16[128,256]{1,0:T(8,128)(2,1)S(1)}, u32[]{:S(2)}, u32[]{:S(2)}) collective-permute-start(bf16[128,256]{1,0:T(8,128)(2,1)S(1)} %shard_map.119.own_ref.right_ref), channel_id=1, source_target_pairs={{0,64},{64,0},{128,192},{192,128},{1,65},{65,1},{129,193},{193,129... | collective-permute-start | bytes 196616 | tf_op jit(solution)/shard_map/ppermute | solution.py:532
  14.5 5.6 %collective-permute-start.3 = (bf16[144,256]{1,0:T(8,128)(2,1)S(1)}, bf16[144,256]{1,0:T(8,128)(2,1)S(1)}, u32[]{:S(2)}, u32[]{:S(2)}) collective-permute-start(bf16[144,256]{1,0:T(8,128)(2,1)S(1)} %get-tuple-element.82), channel_id=1, source_target_pairs={{0,136},{8,128},{16,152},{24,144},{32,168},{40,160},{48,184},{56,1... | collective-permute-start | bytes 221192 | tf_op jit(solution)/shard_map/ppermute | solution.py:540
  16.4 4.4 %collective-permute-start.5 = (bf16[144,256]{1,0:T(8,128)(2,1)S(1)}, bf16[144,256]{1,0:T(8,128)(2,1)S(1)}, u32[]{:S(2)}, u32[]{:S(2)}) collective-permute-start(bf16[144,256]{1,0:T(8,128)(2,1)S(1)} %get-tuple-element.87), channel_id=1, source_target_pairs={{0,8},{8,0},{16,24},{24,16},{32,40},{40,32},{48,56},{56,48},{1,9},... | collective-permute-start | bytes 221192 | tf_op jit(solution)/shard_map/ppermute | solution.py:529
  17.6 4.4 %collective-permute-start.6 = (bf16[144,256]{1,0:T(8,128)(2,1)S(1)}, bf16[144,256]{1,0:T(8,128)(2,1)S(1)}, u32[]{:S(2)}, u32[]{:S(2)}) collective-permute-start(bf16[144,256]{1,0:T(8,128)(2,1)S(1)} %get-tuple-element.88), channel_id=1, source_target_pairs={{0,128},{64,192},{128,0},{192,64},{1,129},{65,193},{129,1},{193,65... | collective-permute-start | bytes 221192 | tf_op jit(solution)/shard_map/ppermute | solution.py:532
  22.0 1.4 %collective-permute-start.7 = (bf16[256,256]{1,0:T(8,128)(2,1)S(1)}, bf16[256,256]{1,0:T(8,128)(2,1)S(1)}, u32[]{:S(2)}, u32[]{:S(2)}) collective-permute-start(bf16[256,256]{1,0:T(8,128)(2,1)S(1)} %get-tuple-element.90.left_ref.right_ref), channel_id=1, source_target_pairs={{0,64},{64,0},{128,192},{192,128},{1,65},{65,1},{129,193},{193,129... | collective-permute-start | bytes 393224 | tf_op jit(solution)/shard_map/ppermute | solution.py:532
  22.1 2.6 %collective-permute-start.9 = (f32[128,128]{1,0:T(8,128)S(1)}, f32[128,128]{1,0:T(8,128)S(1)}, u32[]{:S(2)}, u32[]{:S(2)}) collective-permute-start(f32[128,128]{1,0:T(8,128)S(1)} %get-tuple-element.111), channel_id=1, source_target_pairs={{0,64},{64,0},{128,192},{192,128},{1,65},{65,1},{129,193},{193,129... | collective-permute-start | bytes 196616 | tf_op jit(solution)/shard_map/ppermute | solution.py:532
  24.8 2.2 %collective-permute-start.12 = (bf16[256,256]{1,0:T(8,128)(2,1)S(1)}, bf16[256,256]{1,0:T(8,128)(2,1)S(1)}, u32[]{:S(2)}, u32[]{:S(2)}) collective-permute-start(bf16[256,256]{1,0:T(8,128)(2,1)S(1)} %get-tuple-element.114), channel_id=1, source_target_pairs={{0,64},{64,0},{128,192},{192,128},{1,65},{65,1},{129,193},{193,129... | collective-permute-start | bytes 393224 | tf_op jit(solution)/shard_map/ppermute | solution.py:532
  25.0 5.6 %collective-permute-start.10 = (f32[128,128]{1,0:T(8,128)S(1)}, f32[128,128]{1,0:T(8,128)S(1)}, u32[]{:S(2)}, u32[]{:S(2)}) collective-permute-start(f32[128,128]{1,0:T(8,128)S(1)} %add.13), channel_id=1, source_target_pairs={{0,2},{1,3},{2,0},{3,1},{4,6},{5,7},{6,4},{7,5},{8,10},{9,11},{10,... | collective-permute-start | bytes 196616 | tf_op jit(solution)/shard_map/ppermute | solution.py:545
  27.0 8.4 %collective-permute-start.15 = (bf16[128,256]{1,0:T(8,128)(2,1)S(1)}, bf16[128,256]{1,0:T(8,128)(2,1)S(1)}, u32[]{:S(2)}, u32[]{:S(2)}) collective-permute-start(bf16[128,256]{1,0:T(8,128)(2,1)S(1)} %get-tuple-element.116), channel_id=1, source_target_pairs={{0,136},{8,128},{16,152},{24,144},{32,168},{40,160},{48,184},{56,1... | collective-permute-start | bytes 196616 | tf_op jit(solution)/shard_map/ppermute | solution.py:540
  27.8 7.6 %collective-permute-start.14 = (bf16[128,256]{1,0:T(8,128)(2,1)S(1)}, bf16[128,256]{1,0:T(8,128)(2,1)S(1)}, u32[]{:S(2)}, u32[]{:S(2)}) collective-permute-start(bf16[128,256]{1,0:T(8,128)(2,1)S(1)} %get-tuple-element.116), channel_id=1, source_target_pairs={{0,128},{64,192},{128,0},{192,64},{1,129},{65,193},{129,1},{193,65... | collective-permute-start | bytes 196616 | tf_op jit(solution)/shard_map/ppermute | solution.py:532
  29.4 6.0 %collective-permute-start.13 = (bf16[128,256]{1,0:T(8,128)(2,1)S(1)}, bf16[128,256]{1,0:T(8,128)(2,1)S(1)}, u32[]{:S(2)}, u32[]{:S(2)}) collective-permute-start(bf16[128,256]{1,0:T(8,128)(2,1)S(1)} %get-tuple-element.115.near_ref), channel_id=1, source_target_pairs={{0,8},{8,0},{16,24},{24,16},{32,40},{40,32},{48,56},{56,48},{1,9},... | collective-permute-start | bytes 196616 | tf_op jit(solution)/shard_map/ppermute | solution.py:529
  30.6 4.8 %collective-permute-start.11 = (f32[8,128]{1,0:T(8,128)S(1)}, f32[8,128]{1,0:T(8,128)S(1)}, u32[]{:S(2)}, u32[]{:S(2)}) collective-permute-start(f32[8,128]{1,0:T(8,128)S(1)} %slice_add_fusion), channel_id=1, source_target_pairs={{0,6},{1,7},{2,4},{3,5},{4,2},{5,3},{6,0},{7,1},{8,14},{9,15},{10,... | collective-permute-start | bytes 12296 | tf_op jit(solution)/shard_map/ppermute | solution.py:545
  35.6 9.8 %collective-permute-start.16 = (bf16[144,256]{1,0:T(8,128)(2,1)S(1)}, bf16[144,256]{1,0:T(8,128)(2,1)S(1)}, u32[]{:S(2)}, u32[]{:S(2)}) collective-permute-start(bf16[144,256]{1,0:T(8,128)(2,1)S(1)} %get-tuple-element.120), channel_id=1, source_target_pairs={{0,40},{8,32},{16,56},{24,48},{32,8},{40,0},{48,24},{56,16},{1,41}... | collective-permute-start | bytes 221192 | tf_op jit(solution)/shard_map/ppermute | solution.py:529
  39.4 7.3 %collective-permute-start.17 = (bf16[144,256]{1,0:T(8,128)(2,1)S(1)}, bf16[144,256]{1,0:T(8,128)(2,1)S(1)}, u32[]{:S(2)}, u32[]{:S(2)}) collective-permute-start(bf16[144,256]{1,0:T(8,128)(2,1)S(1)} %get-tuple-element.121), channel_id=1, source_target_pairs={{0,48},{8,56},{16,32},{24,40},{32,16},{40,24},{48,0},{56,8},{1,49}... | collective-permute-start | bytes 221192 | tf_op jit(solution)/shard_map/ppermute | solution.py:529
  40.2 1.3 %collective-permute-start.8 = (bf16[128,256]{1,0:T(8,128)(2,1)S(1)}, bf16[128,256]{1,0:T(8,128)(2,1)S(1)}, u32[]{:S(2)}, u32[]{:S(2)}) collective-permute-start(bf16[128,256]{1,0:T(8,128)(2,1)S(1)} %get-tuple-element.107), channel_id=1, source_target_pairs={{0,64},{64,0},{128,192},{192,128},{1,65},{65,1},{129,193},{193,129... | collective-permute-start | bytes 196616 | tf_op jit(solution)/shard_map/ppermute | solution.py:532
  40.3 4.9 %collective-permute-start.18 = (f32[8,128]{1,0:T(8,128)S(1)}, f32[8,128]{1,0:T(8,128)S(1)}, u32[]{:S(2)}, u32[]{:S(2)}) collective-permute-start(f32[8,128]{1,0:T(8,128)S(1)} %add.15.totals_ref), channel_id=1, source_target_pairs={{0,16},{8,24},{16,0},{24,8},{32,48},{40,56},{48,32},{56,40},{1,17}... | collective-permute-start | bytes 12296 | tf_op jit(solution)/shard_map/ppermute | solution.py:529

commit v5 on v4

--- a/solution.py
+++ b/solution.py
@@ -51,23 +51,14 @@
     return (left[:8] + right[:8]) + left[8:]
 
 
-def pack_kernel(key_ref, value_ref, out_ref, sems):
-    dim = key_ref.shape[1]
-    copies = [
-        pltpu.make_async_copy(ref, out_ref.at[:, pl.ds(i * dim, dim)], sems.at[i])
-        for i, ref in enumerate((key_ref, value_ref))
-    ]
-    for copy in copies:
-        copy.start()
-    for copy in copies:
-        copy.wait()
-
-
 def facts_kernel(
     order_hbm,
     counts_hbm,
     mask_hbm,
     ratio_hbm,
+    key_hbm,
+    value_hbm,
+    own_ref,
     facts_ref,
     totals_ref,
     kept_ref,
@@ -77,6 +68,7 @@
     ratio_ref,
     sems,
 ):
+    dim = key_hbm.shape[1]
     copies = [
         pltpu.make_async_copy(source, target, sems.at[i])
         for i, (source, target) in enumerate(
@@ -85,6 +77,8 @@
                 (counts_hbm, counts_ref),
                 (mask_hbm, mask_ref),
                 (ratio_hbm, ratio_ref),
+                (key_hbm, own_ref.at[:, pl.ds(0, dim)]),
+                (value_hbm, own_ref.at[:, pl.ds(dim, dim)]),
             )
         )
     ]
@@ -95,7 +89,7 @@
     head = lax.axis_index("head")
     pairs = lax.axis_size("grp") // 2
     is_response = grp >= pairs
-    for copy in copies:
+    for copy in copies[:4]:
         copy.wait()
 
     def pair_of(group, half):
@@ -144,6 +138,8 @@
     negative = jnp.logical_and(is_response, order_ref[slot] % 2 == 0)
     sign = jnp.where(valid, jnp.where(negative, -1.0, 1.0), 0.0).astype(F32)
     kept_ref[...] = jnp.where(kept, sign, 0.0)
+    for copy in copies[4:]:
+        copy.wait()
 
 
 def prepare_kernel(
@@ -547,25 +543,28 @@
     def along_y(value):
         return lax.ppermute(value, "head", swap(head_count, 1))
 
-    own = call(
-        pack_kernel, grads, (key_heads[0], value_heads[0]), scratch=[dma((2,))], in_hbm=2
-    )
-    far6 = along_grp(own, 6)
-    far5 = along_grp(own, 5)
-    own, response_order = tie((own, response_order))
-    facts, totals, kept = call(
+    own, facts, totals, kept = call(
         facts_kernel,
-        [shape((FACTS, both), F32), total_tile, shape((1, rows), F32)],
-        (response_order, block_counts, loss_mask, log_ratio),
+        [grads, shape((FACTS, both), F32), total_tile, shape((1, rows), F32)],
+        (
+            response_order,
+            block_counts,
+            loss_mask,
+            log_ratio,
+            key_heads[0],
+            value_heads[0],
+        ),
         scratch=[
             pltpu.SMEM(response_order.shape, jnp.int32),
             pltpu.SMEM(block_counts.shape, jnp.int32),
             pltpu.VMEM(loss_mask.shape, jnp.int32),
             pltpu.VMEM(log_ratio.shape, F32),
-            dma((4,)),
+            dma((6,)),
         ],
-        in_hbm=4,
-    )
+        in_hbm=6,
+    )
+    far6 = along_grp(own, 6)
+    far5 = along_grp(own, 5)
     mate_own = along_seq(own, 1)
     stacked = shape((every, dim), BF16)
     query_rows, query_cols, grad_rows, grad_cols = call(

time: 47.7 us -> 47.5 us (level)
  the two profiles are of different devices: /device:TPU:32 before, /device:TPU:16 now
where the time goes in v5:
time: 47.5 us; the launch traced here: 47.3 us
  starting transfers between devices  25.6 us (54%)
  waiting for transfers between devices  13.3 us (28%)
  Pallas kernels  7.66 us (16%)
  between operations  0.75 us (2%)
    ppermute x7, starting transfers between devices, along_grp(): return lax.ppermute(value, 'grp', swap(group_count, turn))  15.4 us
    ppermute x7, waiting for transfers between devices, along_grp(): return lax.ppermute(value, 'grp', swap(group_count, turn))  9.62 us
    pallas_call x12, Pallas kernels, call(): pl.pallas_call(kernel, out_shape=out_shapes, in_specs=[VMEM_SPEC] * plain...  7.66 us
    ppermute x2, starting transfers between devices, along_x(): return lax.ppermute(value, 'head', round_way if step else near)  3.6 us
    ppermute x2, starting transfers between devices, across(): return lax.ppermute(value, ('seq', 'grp'), turns)  3.45 us
    ppermute x7, starting transfers between devices, along_seq(): return lax.ppermute(value, 'seq', swap(seq_count, turn))  2.86 us
    ppermute x2, waiting for transfers between devices, along_x(): return lax.ppermute(value, 'head', round_way if step else near)  1.34 us
    ppermute x2, waiting for transfers between devices, across(): return lax.ppermute(value, ('seq', 'grp'), turns)  1.2 us
  transfers between devices with their start and end apart: 19, of which 9 were waited for; matrix products, arithmetic and copies ran while one was open for 0% of the time, Pallas kernels for 12%

profile of v5, /device:TPU:16, one launch (start us, length us, event | category | flops | bytes accessed | tf_op | source)
XLA Modules:
  0.0 47.3 jit_solution(9219226040671904639)
XLA Ops:
  0.6 0.9 %shard_map.119 = (bf16[128,256]{1,0:T(8,128)(2,1)S(1)}, f32[16,256]{1,0:T(8,128)S(1)}, f32[8,128]{1,0:T(8,128)S(1)}, f32[1,128]{1,0:T(1,128)S(1)}) custom-call(s32[8]{0:T(128)} %order_hbm.1, s32[8]{0:T(128)} %counts_hbm.1, s32[1,128]{1,0:T(1,128)} %mask_hbm.1, f32[1,16]{1,0:T(1,128)} %ratio_hbm.1, bf16[128,128]{1,0:T(8,128)(2,1)} %bitcast.11, ...), custom_call_target="tpu_custom_call" | custom-call | tf_op jit(solution)/shard_map/pallas_call | solution.py:489
  1.6 6.4 %collective-permute-start = (bf16[128,256]{1,0:T(8,128)(2,1)S(1)}, bf16[128,256]{1,0:T(8,128)(2,1)S(1)}, u32[]{:S(2)}, u32[]{:S(2)}) collective-permute-start(bf16[128,256]{1,0:T(8,128)(2,1)S(1)} %get-tuple-element.69.own_ref.right_ref), channel_id=1, source_target_pairs={{0,48},{8,56},{16,32},{24,40},{32,16},{40,24},{48,0},{56,8},{1,49}... | collective-permute-start | bytes 196616 | tf_op jit(solution)/shard_map/ppermute | solution.py:525
  8.0 1.0 %collective-permute-start.1 = (bf16[128,256]{1,0:T(8,128)(2,1)S(1)}, bf16[128,256]{1,0:T(8,128)(2,1)S(1)}, u32[]{:S(2)}, u32[]{:S(2)}) collective-permute-start(bf16[128,256]{1,0:T(8,128)(2,1)S(1)} %get-tuple-element.69.own_ref.right_ref), channel_id=1, source_target_pairs={{0,40},{8,32},{16,56},{24,48},{32,8},{40,0},{48,24},{56,16},{1,41}... | collective-permute-start | bytes 196616 | tf_op jit(solution)/shard_map/ppermute | solution.py:525
  9.3 1.4 %shard_map.120 = (bf16[1024,128]{1,0:T(8,128)(2,1)S(1)}, bf16[128,1024]{1,0:T(8,128)(2,1)S(1)}, bf16[1024,128]{1,0:T(8,128)(2,1)S(1)}, bf16[128,1024]{1,0:T(8,128)(2,1)S(1)}) custom-call(f32[1,128]{1,0:T(1,128)S(1)} %get-tuple-element.66.kept_ref, bf16[128,1024]{1,0:T(8,128)(2,1)} %bitcast.9, bf16[128,1024]{1,0:T(8,128)(2,1)} %bitcast.10), custom_call_target="tpu_custom_call" | custom-call | tf_op jit(solution)/shard_map/pallas_call | solution.py:489
  10.7 1.9 %collective-permute-done.far6 = bf16[128,256]{1,0:T(8,128)(2,1)S(1)} collective-permute-done((bf16[128,256]{1,0:T(8,128)(2,1)S(1)}, bf16[128,256]{1,0:T(8,128)(2,1)S(1)}, u32[]{:S(2)}, u32[]{:S(2)}) %collective-permute-start) | collective-permute-done | bytes 65568 | tf_op jit(solution)/shard_map/ppermute | solution.py:525
  12.6 2.7 %collective-permute-done.1.far5 = bf16[128,256]{1,0:T(8,128)(2,1)S(1)} collective-permute-done((bf16[128,256]{1,0:T(8,128)(2,1)S(1)}, bf16[128,256]{1,0:T(8,128)(2,1)S(1)}, u32[]{:S(2)}, u32[]{:S(2)}) %collective-permute-start.1) | collective-permute-done | bytes 65568 | tf_op jit(solution)/shard_map/ppermute | solution.py:525
  15.3 2.0 %collective-permute-start.3 = (bf16[144,256]{1,0:T(8,128)(2,1)S(1)}, bf16[144,256]{1,0:T(8,128)(2,1)S(1)}, u32[]{:S(2)}, u32[]{:S(2)}) collective-permute-start(bf16[144,256]{1,0:T(8,128)(2,1)S(1)} %get-tuple-element.80), channel_id=1, source_target_pairs={{0,136},{8,128},{16,152},{24,144},{32,168},{40,160},{48,184},{56,1... | collective-permute-start | bytes 221192 | tf_op jit(solution)/shard_map/ppermute | solution.py:536
  17.3 0.8 %collective-permute-start.5 = (bf16[144,256]{1,0:T(8,128)(2,1)S(1)}, bf16[144,256]{1,0:T(8,128)(2,1)S(1)}, u32[]{:S(2)}, u32[]{:S(2)}) collective-permute-start(bf16[144,256]{1,0:T(8,128)(2,1)S(1)} %get-tuple-element.85), channel_id=1, source_target_pairs={{0,8},{8,0},{16,24},{24,16},{32,40},{40,32},{48,56},{56,48},{1,9},... | collective-permute-start | bytes 221192 | tf_op jit(solution)/shard_map/ppermute | solution.py:525
  19.5 1.2 %collective-permute-done.3.cross_ref = bf16[144,256]{1,0:T(8,128)(2,1)S(1)} collective-permute-done((bf16[144,256]{1,0:T(8,128)(2,1)S(1)}, bf16[144,256]{1,0:T(8,128)(2,1)S(1)}, u32[]{:S(2)}, u32[]{:S(2)}) %collective-permute-start.3) | collective-permute-done | bytes 73760 | tf_op jit(solution)/shard_map/ppermute | solution.py:536
  20.7 1.0 %collective-permute-done.5.group_ref = bf16[144,256]{1,0:T(8,128)(2,1)S(1)} collective-permute-done((bf16[144,256]{1,0:T(8,128)(2,1)S(1)}, bf16[144,256]{1,0:T(8,128)(2,1)S(1)}, u32[]{:S(2)}, u32[]{:S(2)}) %collective-permute-start.5) | collective-permute-done | bytes 73760 | tf_op jit(solution)/shard_map/ppermute | solution.py:525
  21.7 0.8 %collective-permute-done.6.seq_ref = bf16[144,256]{1,0:T(8,128)(2,1)S(1)} collective-permute-done((bf16[144,256]{1,0:T(8,128)(2,1)S(1)}, bf16[144,256]{1,0:T(8,128)(2,1)S(1)}, u32[]{:S(2)}, u32[]{:S(2)}) %collective-permute-start.6) | collective-permute-done | bytes 73760 | tf_op jit(solution)/shard_map/ppermute | solution.py:528
  24.0 1.3 %shard_map.125 = (bf16[256,256]{1,0:T(8,128)(2,1)S(1)}, f32[128,1024]{1,0:T(8,128)S(1)}, bf16[256,1024]{1,0:T(8,128)(2,1)S(1)}, bf16[128,256]{1,0:T(8,128)(2,1)S(1)}, f32[8,1024]{1,0:T(8,128)S(1)}) custom-call(f32[16,256]{1,0:T(8,128)S(1)} %get-tuple-element.65.facts_ref, bf16[1024,128]{1,0:T(8,128)(2,1)S(1)} %get-tuple-element.72.query_ref, ...), custom_call_target="tpu_custom_call" | custom-call | flops 402653184 | tf_op jit(solution)/shard_map/pallas_call | solution.py:489
  25.6 1.5 %collective-permute-start.10 = (f32[128,128]{1,0:T(8,128)S(1)}, f32[128,128]{1,0:T(8,128)S(1)}, u32[]{:S(2)}, u32[]{:S(2)}) collective-permute-start(f32[128,128]{1,0:T(8,128)S(1)} %add.13), channel_id=1, source_target_pairs={{0,2},{1,3},{2,0},{3,1},{4,6},{5,7},{6,4},{7,5},{8,10},{9,11},{10,... | collective-permute-start | bytes 196616 | tf_op jit(solution)/shard_map/ppermute | solution.py:541
  27.6 1.5 %collective-permute-start.15 = (bf16[128,256]{1,0:T(8,128)(2,1)S(1)}, bf16[128,256]{1,0:T(8,128)(2,1)S(1)}, u32[]{:S(2)}, u32[]{:S(2)}) collective-permute-start(bf16[128,256]{1,0:T(8,128)(2,1)S(1)} %get-tuple-element.114), channel_id=1, source_target_pairs={{0,136},{8,128},{16,152},{24,144},{32,168},{40,160},{48,184},{56,1... | collective-permute-start | bytes 196616 | tf_op jit(solution)/shard_map/ppermute | solution.py:536
  29.1 1.3 %collective-permute-start.14 = (bf16[128,256]{1,0:T(8,128)(2,1)S(1)}, bf16[128,256]{1,0:T(8,128)(2,1)S(1)}, u32[]{:S(2)}, u32[]{:S(2)}) collective-permute-start(bf16[128,256]{1,0:T(8,128)(2,1)S(1)} %get-tuple-element.114), channel_id=1, source_target_pairs={{0,128},{64,192},{128,0},{192,64},{1,129},{65,193},{129,1},{193,65... | collective-permute-start | bytes 196616 | tf_op jit(solution)/shard_map/ppermute | solution.py:528
  30.3 0.8 %collective-permute-start.13 = (bf16[128,256]{1,0:T(8,128)(2,1)S(1)}, bf16[128,256]{1,0:T(8,128)(2,1)S(1)}, u32[]{:S(2)}, u32[]{:S(2)}) collective-permute-start(bf16[128,256]{1,0:T(8,128)(2,1)S(1)} %get-tuple-element.113.near_ref), channel_id=1, source_target_pairs={{0,8},{8,0},{16,24},{24,16},{32,40},{40,32},{48,56},{56,48},{1,9},... | collective-permute-start | bytes 196616 | tf_op jit(solution)/shard_map/ppermute | solution.py:525
  31.2 2.1 %collective-permute-start.11 = (f32[8,128]{1,0:T(8,128)S(1)}, f32[8,128]{1,0:T(8,128)S(1)}, u32[]{:S(2)}, u32[]{:S(2)}) collective-permute-start(f32[8,128]{1,0:T(8,128)S(1)} %slice_add_fusion), channel_id=1, source_target_pairs={{0,6},{1,7},{2,4},{3,5},{4,2},{5,3},{6,0},{7,1},{8,14},{9,15},{10,... | collective-permute-start | bytes 12296 | tf_op jit(solution)/shard_map/ppermute | solution.py:541
  33.3 1.4 %shard_map.127 = (bf16[128,1024]{1,0:T(8,128)(2,1)}, f32[128,1024]{1,0:T(8,128)S(1)}, bf16[128,256]{1,0:T(8,128)(2,1)S(1)}, f32[128,256]{1,0:T(8,128)S(1)}) custom-call(f32[16,256]{1,0:T(8,128)S(1)} %get-tuple-element.65.facts_ref, bf16[128,1024]{1,0:T(8,128)(2,1)S(1)} %get-tuple-element.67.query_t_ref, bf16[128,1024]{1,0:T(8,128)(2,1)S(1)} %get-tuple-element.68.grad_t_ref, ...), custom_call_target="tpu_custom_call" | custom-call | flops 335544320 | tf_op jit(solution)/shard_map/pallas_call | solution.py:489
  34.7 1.3 %collective-permute-done.11 = f32[8,128]{1,0:T(8,128)S(1)} collective-permute-done((f32[8,128]{1,0:T(8,128)S(1)}, f32[8,128]{1,0:T(8,128)S(1)}, u32[]{:S(2)}, u32[]{:S(2)}) %collective-permute-start.11) | collective-permute-done | bytes 4128 | tf_op jit(solution)/shard_map/ppermute | solution.py:541
  36.1 3.9 %collective-permute-start.16 = (bf16[144,256]{1,0:T(8,128)(2,1)S(1)}, bf16[144,256]{1,0:T(8,128)(2,1)S(1)}, u32[]{:S(2)}, u32[]{:S(2)}) collective-permute-start(bf16[144,256]{1,0:T(8,128)(2,1)S(1)} %get-tuple-element.118), channel_id=1, source_target_pairs={{0,40},{8,32},{16,56},{24,48},{32,8},{40,0},{48,24},{56,16},{1,41}... | collective-permute-start | bytes 221192 | tf_op jit(solution)/shard_map/ppermute | solution.py:525
  40.8 1.6 %collective-permute-start.18 = (f32[8,128]{1,0:T(8,128)S(1)}, f32[8,128]{1,0:T(8,128)S(1)}, u32[]{:S(2)}, u32[]{:S(2)}) collective-permute-start(f32[8,128]{1,0:T(8,128)S(1)} %add.15.totals_ref), channel_id=1, source_target_pairs={{0,16},{8,24},{16,0},{24,8},{32,48},{40,56},{48,32},{56,40},{1,17}... | collective-permute-start | bytes 12296 | tf_op jit(solution)/shard_map/ppermute | solution.py:525
  42.5 2.9 %collective-permute-done.18.rest_ref = f32[8,128]{1,0:T(8,128)S(1)} collective-permute-done((f32[8,128]{1,0:T(8,128)S(1)}, f32[8,128]{1,0:T(8,128)S(1)}, u32[]{:S(2)}, u32[]{:S(2)}) %collective-permute-start.18) | collective-permute-done | bytes 4128 | tf_op jit(solution)/shard_map/ppermute | solution.py:525
  45.3 1.2 %collective-permute-done.17.far6 = bf16[144,256]{1,0:T(8,128)(2,1)S(1)} collective-permute-done((bf16[144,256]{1,0:T(8,128)(2,1)S(1)}, bf16[144,256]{1,0:T(8,128)(2,1)S(1)}, u32[]{:S(2)}, u32[]{:S(2)}) %collective-permute-start.17) | collective-permute-done | bytes 73760 | tf_op jit(solution)/shard_map/ppermute | solution.py:525
  46.5 0.8 %shard_map.130 = (bf16[128,1024]{1,0:T(8,128)(2,1)}, bf16[128,128]{1,0:T(8,128)(2,1)}, bf16[128,128]{1,0:T(8,128)(2,1)}, f32[1,4]{1,0:T(1,128)}) custom-call(f32[16,256]{1,0:T(8,128)S(1)} %get-tuple-element.65.facts_ref, f32[128,256]{1,0:T(8,128)S(1)} %get-tuple-element.104.local_ref, bf16[128,256]{1,0:T(8,128)(2,1)S(1)} %collective-permute-done.8.mate_ref, ...), custom_call_target="tpu_custom_call" | custom-call | tf_op jit(solution)/shard_map/pallas_call | solution.py:489
  (30 shorter events, 4.9 us)
Async XLA Ops:
  1.6 11.0 %collective-permute-start = (bf16[128,256]{1,0:T(8,128)(2,1)S(1)}, bf16[128,256]{1,0:T(8,128)(2,1)S(1)}, u32[]{:S(2)}, u32[]{:S(2)}) collective-permute-start(bf16[128,256]{1,0:T(8,128)(2,1)S(1)} %get-tuple-element.69.own_ref.right_ref), channel_id=1, source_target_pairs={{0,48},{8,56},{16,32},{24,40},{32,16},{40,24},{48,0},{56,8},{1,49}... | collective-permute-start | bytes 196616 | tf_op jit(solution)/shard_map/ppermute | solution.py:525
  8.0 7.3 %collective-permute-start.1 = (bf16[128,256]{1,0:T(8,128)(2,1)S(1)}, bf16[128,256]{1,0:T(8,128)(2,1)S(1)}, u32[]{:S(2)}, u32[]{:S(2)}) collective-permute-start(bf16[128,256]{1,0:T(8,128)(2,1)S(1)} %get-tuple-element.69.own_ref.right_ref), channel_id=1, source_target_pairs={{0,40},{8,32},{16,56},{24,48},{32,8},{40,0},{48,24},{56,16},{1,41}... | collective-permute-start | bytes 196616 | tf_op jit(solution)/shard_map/ppermute | solution.py:525
  9.0 6.3 %collective-permute-start.2 = (f32[8,128]{1,0:T(8,128)S(1)}, f32[8,128]{1,0:T(8,128)S(1)}, u32[]{:S(2)}, u32[]{:S(2)}) collective-permute-start(f32[8,128]{1,0:T(8,128)S(1)} %get-tuple-element.76), channel_id=1, source_target_pairs={{0,1},{1,0},{2,3},{3,2},{4,5},{5,4},{6,7},{7,6},{8,9},{9,8},{10,11... | collective-permute-start | bytes 12296 | tf_op jit(solution)/shard_map/ppermute | solution.py:544
  9.3 9.6 %collective-permute-start.4 = (bf16[128,256]{1,0:T(8,128)(2,1)S(1)}, bf16[128,256]{1,0:T(8,128)(2,1)S(1)}, u32[]{:S(2)}, u32[]{:S(2)}) collective-permute-start(bf16[128,256]{1,0:T(8,128)(2,1)S(1)} %get-tuple-element.69.own_ref.right_ref), channel_id=1, source_target_pairs={{0,64},{64,0},{128,192},{192,128},{1,65},{65,1},{129,193},{193,129... | collective-permute-start | bytes 196616 | tf_op jit(solution)/shard_map/ppermute | solution.py:528
  15.3 5.3 %collective-permute-start.3 = (bf16[144,256]{1,0:T(8,128)(2,1)S(1)}, bf16[144,256]{1,0:T(8,128)(2,1)S(1)}, u32[]{:S(2)}, u32[]{:S(2)}) collective-permute-start(bf16[144,256]{1,0:T(8,128)(2,1)S(1)} %get-tuple-element.80), channel_id=1, source_target_pairs={{0,136},{8,128},{16,152},{24,144},{32,168},{40,160},{48,184},{56,1... | collective-permute-start | bytes 221192 | tf_op jit(solution)/shard_map/ppermute | solution.py:536
  17.3 4.4 %collective-permute-start.5 = (bf16[144,256]{1,0:T(8,128)(2,1)S(1)}, bf16[144,256]{1,0:T(8,128)(2,1)S(1)}, u32[]{:S(2)}, u32[]{:S(2)}) collective-permute-start(bf16[144,256]{1,0:T(8,128)(2,1)S(1)} %get-tuple-element.85), channel_id=1, source_target_pairs={{0,8},{8,0},{16,24},{24,16},{32,40},{40,32},{48,56},{56,48},{1,9},... | collective-permute-start | bytes 221192 | tf_op jit(solution)/shard_map/ppermute | solution.py:525
  18.2 4.4 %collective-permute-start.6 = (bf16[144,256]{1,0:T(8,128)(2,1)S(1)}, bf16[144,256]{1,0:T(8,128)(2,1)S(1)}, u32[]{:S(2)}, u32[]{:S(2)}) collective-permute-start(bf16[144,256]{1,0:T(8,128)(2,1)S(1)} %get-tuple-element.86), channel_id=1, source_target_pairs={{0,128},{64,192},{128,0},{192,64},{1,129},{65,193},{129,1},{193,65... | collective-permute-start | bytes 221192 | tf_op jit(solution)/shard_map/ppermute | solution.py:528
  22.6 1.4 %collective-permute-start.7 = (bf16[256,256]{1,0:T(8,128)(2,1)S(1)}, bf16[256,256]{1,0:T(8,128)(2,1)S(1)}, u32[]{:S(2)}, u32[]{:S(2)}) collective-permute-start(bf16[256,256]{1,0:T(8,128)(2,1)S(1)} %get-tuple-element.88.left_ref.right_ref), channel_id=1, source_target_pairs={{0,64},{64,0},{128,192},{192,128},{1,65},{65,1},{129,193},{193,129... | collective-permute-start | bytes 393224 | tf_op jit(solution)/shard_map/ppermute | solution.py:528
  22.7 2.6 %collective-permute-start.9 = (f32[128,128]{1,0:T(8,128)S(1)}, f32[128,128]{1,0:T(8,128)S(1)}, u32[]{:S(2)}, u32[]{:S(2)}) collective-permute-start(f32[128,128]{1,0:T(8,128)S(1)} %get-tuple-element.109), channel_id=1, source_target_pairs={{0,64},{64,0},{128,192},{192,128},{1,65},{65,1},{129,193},{193,129... | collective-permute-start | bytes 196616 | tf_op jit(solution)/shard_map/ppermute | solution.py:528
  25.4 2.2 %collective-permute-start.12 = (bf16[256,256]{1,0:T(8,128)(2,1)S(1)}, bf16[256,256]{1,0:T(8,128)(2,1)S(1)}, u32[]{:S(2)}, u32[]{:S(2)}) collective-permute-start(bf16[256,256]{1,0:T(8,128)(2,1)S(1)} %get-tuple-element.112), channel_id=1, source_target_pairs={{0,64},{64,0},{128,192},{192,128},{1,65},{65,1},{129,193},{193,129... | collective-permute-start | bytes 393224 | tf_op jit(solution)/shard_map/ppermute | solution.py:528
  25.6 5.6 %collective-permute-start.10 = (f32[128,128]{1,0:T(8,128)S(1)}, f32[128,128]{1,0:T(8,128)S(1)}, u32[]{:S(2)}, u32[]{:S(2)}) collective-permute-start(f32[128,128]{1,0:T(8,128)S(1)} %add.13), channel_id=1, source_target_pairs={{0,2},{1,3},{2,0},{3,1},{4,6},{5,7},{6,4},{7,5},{8,10},{9,11},{10,... | collective-permute-start | bytes 196616 | tf_op jit(solution)/shard_map/ppermute | solution.py:541
  27.6 8.4 %collective-permute-start.15 = (bf16[128,256]{1,0:T(8,128)(2,1)S(1)}, bf16[128,256]{1,0:T(8,128)(2,1)S(1)}, u32[]{:S(2)}, u32[]{:S(2)}) collective-permute-start(bf16[128,256]{1,0:T(8,128)(2,1)S(1)} %get-tuple-element.114), channel_id=1, source_target_pairs={{0,136},{8,128},{16,152},{24,144},{32,168},{40,160},{48,184},{56,1... | collective-permute-start | bytes 196616 | tf_op jit(solution)/shard_map/ppermute | solution.py:536
  29.1 7.0 %collective-permute-start.14 = (bf16[128,256]{1,0:T(8,128)(2,1)S(1)}, bf16[128,256]{1,0:T(8,128)(2,1)S(1)}, u32[]{:S(2)}, u32[]{:S(2)}) collective-permute-start(bf16[128,256]{1,0:T(8,128)(2,1)S(1)} %get-tuple-element.114), channel_id=1, source_target_pairs={{0,128},{64,192},{128,0},{192,64},{1,129},{65,193},{129,1},{193,65... | collective-permute-start | bytes 196616 | tf_op jit(solution)/shard_map/ppermute | solution.py:528
  30.3 5.7 %collective-permute-start.13 = (bf16[128,256]{1,0:T(8,128)(2,1)S(1)}, bf16[128,256]{1,0:T(8,128)(2,1)S(1)}, u32[]{:S(2)}, u32[]{:S(2)}) collective-permute-start(bf16[128,256]{1,0:T(8,128)(2,1)S(1)} %get-tuple-element.113.near_ref), channel_id=1, source_target_pairs={{0,8},{8,0},{16,24},{24,16},{32,40},{40,32},{48,56},{56,48},{1,9},... | collective-permute-start | bytes 196616 | tf_op jit(solution)/shard_map/ppermute | solution.py:525
  31.2 4.8 %collective-permute-start.11 = (f32[8,128]{1,0:T(8,128)S(1)}, f32[8,128]{1,0:T(8,128)S(1)}, u32[]{:S(2)}, u32[]{:S(2)}) collective-permute-start(f32[8,128]{1,0:T(8,128)S(1)} %slice_add_fusion), channel_id=1, source_target_pairs={{0,6},{1,7},{2,4},{3,5},{4,2},{5,3},{6,0},{7,1},{8,14},{9,15},{10,... | collective-permute-start | bytes 12296 | tf_op jit(solution)/shard_map/ppermute | solution.py:541
  36.1 9.2 %collective-permute-start.16 = (bf16[144,256]{1,0:T(8,128)(2,1)S(1)}, bf16[144,256]{1,0:T(8,128)(2,1)S(1)}, u32[]{:S(2)}, u32[]{:S(2)}) collective-permute-start(bf16[144,256]{1,0:T(8,128)(2,1)S(1)} %get-tuple-element.118), channel_id=1, source_target_pairs={{0,40},{8,32},{16,56},{24,48},{32,8},{40,0},{48,24},{56,16},{1,41}... | collective-permute-start | bytes 221192 | tf_op jit(solution)/shard_map/ppermute | solution.py:525
  40.0 6.5 %collective-permute-start.17 = (bf16[144,256]{1,0:T(8,128)(2,1)S(1)}, bf16[144,256]{1,0:T(8,128)(2,1)S(1)}, u32[]{:S(2)}, u32[]{:S(2)}) collective-permute-start(bf16[144,256]{1,0:T(8,128)(2,1)S(1)} %get-tuple-element.119), channel_id=1, source_target_pairs={{0,48},{8,56},{16,32},{24,40},{32,16},{40,24},{48,0},{56,8},{1,49}... | collective-permute-start | bytes 221192 | tf_op jit(solution)/shard_map/ppermute | solution.py:525
  40.8 1.7 %collective-permute-start.8 = (bf16[128,256]{1,0:T(8,128)(2,1)S(1)}, bf16[128,256]{1,0:T(8,128)(2,1)S(1)}, u32[]{:S(2)}, u32[]{:S(2)}) collective-permute-start(bf16[128,256]{1,0:T(8,128)(2,1)S(1)} %get-tuple-element.105), channel_id=1, source_target_pairs={{0,64},{64,0},{128,192},{192,128},{1,65},{65,1},{129,193},{193,129... | collective-permute-start | bytes 196616 | tf_op jit(solution)/shard_map/ppermute | solution.py:528
  40.8 4.5 %collective-permute-start.18 = (f32[8,128]{1,0:T(8,128)S(1)}, f32[8,128]{1,0:T(8,128)S(1)}, u32[]{:S(2)}, u32[]{:S(2)}) collective-permute-start(f32[8,128]{1,0:T(8,128)S(1)} %add.15.totals_ref), channel_id=1, source_target_pairs={{0,16},{8,24},{16,0},{24,8},{32,48},{40,56},{48,32},{56,40},{1,17}... | collective-permute-start | bytes 12296 | tf_op jit(solution)/shard_map/ppermute | solution.py:525

commit v6 on v5

--- a/solution.py
+++ b/solution.py
@@ -604,7 +604,7 @@
     from_cross, own_powers = tie((from_cross, own_set[0]))
     near, totals = call(
         select_kernel,
-        [shape((2 * rows, both), BF16), shape((rows, 128), F32)],
+        [shape((2 * rows, both), BF16), shape((rows // 2, 128), F32)],
         (facts, totals, own, far6, far5, from_group, from_seq, from_cross),
     )
     mate = along_seq(near, 1)

time: 47.5 us -> 47.5 us (level)
  no operation moved by 1% of the time
where the time goes in v6:
time: 47.5 us; the launch traced here: 47.3 us
  starting transfers between devices  25.6 us (54%)
  waiting for transfers between devices  13.3 us (28%)
  Pallas kernels  7.64 us (16%)
  between operations  0.75 us (2%)
    ppermute x7, starting transfers between devices, along_grp(): return lax.ppermute(value, 'grp', swap(group_count, turn))  15.4 us
    ppermute x7, waiting for transfers between devices, along_grp(): return lax.ppermute(value, 'grp', swap(group_count, turn))  9.61 us
    pallas_call x12, Pallas kernels, call(): pl.pallas_call(kernel, out_shape=out_shapes, in_specs=[VMEM_SPEC] * plain...  7.64 us
    ppermute x2, starting transfers between devices, along_x(): return lax.ppermute(value, 'head', round_way if step else near)  3.61 us
    ppermute x2, starting transfers between devices, across(): return lax.ppermute(value, ('seq', 'grp'), turns)  3.46 us
    ppermute x7, starting transfers between devices, along_seq(): return lax.ppermute(value, 'seq', swap(seq_count, turn))  2.86 us
    ppermute x2, waiting for transfers between devices, along_x(): return lax.ppermute(value, 'head', round_way if step else near)  1.34 us
    ppermute x2, waiting for transfers between devices, across(): return lax.ppermute(value, ('seq', 'grp'), turns)  1.2 us
  transfers between devices with their start and end apart: 19, of which 9 were waited for; matrix products, arithmetic and copies ran while one was open for 0% of the time, Pallas kernels for 12%

profile of v6, /device:TPU:16, one launch (start us, length us, event | category | flops | bytes accessed | tf_op | source)
XLA Modules:
  0.0 47.3 jit_solution(1724597327184628448)
XLA Ops:
  0.6 0.9 %shard_map.119 = (bf16[128,256]{1,0:T(8,128)(2,1)S(1)}, f32[16,256]{1,0:T(8,128)S(1)}, f32[8,128]{1,0:T(8,128)S(1)}, f32[1,128]{1,0:T(1,128)S(1)}) custom-call(s32[8]{0:T(128)} %order_hbm.1, s32[8]{0:T(128)} %counts_hbm.1, s32[1,128]{1,0:T(1,128)} %mask_hbm.1, f32[1,16]{1,0:T(1,128)} %ratio_hbm.1, bf16[128,128]{1,0:T(8,128)(2,1)} %bitcast.11, ...), custom_call_target="tpu_custom_call" | custom-call | tf_op jit(solution)/shard_map/pallas_call | solution.py:489
  1.6 6.4 %collective-permute-start = (bf16[128,256]{1,0:T(8,128)(2,1)S(1)}, bf16[128,256]{1,0:T(8,128)(2,1)S(1)}, u32[]{:S(2)}, u32[]{:S(2)}) collective-permute-start(bf16[128,256]{1,0:T(8,128)(2,1)S(1)} %get-tuple-element.69.own_ref.right_ref), channel_id=1, source_target_pairs={{0,48},{8,56},{16,32},{24,40},{32,16},{40,24},{48,0},{56,8},{1,49}... | collective-permute-start | bytes 196616 | tf_op jit(solution)/shard_map/ppermute | solution.py:525
  8.0 1.0 %collective-permute-start.1 = (bf16[128,256]{1,0:T(8,128)(2,1)S(1)}, bf16[128,256]{1,0:T(8,128)(2,1)S(1)}, u32[]{:S(2)}, u32[]{:S(2)}) collective-permute-start(bf16[128,256]{1,0:T(8,128)(2,1)S(1)} %get-tuple-element.69.own_ref.right_ref), channel_id=1, source_target_pairs={{0,40},{8,32},{16,56},{24,48},{32,8},{40,0},{48,24},{56,16},{1,41}... | collective-permute-start | bytes 196616 | tf_op jit(solution)/shard_map/ppermute | solution.py:525
  9.3 1.4 %shard_map.120 = (bf16[1024,128]{1,0:T(8,128)(2,1)S(1)}, bf16[128,1024]{1,0:T(8,128)(2,1)S(1)}, bf16[1024,128]{1,0:T(8,128)(2,1)S(1)}, bf16[128,1024]{1,0:T(8,128)(2,1)S(1)}) custom-call(f32[1,128]{1,0:T(1,128)S(1)} %get-tuple-element.66.kept_ref, bf16[128,1024]{1,0:T(8,128)(2,1)} %bitcast.9, bf16[128,1024]{1,0:T(8,128)(2,1)} %bitcast.10), custom_call_target="tpu_custom_call" | custom-call | tf_op jit(solution)/shard_map/pallas_call | solution.py:489
  10.7 1.9 %collective-permute-done.far6 = bf16[128,256]{1,0:T(8,128)(2,1)S(1)} collective-permute-done((bf16[128,256]{1,0:T(8,128)(2,1)S(1)}, bf16[128,256]{1,0:T(8,128)(2,1)S(1)}, u32[]{:S(2)}, u32[]{:S(2)}) %collective-permute-start) | collective-permute-done | bytes 65568 | tf_op jit(solution)/shard_map/ppermute | solution.py:525
  12.6 2.7 %collective-permute-done.1.far5 = bf16[128,256]{1,0:T(8,128)(2,1)S(1)} collective-permute-done((bf16[128,256]{1,0:T(8,128)(2,1)S(1)}, bf16[128,256]{1,0:T(8,128)(2,1)S(1)}, u32[]{:S(2)}, u32[]{:S(2)}) %collective-permute-start.1) | collective-permute-done | bytes 65568 | tf_op jit(solution)/shard_map/ppermute | solution.py:525
  15.3 2.0 %collective-permute-start.3 = (bf16[144,256]{1,0:T(8,128)(2,1)S(1)}, bf16[144,256]{1,0:T(8,128)(2,1)S(1)}, u32[]{:S(2)}, u32[]{:S(2)}) collective-permute-start(bf16[144,256]{1,0:T(8,128)(2,1)S(1)} %get-tuple-element.80), channel_id=1, source_target_pairs={{0,136},{8,128},{16,152},{24,144},{32,168},{40,160},{48,184},{56,1... | collective-permute-start | bytes 221192 | tf_op jit(solution)/shard_map/ppermute | solution.py:536
  17.3 0.8 %collective-permute-start.5 = (bf16[144,256]{1,0:T(8,128)(2,1)S(1)}, bf16[144,256]{1,0:T(8,128)(2,1)S(1)}, u32[]{:S(2)}, u32[]{:S(2)}) collective-permute-start(bf16[144,256]{1,0:T(8,128)(2,1)S(1)} %get-tuple-element.85), channel_id=1, source_target_pairs={{0,8},{8,0},{16,24},{24,16},{32,40},{40,32},{48,56},{56,48},{1,9},... | collective-permute-start | bytes 221192 | tf_op jit(solution)/shard_map/ppermute | solution.py:525
  19.5 1.2 %collective-permute-done.3.cross_ref = bf16[144,256]{1,0:T(8,128)(2,1)S(1)} collective-permute-done((bf16[144,256]{1,0:T(8,128)(2,1)S(1)}, bf16[144,256]{1,0:T(8,128)(2,1)S(1)}, u32[]{:S(2)}, u32[]{:S(2)}) %collective-permute-start.3) | collective-permute-done | bytes 73760 | tf_op jit(solution)/shard_map/ppermute | solution.py:536
  20.7 1.0 %collective-permute-done.5.group_ref = bf16[144,256]{1,0:T(8,128)(2,1)S(1)} collective-permute-done((bf16[144,256]{1,0:T(8,128)(2,1)S(1)}, bf16[144,256]{1,0:T(8,128)(2,1)S(1)}, u32[]{:S(2)}, u32[]{:S(2)}) %collective-permute-start.5) | collective-permute-done | bytes 73760 | tf_op jit(solution)/shard_map/ppermute | solution.py:525
  21.7 0.8 %collective-permute-done.6.seq_ref = bf16[144,256]{1,0:T(8,128)(2,1)S(1)} collective-permute-done((bf16[144,256]{1,0:T(8,128)(2,1)S(1)}, bf16[144,256]{1,0:T(8,128)(2,1)S(1)}, u32[]{:S(2)}, u32[]{:S(2)}) %collective-permute-start.6) | collective-permute-done | bytes 73760 | tf_op jit(solution)/shard_map/ppermute | solution.py:528
  24.0 1.3 %shard_map.125 = (bf16[256,256]{1,0:T(8,128)(2,1)S(1)}, f32[128,1024]{1,0:T(8,128)S(1)}, bf16[256,1024]{1,0:T(8,128)(2,1)S(1)}, bf16[128,256]{1,0:T(8,128)(2,1)S(1)}, f32[8,1024]{1,0:T(8,128)S(1)}) custom-call(f32[16,256]{1,0:T(8,128)S(1)} %get-tuple-element.65.facts_ref, bf16[1024,128]{1,0:T(8,128)(2,1)S(1)} %get-tuple-element.72.query_ref, ...), custom_call_target="tpu_custom_call" | custom-call | flops 402653184 | tf_op jit(solution)/shard_map/pallas_call | solution.py:489
  25.6 1.5 %collective-permute-start.10 = (f32[64,128]{1,0:T(8,128)S(1)}, f32[64,128]{1,0:T(8,128)S(1)}, u32[]{:S(2)}, u32[]{:S(2)}) collective-permute-start(f32[64,128]{1,0:T(8,128)S(1)} %add.13), channel_id=1, source_target_pairs={{0,2},{1,3},{2,0},{3,1},{4,6},{5,7},{6,4},{7,5},{8,10},{9,11},{10,... | collective-permute-start | bytes 98312 | tf_op jit(solution)/shard_map/ppermute | solution.py:541
  27.6 1.5 %collective-permute-start.15 = (bf16[128,256]{1,0:T(8,128)(2,1)S(1)}, bf16[128,256]{1,0:T(8,128)(2,1)S(1)}, u32[]{:S(2)}, u32[]{:S(2)}) collective-permute-start(bf16[128,256]{1,0:T(8,128)(2,1)S(1)} %get-tuple-element.114), channel_id=1, source_target_pairs={{0,136},{8,128},{16,152},{24,144},{32,168},{40,160},{48,184},{56,1... | collective-permute-start | bytes 196616 | tf_op jit(solution)/shard_map/ppermute | solution.py:536
  29.1 1.3 %collective-permute-start.14 = (bf16[128,256]{1,0:T(8,128)(2,1)S(1)}, bf16[128,256]{1,0:T(8,128)(2,1)S(1)}, u32[]{:S(2)}, u32[]{:S(2)}) collective-permute-start(bf16[128,256]{1,0:T(8,128)(2,1)S(1)} %get-tuple-element.114), channel_id=1, source_target_pairs={{0,128},{64,192},{128,0},{192,64},{1,129},{65,193},{129,1},{193,65... | collective-permute-start | bytes 196616 | tf_op jit(solution)/shard_map/ppermute | solution.py:528
  30.3 0.8 %collective-permute-start.13 = (bf16[128,256]{1,0:T(8,128)(2,1)S(1)}, bf16[128,256]{1,0:T(8,128)(2,1)S(1)}, u32[]{:S(2)}, u32[]{:S(2)}) collective-permute-start(bf16[128,256]{1,0:T(8,128)(2,1)S(1)} %get-tuple-element.113.near_ref), channel_id=1, source_target_pairs={{0,8},{8,0},{16,24},{24,16},{32,40},{40,32},{48,56},{56,48},{1,9},... | collective-permute-start | bytes 196616 | tf_op jit(solution)/shard_map/ppermute | solution.py:525
  31.2 2.1 %collective-permute-start.11 = (f32[8,128]{1,0:T(8,128)S(1)}, f32[8,128]{1,0:T(8,128)S(1)}, u32[]{:S(2)}, u32[]{:S(2)}) collective-permute-start(f32[8,128]{1,0:T(8,128)S(1)} %slice_add_fusion), channel_id=1, source_target_pairs={{0,6},{1,7},{2,4},{3,5},{4,2},{5,3},{6,0},{7,1},{8,14},{9,15},{10,... | collective-permute-start | bytes 12296 | tf_op jit(solution)/shard_map/ppermute | solution.py:541
  33.3 1.4 %shard_map.127 = (bf16[128,1024]{1,0:T(8,128)(2,1)}, f32[128,1024]{1,0:T(8,128)S(1)}, bf16[128,256]{1,0:T(8,128)(2,1)S(1)}, f32[128,256]{1,0:T(8,128)S(1)}) custom-call(f32[16,256]{1,0:T(8,128)S(1)} %get-tuple-element.65.facts_ref, bf16[128,1024]{1,0:T(8,128)(2,1)S(1)} %get-tuple-element.67.query_t_ref, bf16[128,1024]{1,0:T(8,128)(2,1)S(1)} %get-tuple-element.68.grad_t_ref, ...), custom_call_target="tpu_custom_call" | custom-call | flops 335544320 | tf_op jit(solution)/shard_map/pallas_call | solution.py:489
  34.7 1.3 %collective-permute-done.11 = f32[8,128]{1,0:T(8,128)S(1)} collective-permute-done((f32[8,128]{1,0:T(8,128)S(1)}, f32[8,128]{1,0:T(8,128)S(1)}, u32[]{:S(2)}, u32[]{:S(2)}) %collective-permute-start.11) | collective-permute-done | bytes 4128 | tf_op jit(solution)/shard_map/ppermute | solution.py:541
  36.1 3.9 %collective-permute-start.16 = (bf16[144,256]{1,0:T(8,128)(2,1)S(1)}, bf16[144,256]{1,0:T(8,128)(2,1)S(1)}, u32[]{:S(2)}, u32[]{:S(2)}) collective-permute-start(bf16[144,256]{1,0:T(8,128)(2,1)S(1)} %get-tuple-element.118), channel_id=1, source_target_pairs={{0,40},{8,32},{16,56},{24,48},{32,8},{40,0},{48,24},{56,16},{1,41}... | collective-permute-start | bytes 221192 | tf_op jit(solution)/shard_map/ppermute | solution.py:525
  40.8 1.6 %collective-permute-start.18 = (f32[8,128]{1,0:T(8,128)S(1)}, f32[8,128]{1,0:T(8,128)S(1)}, u32[]{:S(2)}, u32[]{:S(2)}) collective-permute-start(f32[8,128]{1,0:T(8,128)S(1)} %add.15.totals_ref), channel_id=1, source_target_pairs={{0,16},{8,24},{16,0},{24,8},{32,48},{40,56},{48,32},{56,40},{1,17}... | collective-permute-start | bytes 12296 | tf_op jit(solution)/shard_map/ppermute | solution.py:525
  42.5 2.9 %collective-permute-done.18.rest_ref = f32[8,128]{1,0:T(8,128)S(1)} collective-permute-done((f32[8,128]{1,0:T(8,128)S(1)}, f32[8,128]{1,0:T(8,128)S(1)}, u32[]{:S(2)}, u32[]{:S(2)}) %collective-permute-start.18) | collective-permute-done | bytes 4128 | tf_op jit(solution)/shard_map/ppermute | solution.py:525
  45.3 1.2 %collective-permute-done.17.far6 = bf16[144,256]{1,0:T(8,128)(2,1)S(1)} collective-permute-done((bf16[144,256]{1,0:T(8,128)(2,1)S(1)}, bf16[144,256]{1,0:T(8,128)(2,1)S(1)}, u32[]{:S(2)}, u32[]{:S(2)}) %collective-permute-start.17) | collective-permute-done | bytes 73760 | tf_op jit(solution)/shard_map/ppermute | solution.py:525
  46.5 0.8 %shard_map.130 = (bf16[128,1024]{1,0:T(8,128)(2,1)}, bf16[128,128]{1,0:T(8,128)(2,1)}, bf16[128,128]{1,0:T(8,128)(2,1)}, f32[1,4]{1,0:T(1,128)}) custom-call(f32[16,256]{1,0:T(8,128)S(1)} %get-tuple-element.65.facts_ref, f32[128,256]{1,0:T(8,128)S(1)} %get-tuple-element.104.local_ref, bf16[128,256]{1,0:T(8,128)(2,1)S(1)} %collective-permute-done.8.mate_ref, ...), custom_call_target="tpu_custom_call" | custom-call | tf_op jit(solution)/shard_map/pallas_call | solution.py:489
  (30 shorter events, 4.9 us)
Async XLA Ops:
  1.6 11.0 %collective-permute-start = (bf16[128,256]{1,0:T(8,128)(2,1)S(1)}, bf16[128,256]{1,0:T(8,128)(2,1)S(1)}, u32[]{:S(2)}, u32[]{:S(2)}) collective-permute-start(bf16[128,256]{1,0:T(8,128)(2,1)S(1)} %get-tuple-element.69.own_ref.right_ref), channel_id=1, source_target_pairs={{0,48},{8,56},{16,32},{24,40},{32,16},{40,24},{48,0},{56,8},{1,49}... | collective-permute-start | bytes 196616 | tf_op jit(solution)/shard_map/ppermute | solution.py:525
  8.0 7.3 %collective-permute-start.1 = (bf16[128,256]{1,0:T(8,128)(2,1)S(1)}, bf16[128,256]{1,0:T(8,128)(2,1)S(1)}, u32[]{:S(2)}, u32[]{:S(2)}) collective-permute-start(bf16[128,256]{1,0:T(8,128)(2,1)S(1)} %get-tuple-element.69.own_ref.right_ref), channel_id=1, source_target_pairs={{0,40},{8,32},{16,56},{24,48},{32,8},{40,0},{48,24},{56,16},{1,41}... | collective-permute-start | bytes 196616 | tf_op jit(solution)/shard_map/ppermute | solution.py:525
  9.0 6.3 %collective-permute-start.2 = (f32[8,128]{1,0:T(8,128)S(1)}, f32[8,128]{1,0:T(8,128)S(1)}, u32[]{:S(2)}, u32[]{:S(2)}) collective-permute-start(f32[8,128]{1,0:T(8,128)S(1)} %get-tuple-element.76), channel_id=1, source_target_pairs={{0,1},{1,0},{2,3},{3,2},{4,5},{5,4},{6,7},{7,6},{8,9},{9,8},{10,11... | collective-permute-start | bytes 12296 | tf_op jit(solution)/shard_map/ppermute | solution.py:544
  9.3 9.6 %collective-permute-start.4 = (bf16[128,256]{1,0:T(8,128)(2,1)S(1)}, bf16[128,256]{1,0:T(8,128)(2,1)S(1)}, u32[]{:S(2)}, u32[]{:S(2)}) collective-permute-start(bf16[128,256]{1,0:T(8,128)(2,1)S(1)} %get-tuple-element.69.own_ref.right_ref), channel_id=1, source_target_pairs={{0,64},{64,0},{128,192},{192,128},{1,65},{65,1},{129,193},{193,129... | collective-permute-start | bytes 196616 | tf_op jit(solution)/shard_map/ppermute | solution.py:528
  15.3 5.3 %collective-permute-start.3 = (bf16[144,256]{1,0:T(8,128)(2,1)S(1)}, bf16[144,256]{1,0:T(8,128)(2,1)S(1)}, u32[]{:S(2)}, u32[]{:S(2)}) collective-permute-start(bf16[144,256]{1,0:T(8,128)(2,1)S(1)} %get-tuple-element.80), channel_id=1, source_target_pairs={{0,136},{8,128},{16,152},{24,144},{32,168},{40,160},{48,184},{56,1... | collective-permute-start | bytes 221192 | tf_op jit(solution)/shard_map/ppermute | solution.py:536
  17.3 4.4 %collective-permute-start.5 = (bf16[144,256]{1,0:T(8,128)(2,1)S(1)}, bf16[144,256]{1,0:T(8,128)(2,1)S(1)}, u32[]{:S(2)}, u32[]{:S(2)}) collective-permute-start(bf16[144,256]{1,0:T(8,128)(2,1)S(1)} %get-tuple-element.85), channel_id=1, source_target_pairs={{0,8},{8,0},{16,24},{24,16},{32,40},{40,32},{48,56},{56,48},{1,9},... | collective-permute-start | bytes 221192 | tf_op jit(solution)/shard_map/ppermute | solution.py:525
  18.2 4.4 %collective-permute-start.6 = (bf16[144,256]{1,0:T(8,128)(2,1)S(1)}, bf16[144,256]{1,0:T(8,128)(2,1)S(1)}, u32[]{:S(2)}, u32[]{:S(2)}) collective-permute-start(bf16[144,256]{1,0:T(8,128)(2,1)S(1)} %get-tuple-element.86), channel_id=1, source_target_pairs={{0,128},{64,192},{128,0},{192,64},{1,129},{65,193},{129,1},{193,65... | collective-permute-start | bytes 221192 | tf_op jit(solution)/shard_map/ppermute | solution.py:528
  22.6 1.4 %collective-permute-start.7 = (bf16[256,256]{1,0:T(8,128)(2,1)S(1)}, bf16[256,256]{1,0:T(8,128)(2,1)S(1)}, u32[]{:S(2)}, u32[]{:S(2)}) collective-permute-start(bf16[256,256]{1,0:T(8,128)(2,1)S(1)} %get-tuple-element.88.left_ref.right_ref), channel_id=1, source_target_pairs={{0,64},{64,0},{128,192},{192,128},{1,65},{65,1},{129,193},{193,129... | collective-permute-start | bytes 393224 | tf_op jit(solution)/shard_map/ppermute | solution.py:528
  22.7 2.6 %collective-permute-start.9 = (f32[64,128]{1,0:T(8,128)S(1)}, f32[64,128]{1,0:T(8,128)S(1)}, u32[]{:S(2)}, u32[]{:S(2)}) collective-permute-start(f32[64,128]{1,0:T(8,128)S(1)} %get-tuple-element.109), channel_id=1, source_target_pairs={{0,64},{64,0},{128,192},{192,128},{1,65},{65,1},{129,193},{193,129... | collective-permute-start | bytes 98312 | tf_op jit(solution)/shard_map/ppermute | solution.py:528
  25.3 2.2 %collective-permute-start.12 = (bf16[256,256]{1,0:T(8,128)(2,1)S(1)}, bf16[256,256]{1,0:T(8,128)(2,1)S(1)}, u32[]{:S(2)}, u32[]{:S(2)}) collective-permute-start(bf16[256,256]{1,0:T(8,128)(2,1)S(1)} %get-tuple-element.112), channel_id=1, source_target_pairs={{0,64},{64,0},{128,192},{192,128},{1,65},{65,1},{129,193},{193,129... | collective-permute-start | bytes 393224 | tf_op jit(solution)/shard_map/ppermute | solution.py:528
  25.6 5.6 %collective-permute-start.10 = (f32[64,128]{1,0:T(8,128)S(1)}, f32[64,128]{1,0:T(8,128)S(1)}, u32[]{:S(2)}, u32[]{:S(2)}) collective-permute-start(f32[64,128]{1,0:T(8,128)S(1)} %add.13), channel_id=1, source_target_pairs={{0,2},{1,3},{2,0},{3,1},{4,6},{5,7},{6,4},{7,5},{8,10},{9,11},{10,... | collective-permute-start | bytes 98312 | tf_op jit(solution)/shard_map/ppermute | solution.py:541
  27.6 8.4 %collective-permute-start.15 = (bf16[128,256]{1,0:T(8,128)(2,1)S(1)}, bf16[128,256]{1,0:T(8,128)(2,1)S(1)}, u32[]{:S(2)}, u32[]{:S(2)}) collective-permute-start(bf16[128,256]{1,0:T(8,128)(2,1)S(1)} %get-tuple-element.114), channel_id=1, source_target_pairs={{0,136},{8,128},{16,152},{24,144},{32,168},{40,160},{48,184},{56,1... | collective-permute-start | bytes 196616 | tf_op jit(solution)/shard_map/ppermute | solution.py:536
  29.1 7.0 %collective-permute-start.14 = (bf16[128,256]{1,0:T(8,128)(2,1)S(1)}, bf16[128,256]{1,0:T(8,128)(2,1)S(1)}, u32[]{:S(2)}, u32[]{:S(2)}) collective-permute-start(bf16[128,256]{1,0:T(8,128)(2,1)S(1)} %get-tuple-element.114), channel_id=1, source_target_pairs={{0,128},{64,192},{128,0},{192,64},{1,129},{65,193},{129,1},{193,65... | collective-permute-start | bytes 196616 | tf_op jit(solution)/shard_map/ppermute | solution.py:528
  30.3 5.7 %collective-permute-start.13 = (bf16[128,256]{1,0:T(8,128)(2,1)S(1)}, bf16[128,256]{1,0:T(8,128)(2,1)S(1)}, u32[]{:S(2)}, u32[]{:S(2)}) collective-permute-start(bf16[128,256]{1,0:T(8,128)(2,1)S(1)} %get-tuple-element.113.near_ref), channel_id=1, source_target_pairs={{0,8},{8,0},{16,24},{24,16},{32,40},{40,32},{48,56},{56,48},{1,9},... | collective-permute-start | bytes 196616 | tf_op jit(solution)/shard_map/ppermute | solution.py:525
  31.2 4.8 %collective-permute-start.11 = (f32[8,128]{1,0:T(8,128)S(1)}, f32[8,128]{1,0:T(8,128)S(1)}, u32[]{:S(2)}, u32[]{:S(2)}) collective-permute-start(f32[8,128]{1,0:T(8,128)S(1)} %slice_add_fusion), channel_id=1, source_target_pairs={{0,6},{1,7},{2,4},{3,5},{4,2},{5,3},{6,0},{7,1},{8,14},{9,15},{10,... | collective-permute-start | bytes 12296 | tf_op jit(solution)/shard_map/ppermute | solution.py:541
  36.1 9.2 %collective-permute-start.16 = (bf16[144,256]{1,0:T(8,128)(2,1)S(1)}, bf16[144,256]{1,0:T(8,128)(2,1)S(1)}, u32[]{:S(2)}, u32[]{:S(2)}) collective-permute-start(bf16[144,256]{1,0:T(8,128)(2,1)S(1)} %get-tuple-element.118), channel_id=1, source_target_pairs={{0,40},{8,32},{16,56},{24,48},{32,8},{40,0},{48,24},{56,16},{1,41}... | collective-permute-start | bytes 221192 | tf_op jit(solution)/shard_map/ppermute | solution.py:525
  40.0 6.5 %collective-permute-start.17 = (bf16[144,256]{1,0:T(8,128)(2,1)S(1)}, bf16[144,256]{1,0:T(8,128)(2,1)S(1)}, u32[]{:S(2)}, u32[]{:S(2)}) collective-permute-start(bf16[144,256]{1,0:T(8,128)(2,1)S(1)} %get-tuple-element.119), channel_id=1, source_target_pairs={{0,48},{8,56},{16,32},{24,40},{32,16},{40,24},{48,0},{56,8},{1,49}... | collective-permute-start | bytes 221192 | tf_op jit(solution)/shard_map/ppermute | solution.py:525
  40.8 4.5 %collective-permute-start.8 = (bf16[128,256]{1,0:T(8,128)(2,1)S(1)}, bf16[128,256]{1,0:T(8,128)(2,1)S(1)}, u32[]{:S(2)}, u32[]{:S(2)}) collective-permute-start(bf16[128,256]{1,0:T(8,128)(2,1)S(1)} %get-tuple-element.105), channel_id=1, source_target_pairs={{0,64},{64,0},{128,192},{192,128},{1,65},{65,1},{129,193},{193,129... | collective-permute-start | bytes 196616 | tf_op jit(solution)/shard_map/ppermute | solution.py:528
  40.8 4.5 %collective-permute-start.18 = (f32[8,128]{1,0:T(8,128)S(1)}, f32[8,128]{1,0:T(8,128)S(1)}, u32[]{:S(2)}, u32[]{:S(2)}) collective-permute-start(f32[8,128]{1,0:T(8,128)S(1)} %add.15.totals_ref), channel_id=1, source_target_pairs={{0,16},{8,24},{16,0},{24,8},{32,48},{40,56},{48,32},{56,40},{1,17}... | collective-permute-start | bytes 12296 | tf_op jit(solution)/shard_map/ppermute | solution.py:525
